TPU v7x, 32 devices: a whole 2x2x4 slice. The times are simulated.
32 devices in a mesh: graph: 8 (over y, x, core), col: 4 (over z).
Axes of the slice: x: 2, y: 2, z: 4, core: 2. Of those that a mesh axis runs over, the one named last changes fastest.
Arguments:
- features: float32 [8, 100, 8192], P('graph'), may hold values from -6 to 6
- blocks: int32 [8, 2, 512], P('graph'), may hold values from 0 to 63, as said below
- block_values: float32 [8, 512, 128, 128], P('graph'), may hold values from 0 to 0.001953125
- group_sizes: int32 [8, 2], replicated, may hold values from 8 to 8192, as said below
- labels: int32 [8, 8192], P('graph'), may hold values from 0 to 46
- pair_nodes: int32 [8, 2, 8, 8], P('graph'), may hold values from 0 to 8191, as said below
- weight_first: float32 [2, 100, 256], P(None, None, 'col'), may hold values from -0.4375 to 0.4375
- weight_second: float32 [2, 256, 256], P(None, None, 'col'), may hold values from -0.25 to 0.25
- weight_head: float32 [2, 256, 47], P(None, 'col'), may hold values from -0.25 to 0.25
- norm_params: float32 [2, 2, 256], P(None, None, 'col'), may hold values from 0.5 to 1.5
- momentum_first: float32 [2, 100, 256], P(None, None, 'col'), may hold values from -0.125 to 0.125
- momentum_second: float32 [2, 256, 256], P(None, None, 'col'), may hold values from -0.125 to 0.125
- momentum_head: float32 [2, 256, 47], P(None, 'col'), may hold values from -0.125 to 0.125
- momentum_norms: float32 [2, 2, 256], P(None, None, 'col'), may hold values from -0.5 to 0.5
- average_first: float32 [2, 100, 256], P(None, None, 'col'), may hold values from -0.4375 to 0.4375
- average_second: float32 [2, 256, 256], P(None, None, 'col'), may hold values from -0.25 to 0.25
- average_head: float32 [2, 256, 47], P(None, 'col'), may hold values from -0.25 to 0.25
- average_norms: float32 [2, 2, 256], P(None, None, 'col'), may hold values from 0.5 to 1.5
Outputs:
- loss_sum: float32 [], replicated
- node_count: float32 [], replicated
- momentum_first_new: float32 [2, 100, 256], P(None, None, 'col')
- average_first_new: float32 [2, 100, 256], P(None, None, 'col')
- weight_first_new: float32 [2, 100, 256], P(None, None, 'col')
- momentum_second_new: float32 [2, 256, 256], P(None, None, 'col')
- average_second_new: float32 [2, 256, 256], P(None, None, 'col')
- weight_second_new: float32 [2, 256, 256], P(None, None, 'col')
- momentum_head_new: float32 [2, 256, 47], P(None, 'col')
- average_head_new: float32 [2, 256, 47], P(None, 'col')
- weight_head_new: float32 [2, 256, 47], P(None, 'col')
- momentum_norms_new: float32 [2, 2, 256], P(None, None, 'col')
- average_norms_new: float32 [2, 2, 256], P(None, None, 'col')
- norms_new: float32 [2, 2, 256], P(None, None, 'col')
Inputs may be any that keep to these rules, and one draw needn't show every extreme that they name: `group_sizes`: row g gives subgraph g's live nodes, a multiple of 128, then its live blocks, live nodes * 8 / 128; some subgraph has all 8192 nodes live. Both block numbers of subgraph g lie below its live nodes / 128; only the first group_sizes[g,1] blocks count. `pair_nodes`: node numbers of subgraph g lie below its live nodes.
All inputs are finite; a program needn't handle non-finite values.
Results may differ from a plain program's by a relative error of at most 0.0003.
Values sent between devices are 32-bit elements; how exact they have to be, the bound alone decides.
A program may use at most 192 MiB of HBM per device.

v0:
```python
import jax
import jax.numpy as jnp
from jax import lax
from jax.sharding import PartitionSpec as P

PRECISE = lax.Precision.HIGHEST
NORM_EPS = 1e-05
MOMENTUM = 0.9
STEP_RATE = 2.0
AVERAGE_KEEP = 0.9
PAIR_WEIGHT = 0.5


def aggregate(source, coords, values, live_blocks, reverse):
    channels, node_total = source.shape
    block_width = values.shape[-1]
    row_blocks = node_total // block_width
    slab_size = min(32, coords.shape[1])
    shaped = source.reshape(channels, row_blocks, block_width)
    block_ids = jnp.arange(row_blocks, dtype=jnp.int32)

    def one_slab(index, running):
        first_block = index * slab_size
        rows_here = lax.dynamic_slice_in_dim(coords[0], first_block, slab_size)
        cols_here = lax.dynamic_slice_in_dim(coords[1], first_block, slab_size)
        slab_values = lax.dynamic_slice_in_dim(values, first_block, slab_size, 0)
        alive_here = (first_block + jnp.arange(slab_size, dtype=jnp.int32) < live_blocks).astype(
            jnp.float32
        )
        if reverse:
            product = jnp.einsum(
                "cbi,bji->cbj", shaped[:, rows_here, :], slab_values, precision=PRECISE
            )
            target_rows = cols_here
        else:
            product = jnp.einsum(
                "cbj,bji->cbi", shaped[:, cols_here, :], slab_values, precision=PRECISE
            )
            target_rows = rows_here
        onehot = (target_rows[:, None] == block_ids[None, :]).astype(jnp.float32)
        return running + jnp.einsum(
            "cbi,br->cri", product * alive_here[None, :, None], onehot, precision=PRECISE
        )

    slab_turns = (live_blocks + slab_size - 1) // slab_size
    result = lax.fori_loop(
        0, slab_turns, one_slab, jnp.zeros((channels, row_blocks, block_width), jnp.float32)
    )
    return result.reshape(channels, node_total)


def project(weight, direct, spread):
    return jnp.einsum("fo,fn->on", weight[0], direct, precision=PRECISE) + jnp.einsum(
        "fo,fn->on", weight[1], spread, precision=PRECISE
    )


def outer_grad(inputs, upstream):
    return jnp.einsum("fn,on->fo", inputs, upstream, precision=PRECISE)


def back_project(weight, upstream):
    return jnp.einsum("fo,on->fn", weight, upstream, precision=PRECISE)


def norm_act(pre_act, gain_bias, live_mask, live_count):
    average = jnp.sum(pre_act * live_mask, axis=1, keepdims=True) / live_count
    centred = pre_act - average
    variance = jnp.sum(centred * centred * live_mask, axis=1, keepdims=True) / live_count
    scaled = (
        centred * lax.rsqrt(variance + NORM_EPS) * gain_bias[0][:, None] + gain_bias[1][:, None]
    )
    return jax.nn.gelu(scaled, approximate=True)


def renew(weight, momentum, average, gradient):
    momentum_new = MOMENTUM * momentum + gradient
    weight_new = weight - STEP_RATE * (gradient + MOMENTUM * momentum_new)
    average_new = AVERAGE_KEEP * average + (1.0 - AVERAGE_KEEP) * weight_new
    return (momentum_new, average_new, weight_new)


def per_device(
    features,
    blocks,
    block_values,
    group_sizes,
    labels,
    pair_nodes,
    weight_first,
    weight_second,
    weight_head,
    norm_params,
    momentum_first,
    momentum_second,
    momentum_head,
    momentum_norms,
    average_first,
    average_second,
    average_head,
    average_norms,
):
    inputs = features[0]
    coords = blocks[0]
    values = block_values[0]
    label_row = labels[0]
    pair_row = pair_nodes[0]
    own_sizes = group_sizes[lax.axis_index("graph")]
    total_nodes = jnp.sum(group_sizes[:, 0]).astype(jnp.float32)
    node_total = inputs.shape[1]
    live_mask = (jnp.arange(node_total, dtype=jnp.int32) < own_sizes[0]).astype(jnp.float32)
    live_count = own_sizes[0].astype(jnp.float32)

    def spread_of(source):
        return aggregate(source, coords, values, own_sizes[1], False)

    def spread_back(source):
        return aggregate(source, coords, values, own_sizes[1], True)

    def norm_back(pre_act, gain_bias, upstream):
        outputs, pullback = jax.vjp(
            lambda p, g: norm_act(p, g, live_mask, live_count), pre_act, gain_bias
        )
        return pullback(upstream)

    spread_input = spread_of(inputs)
    pre_one = project(weight_first, inputs, spread_input)
    hidden_one = norm_act(pre_one, norm_params[0], live_mask, live_count)
    spread_one = spread_of(hidden_one)
    full_one, full_spread = (
        lax.all_gather(hidden_one, "col", axis=0, tiled=True),
        lax.all_gather(spread_one, "col", axis=0, tiled=True),
    )
    pre_two = project(weight_second, full_one, full_spread)
    hidden_two = norm_act(pre_two, norm_params[1], live_mask, live_count)
    spread_two = spread_of(hidden_two)
    logits = lax.psum(project(weight_head, hidden_two, spread_two), "col")
    class_ids = jnp.arange(logits.shape[0], dtype=jnp.int32)
    largest = jnp.max(logits, axis=0, keepdims=True)
    expon = jnp.exp(logits - largest)
    totals = jnp.sum(expon, axis=0, keepdims=True)
    log_total = largest[0] + jnp.log(totals[0])
    onehot = (label_row[None, :] == class_ids[:, None]).astype(jnp.float32)
    target = jnp.sum(onehot * logits, axis=0)
    cross_sum = jnp.sum((log_total - target) * live_mask)
    grad_logits = (expon / totals - onehot) * live_mask[None, :] / total_nodes
    send_ids = pair_row[0].reshape(-1)
    recv_ids = pair_row[1].reshape(-1)
    incoming = lax.all_to_all(
        jnp.take(logits, send_ids, axis=1), "graph", split_axis=1, concat_axis=1, tiled=True
    )
    difference = jnp.take(logits, recv_ids, axis=1) - incoming
    pair_sum = PAIR_WEIGHT * jnp.sum(difference * difference)
    pair_grad = 2.0 * PAIR_WEIGHT * difference / total_nodes
    returned = lax.all_to_all(-pair_grad, "graph", split_axis=1, concat_axis=1, tiled=True)
    grad_logits = grad_logits.at[:, recv_ids].add(pair_grad).at[:, send_ids].add(returned)
    loss_local = cross_sum + pair_sum
    grad_head = jnp.stack(
        [outer_grad(hidden_two, grad_logits), outer_grad(spread_two, grad_logits)]
    )
    grad_hidden_two = back_project(weight_head[0], grad_logits) + spread_back(
        back_project(weight_head[1], grad_logits)
    )
    grad_pre_two, grad_norm_two = norm_back(pre_two, norm_params[1], grad_hidden_two)
    grad_second = jnp.stack(
        [outer_grad(full_one, grad_pre_two), outer_grad(full_spread, grad_pre_two)]
    )
    back_one, back_spread = (
        lax.psum_scatter(
            back_project(weight_second[0], grad_pre_two), "col", scatter_dimension=0, tiled=True
        ),
        lax.psum_scatter(
            back_project(weight_second[1], grad_pre_two), "col", scatter_dimension=0, tiled=True
        ),
    )
    grad_hidden_one = back_one + spread_back(back_spread)
    grad_pre_one, grad_norm_one = norm_back(pre_one, norm_params[0], grad_hidden_one)
    grad_first = jnp.stack(
        [outer_grad(inputs, grad_pre_one), outer_grad(spread_input, grad_pre_one)]
    )
    grad_norms = jnp.stack([grad_norm_one, grad_norm_two])
    grad_first, grad_second, grad_head, grad_norms, loss_sum = lax.psum(
        (grad_first, grad_second, grad_head, grad_norms, loss_local), "graph"
    )
    first = renew(weight_first, momentum_first, average_first, grad_first)
    second = renew(weight_second, momentum_second, average_second, grad_second)
    head = renew(weight_head, momentum_head, average_head, grad_head)
    norms = renew(norm_params, momentum_norms, average_norms, grad_norms)
    return (
        loss_sum,
        total_nodes,
        first[0],
        first[1],
        first[2],
        second[0],
        second[1],
        second[2],
        head[0],
        head[1],
        head[2],
        norms[0],
        norms[1],
        norms[2],
    )


def solution(mesh):
    in_specs = (
        P("graph", None, None),
        P("graph", None, None),
        P("graph", None, None, None),
        P(),
        P("graph", None),
        P("graph", None, None, None),
        P(None, None, "col"),
        P(None, None, "col"),
        P(None, "col", None),
        P(None, None, "col"),
        P(None, None, "col"),
        P(None, None, "col"),
        P(None, "col", None),
        P(None, None, "col"),
        P(None, None, "col"),
        P(None, None, "col"),
        P(None, "col", None),
        P(None, None, "col"),
    )
    out_specs = (
        P(),
        P(),
        P(None, None, "col"),
        P(None, None, "col"),
        P(None, None, "col"),
        P(None, None, "col"),
        P(None, None, "col"),
        P(None, None, "col"),
        P(None, "col", None),
        P(None, "col", None),
        P(None, "col", None),
        P(None, None, "col"),
        P(None, None, "col"),
        P(None, None, "col"),
    )
    return jax.shard_map(
        per_device, mesh=mesh, in_specs=in_specs, out_specs=out_specs, check_vma=False
    )
```

profile of v0, /device:TPU:0, one launch (start us, length us, event | category | flops | bytes accessed | tf_op | source)
XLA Modules:
  0.0 1463.8 jit_solution(12968433393092234619)
XLA Ops:
  10.5 5.5 copy.87
  18.2 54.0 %while.55 = (s32[]{:T(128)}, f32[100,64,128]{2,1,0:T(8,128)}, s32[]{:T(128)}, s32[2,512]{1,0:T(2,128)S(1)}, f32[512,128,128]{2,1,0:T(8,128)}, /*index=5*/f32[100...) while((s32[]{:T(128)}, f32[100,64,128]{2,1,0:T(8,128)}, ...), condition=%wide.region_1.2_spmd.clone, body=%wide.region_0.0_spmd.clone.sunk | while | flops 944950464 | bytes 16856368 | solution.py:46
  21.5 4.6 multiply_bitcast_fusion.2
  26.2 5.3 bitcast_add_fusion.11
  34.9 4.6 multiply_bitcast_fusion.2
  39.6 5.3 bitcast_add_fusion.11
  48.3 4.6 multiply_bitcast_fusion.2
  53.0 5.3 bitcast_add_fusion.11
  61.7 4.6 multiply_bitcast_fusion.2
  66.4 5.3 bitcast_add_fusion.11
  76.9 4.0 fusion.98
  90.5 35.9 %while.56 = (s32[]{:T(128)}, f32[64,64,128]{2,1,0:T(8,128)S(1)}, s32[]{:T(128)}, s32[2,512]{1,0:T(2,128)S(1)}, f32[512,128,128]{2,1,0:T(8,128)}, /*index=5*/f32[...) while((s32[]{:T(128)}, f32[64,64,128]{2,1,0:T(8,128)S(1)}, ...), condition=%wide.region_5.6_spmd.clone, body=%wide.region_4.5_spmd.clone.sunk | while | flops 604769472 | bytes 11547951 | solution.py:46
  93.5 3.5 fusion.252
  102.5 3.5 fusion.252
  111.4 3.5 fusion.252
  131.2 268.8 %all-gather.3.cloned.1.call-done = f32[256,8192]{1,0:T(8,128)} async-done(((f32[64,8192]{1,0:T(8,128)}), f32[256,8192]{1,0:T(8,128)}) %all-gather.3.cloned.1.call-update) | async-done | bytes 8388624 | tf_op jit(solution)/shard_map/all_gather | solution.py:131
  400.0 7.9 fusion.150
  407.9 141.6 %all-gather.5.cloned.1.call-done = f32[256,8192]{1,0:T(8,128)} async-done(((f32[64,8192]{1,0:T(8,128)}), f32[256,8192]{1,0:T(8,128)}) %all-gather.5.cloned.1.call-update) | async-done | bytes 8388624 | tf_op jit(solution)/shard_map/all_gather | solution.py:132
  549.5 8.1 multiply_reduce_fusion.3
  563.6 36.3 %while.57 = (s32[]{:T(128)}, f32[64,64,128]{2,1,0:T(8,128)S(1)}, s32[]{:T(128)}, s32[2,512]{1,0:T(2,128)S(1)}, f32[512,128,128]{2,1,0:T(8,128)}, /*index=5*/f32[...) while((s32[]{:T(128)}, f32[64,64,128]{2,1,0:T(8,128)S(1)}, ...), condition=%wide.region_9.10_spmd.clone, body=%wide.region_8.9_spmd.clone.sunk | while | flops 604769472 | bytes 11547951 | solution.py:46
  566.6 3.5 fusion.260
  575.5 3.5 fusion.260
  584.5 3.5 fusion.260
  593.5 3.5 fusion.260
  603.2 4.1 fusion.95
  607.4 174.1 %all-reduce.9.cloned.1.call-done = f32[47,8192]{1,0:T(8,128)} async-done(((f32[47,8192]{1,0:T(8,128)}), f32[47,8192]{1,0:T(8,128)}) %all-reduce.9.cloned.1.call-update) | async-done | bytes 1540112 | tf_op jit(solution)/shard_map/psum | solution.py:137
  781.5 3.8 copy.92
  788.9 3.7 all-to-all-start
  801.5 4.2 all-to-all-start.1
  808.7 3.8 copy.94
  812.6 5.1 scatter_custom_fusion
  818.4 5.1 scatter_custom_fusion.1
  823.5 6.6 convolution_bitcast_fusion.4
  833.3 53.7 %while.58 = (s32[]{:T(128)}, f32[64,64,128]{2,1,0:T(8,128)}, s32[]{:T(128)}, s32[2,512]{1,0:T(2,128)S(1)}, f32[512,128,128]{2,1,0:T(8,128)}, /*index=5*/f32[64,6...) while((s32[]{:T(128)}, f32[64,64,128]{2,1,0:T(8,128)}, ...), condition=%wide.region_21.23_spmd.clone, body=%wide.region_20.22_spmd.clone.sunk | while | flops 604769472 | bytes 11547951 | solution.py:46
  836.3 5.7 fusion.268
  842.1 4.6 bitcast_add_fusion.14
  849.7 5.7 fusion.268
  855.5 4.6 bitcast_add_fusion.14
  863.0 5.7 fusion.268
  868.9 4.6 bitcast_add_fusion.14
  876.4 5.7 fusion.268
  882.3 4.6 bitcast_add_fusion.14
  887.1 11.3 multiply_reduce_fusion
  900.6 9.0 convolution_bitcast_fusion
  909.7 8.9 copy.105
  918.9 10.2 convolution_bitcast_fusion.1
  933.0 11.9 fusion.126
  944.9 10.6 fusion.127
  956.2 9.5 fusion.132
  965.7 6.7 convolution_bitcast_fusion.5
  972.5 250.0 %reduce-scatter.7.cloned.1.call-done = f32[64,8192]{1,0:T(8,128)} async-done(((f32[256,8192]{1,0:T(8,128)}), f32[64,8192]{1,0:T(8,128)}) %reduce-scatter.7.cloned.1.call-update) | async-done | bytes 2097168
  1222.5 3.9 copy.106
  1226.4 3.8 copy.97
  1230.4 45.3 %while.59 = (s32[]{:T(128)}, f32[64,64,128]{2,1,0:T(8,128)S(1)}, s32[]{:T(128)}, s32[2,512]{1,0:T(2,128)S(1)}, f32[512,128,128]{2,1,0:T(8,128)}, /*index=5*/f32[...) while((s32[]{:T(128)}, f32[64,64,128]{2,1,0:T(8,128)S(1)}, ...), condition=%wide.region_27.29_spmd.clone, body=%wide.region_26.28_spmd.clone.sunk | while | flops 604769472 | bytes 11547951 | solution.py:46
  1234.0 5.7 fusion.276
  1245.2 5.8 fusion.276
  1256.4 5.7 fusion.276
  1267.6 5.7 fusion.276
  1275.8 94.1 %reduce-scatter.5.cloned.1.call-done = f32[64,8192]{1,0:T(8,128)} async-done(((f32[256,8192]{1,0:T(8,128)}), f32[64,8192]{1,0:T(8,128)}) %reduce-scatter.5.cloned.1.call-update) | async-done | bytes 2097168 | tf_op jit(solution)/shard_map/reduce_scatter | solution.py:169
  1369.9 4.6 multiply_reduce_fusion.1
  1376.5 5.1 fusion.129
  1381.8 4.0 fusion.128
  1385.8 41.3 %all-reduce.11.cloned.1.call-done = f32[2,256,64]{1,2,0:T(8,128)} async-done(((f32[2,256,64]{1,2,0:T(8,128)}), f32[2,256,64]{1,2,0:T(8,128)}) %all-reduce.11.cloned.1.call-update) | async-done | bytes 131088 | tf_op jit(solution)/shard_map/psum | solution.py:182
  1428.8 23.5 %all-reduce.12 = (f32[]{:T(128)}, f32[2,100,64]{1,2,0:T(8,128)S(1)}, f32[2,64,47]{1,2,0:T(8,128)S(1)}, f32[2,2,64]{2,1,0:T(2,128)S(1)}) all-reduce(f32[]{:T(128)S(6)} %add.368, f32[2,100,64]{1,2,0:T(8,128)S(1)} %pad_maximum_fusion.1, f32[2,64,47]{1,2,0:T(8,128)S(1)} %pad_maximum_fusion.2, ...), channel_id=1, replica_groups=mesh['graph'=8,'col'=4] {'graph'}, use_global_device_ids=true, to_apply=%region_16.18 | all-reduce | flops 19073 | bytes 152584 | tf_op jit(solution)/shard_map/psum | solution.py:182
  (303 shorter events, 158.6 us)
Async XLA Ops:
  7.2 392.8 %all-gather.3.cloned.1.call-start = ((), (), s32[]{:S(2)}) async-start(), calls=%async_computation.4 | async-start | bytes 10485760 | tf_op jit(solution)/shard_map/all_gather | solution.py:131
  16.0 2.1 copy-start.12
  74.4 2.5 copy-start.7
  74.4 2.5 copy-start.14
  76.9 4.1 copy-start.9
  84.1 3.8 copy-start.2
  84.1 1.2 copy-start.25
  85.3 2.6 copy-start.27
  85.3 475.7 %copy-start.29 = (f32[64]{0:T(128)}, f32[64]{0:T(128)S(1)}, u32[]{:S(2)}) copy-start(f32[64]{0:T(128)S(1)} %get-tuple-element.598) | copy-start | bytes 772
  85.3 475.7 %copy-start.33 = (f32[64]{0:T(128)}, f32[64]{0:T(128)S(1)}, u32[]{:S(2)}) copy-start(f32[64]{0:T(128)S(1)} %get-tuple-element.601) | copy-start | bytes 772
  87.7 461.8 %all-gather.5.cloned.1.call-start = ((), (), s32[]{:S(2)}) async-start(), calls=%async_computation.5 | async-start | bytes 10485760 | tf_op jit(solution)/shard_map/all_gather | solution.py:132
  128.9 0.7 copy-start.26
  128.9 1.0 copy-start.15
  128.9 1.0 copy-start.38
  128.9 271.1 %copy-start.13 = (f32[2,256,64]{1,2,0:T(8,128)S(1)}, f32[2,256,64]{1,2,0:T(8,128)}, u32[]{:S(2)}) copy-start(f32[2,256,64]{1,2,0:T(8,128)} %param.37) | copy-start | bytes 393220
  128.9 652.6 %all-reduce.9.cloned.1.call-start = ((), (), s32[]{:S(2)}) async-start(), calls=%async_computation.6 | async-start | bytes 3145728 | tf_op jit(solution)/shard_map/psum | solution.py:137
  557.5 3.5 copy-start.5
  557.6 3.5 copy-start.31
  607.4 186.6 %copy-start.19 = (s32[1,8192]{1,0:T(1,128)S(1)}, s32[1,8192]{1,0:T(1,128)}, u32[]{:S(2)}) copy-start(s32[1,8192]{1,0:T(1,128)} %param.34) | copy-start | bytes 98308
  788.9 10.5 all-to-all-start
  801.5 16.2 %all-to-all-start.1 = ((f32[8,1,376]{2,1,0:T(1,128)}), f32[8,1,376]{2,1,0:T(1,128)S(1)}, u32[]{:S(2)}, u32[]{:S(2)}) async-start(f32[8,1,376]{2,1,0:T(1,128)} %reshape.521), calls=%async_computation.1 | async-start | bytes 24576 | tf_op jit(solution)/shard_map/all_to_all | solution.py:155
  805.7 416.8 %reduce-scatter.7.cloned.1.call-start = ((), (), s32[]{:S(2)}) async-start(), calls=%async_computation.9 | async-start | bytes 10485760
  887.0 11.4 copy-start.37
  887.0 11.4 copy-start.6
  887.0 11.4 copy-start.30
  887.0 11.4 copy-start.32
  899.3 1.3 copy-start
  918.6 451.3 %reduce-scatter.5.cloned.1.call-start = ((), (), s32[]{:S(2)}) async-start(), calls=%async_computation.7 | async-start | bytes 10485760 | tf_op jit(solution)/shard_map/reduce_scatter | solution.py:169
  929.1 0.8 copy-start.20
  929.1 498.0 %all-reduce.11.cloned.1.call-start = ((), (), s32[]{:S(2)}) async-start(), calls=%async_computation.8 | async-start | bytes 262144 | tf_op jit(solution)/shard_map/psum | solution.py:182
  933.0 11.9 copy-start.1
  956.2 9.5 copy-start.4
  956.2 9.5 copy-start.11
  1230.4 139.5 %copy-start.28 = (f32[64]{0:T(128)S(1)}, f32[64]{0:T(128)}, u32[]{:S(2)}) copy-start(f32[64]{0:T(128)} %copy-done.27) | copy-start | bytes 772
  1369.9 4.6 copy-start.36
  1369.9 4.7 copy-start.3
  1374.6 1.9 copy-start.8
  1376.5 5.1 copy-start.10
  1381.7 4.1 copy-start.39
  1381.7 4.1 copy-start.40
  1381.7 45.4 %copy-start.17 = (f32[2,256,64]{1,2,0:T(8,128)S(1)}, f32[2,256,64]{1,2,0:T(8,128)}, u32[]{:S(2)}) copy-start(f32[2,256,64]{1,2,0:T(8,128)} %param.45) | copy-start | bytes 393220
  1381.7 45.4 %copy-start.18 = (f32[2,256,64]{1,2,0:T(8,128)S(1)}, f32[2,256,64]{1,2,0:T(8,128)}, u32[]{:S(2)}) copy-start(f32[2,256,64]{1,2,0:T(8,128)} %param.41) | copy-start | bytes 393220
  1381.7 70.6 %copy-start.16 = (f32[2,64,47]{1,0,2:T(2,128)S(1)}, f32[2,64,47]{1,0,2:T(2,128)}, u32[]{:S(2)}) copy-start(f32[2,64,47]{1,0,2:T(2,128)} %param.38) | copy-start | bytes 72196
  1381.7 70.6 %copy-start.23 = (f32[2,64,47]{1,0,2:T(2,128)S(1)}, f32[2,64,47]{1,0,2:T(2,128)}, u32[]{:S(2)}) copy-start(f32[2,64,47]{1,0,2:T(2,128)} %param.46) | copy-start | bytes 72196
  1381.7 70.6 %copy-start.24 = (f32[2,64,47]{1,0,2:T(2,128)S(1)}, f32[2,64,47]{1,0,2:T(2,128)}, u32[]{:S(2)}) copy-start(f32[2,64,47]{1,0,2:T(2,128)} %param.42) | copy-start | bytes 72196
  1381.7 72.6 %copy-start.21 = (f32[2,100,64]{1,2,0:T(8,128)S(1)}, f32[2,100,64]{1,2,0:T(8,128)}, u32[]{:S(2)}) copy-start(f32[2,100,64]{1,2,0:T(8,128)} %param.44) | copy-start | bytes 153604
  1381.8 72.6 %copy-start.22 = (f32[2,100,64]{1,2,0:T(8,128)S(1)}, f32[2,100,64]{1,2,0:T(8,128)}, u32[]{:S(2)}) copy-start(f32[2,100,64]{1,2,0:T(8,128)} %param.40) | copy-start | bytes 153604
  1385.7 69.3 %copy-start.34 = (f32[2,2,64]{2,1,0:T(2,128)S(1)}, f32[2,2,64]{2,1,0:T(2,128)}, u32[]{:S(2)}) copy-start(f32[2,2,64]{2,1,0:T(2,128)} %param.47) | copy-start | bytes 3076
  1385.7 69.3 %copy-start.35 = (f32[2,2,64]{2,1,0:T(2,128)S(1)}, f32[2,2,64]{2,1,0:T(2,128)}, u32[]{:S(2)}) copy-start(f32[2,2,64]{2,1,0:T(2,128)} %param.43) | copy-start | bytes 3076
Sparse Core Ops, SparseCore 0:
  87.8 312.1 all-gather.2
  401.5 147.8 all-gather.4
  607.4 174.0 all-reduce.8
  918.7 303.7 reduce-scatter.6
  1224.7 145.1 reduce-scatter.4
  1373.4 53.6 all-reduce.10
where the time goes:
time: 1480 us; the launch traced here: 1460 us
  waiting for transfers between devices  970 us (66%)
  matrix products  276 us (19%)
  local copies, waits for them, and re-layouts  106 us (7%)
  other arithmetic  58.4 us (4%)
  blocking collectives  23.5 us (2%)
  between operations  19.5 us (1%)
    all_gather x1, waiting for transfers between devices, per_device(): lax.all_gather(hidden_one, 'col', axis=0, tiled=True)  269 us
    unnamed x7, waiting for transfers between devices  250 us
    psum x1, waiting for transfers between devices, per_device(): logits = lax.psum(project(weight_head, hidden_two, spread_two), 'col')  174 us
    all_gather x1, waiting for transfers between devices, per_device(): lax.all_gather(spread_one, 'col', axis=0, tiled=True)  142 us
    reduce_scatter x1, waiting for transfers between devices, per_device(): lax.psum_scatter(back_project(weight_second[0], grad_pre_two), 'col', sca...  94.1 us
    dot_general x20, matrix products, one_slab(): jnp.einsum('cbi,br->cri', product * alive_here[None, :, None], onehot, pr...  67.9 us
    dot_general x6, matrix products, outer_grad(): return jnp.einsum('fn,on->fo', inputs, upstream, precision=PRECISE)  47.8 us
    dot_general x12, matrix products, one_slab(): jnp.einsum('cbj,bji->cbi', shaped[:, cols_here, :], slab_values, precisio...  46.7 us
  transfers between devices with their start and end apart: 8, of which 6 were waited for; matrix products, arithmetic and copies ran while one was open for 13% of the time, Pallas kernels for 0%

commit v1 on v0

v1 whole, which is shorter than its diff:
```python
import functools
import jax, jax.numpy as jnp
from jax import lax
from jax.experimental import pallas as pl
from jax.experimental.pallas import tpu as pltpu
BF=jnp.bfloat16; F32=jnp.float32; I32=jnp.int32
VLIM=60<<20
def dot(a,b): return jnp.dot(a,b,preferred_element_type=F32)
def dot_nt(a,b): return lax.dot_general(a,b,(((1,),(1,)),((),())),preferred_element_type=F32)
def split(x):
    h=x.astype(BF); return h,(x-h.astype(F32)).astype(BF)
GROUP=16

def make_lists(blk_l, blk_c, lb, NB, L):
    BLK=blk_l.shape[1]
    b_c=lax.broadcasted_iota(I32,(BLK,1),0); b_l=lax.broadcasted_iota(I32,(1,BLK),1)
    live=b_c<lb
    r_l=lax.broadcasted_iota(I32,(1,128),1)
    p_l=lax.broadcasted_iota(I32,(1,L),1)
    outs=[];counts=[]
    for k in range(2):
        kc=blk_c[:,k:k+1]; oc=blk_c[:,1-k:2-k]; kl=blk_l[k:k+1,:]
        before=jnp.where((kl==kc)&(b_l<b_c),1.0,0.0)
        rank=jnp.sum(before,axis=1,keepdims=True)
        cnt=jnp.sum(jnp.where((kc==r_l)&live,1.0,0.0),axis=0,keepdims=True)
        half=jnp.floor(cnt*0.5)
        pc=cnt+(cnt-2.0*half)
        start=jnp.sum(jnp.where(r_l<kc,pc,0.0),axis=1,keepdims=True)
        pos=jnp.where(live,(start+rank).astype(I32),-1)
        null=BLK+NB*(1<<20)
        enc=b_c+oc*(1<<12)+kc*(1<<20)-null
        lo=jnp.where(pos==p_l,(enc&0xfff).astype(F32),0.0); hi=jnp.where(pos==p_l,(enc>>12).astype(F32),0.0)
        lo=jnp.sum(lo,axis=0,keepdims=True).astype(I32); hi=jnp.sum(hi,axis=0,keepdims=True).astype(I32)
        outs.append(hi*4096+lo+null)
        counts.append(jnp.broadcast_to(jnp.sum(pc,axis=1,keepdims=True).astype(I32),(1,L)))
    return jnp.concatenate(outs+counts+[jnp.zeros((4,L),I32)],axis=0)

def pair_fields(lists, which, q):
    e0=lists[which,2*q]; e1=lists[which,2*q+1]
    return e0>>20, (e0>>12)&0xff, (e1>>12)&0xff, e0&0xfff, e1&0xfff

def agg_nodes(lists, which, S, v, acc):
    n=lists[2+which,0]//2
    def step(s,_):
        for u in range(GROUP):
            r,c0,c1,b0,b1=pair_fields(lists,which,s*GROUP+u)
            lhs=jnp.concatenate([S[b0],S[b1]],axis=1)
            rhs=jnp.concatenate([v[c0],v[c1]],axis=0)
            acc[r]+=dot(lhs,rhs)
        return 0
    lax.fori_loop(0,pl.cdiv(n,GROUP),step,0)

def k0(sizes, blk_l, blk_c, feat, vals, S_out, lists_out, fth_out, ftl_out, af_out,
       S, lists_v, lists_s, ft_v, fth, ftl, acc, af, buf, sem_in, sem_f, sem_l, sem_o, sem_S, CH, NBUF):
    nb=sizes[0]; lb=sizes[1]
    NB=acc.shape[0]-1; BLK=vals.shape[0]; FIN=feat.shape[0]
    L=lists_v.shape[1]
    nch=pl.cdiv(lb,CH)
    def chunk_in(i,slot): return pltpu.make_async_copy(vals.at[pl.ds(i*CH,CH)],buf.at[slot],sem_in.at[slot])
    def chunk_out(i): return pltpu.make_async_copy(S.at[pl.ds(i*CH,CH)],S_out.at[pl.ds(i*CH,CH)],sem_S.at[i])
    for i in range(NBUF):
        @pl.when(i<nch)
        def _(): chunk_in(i,i).start()
    cf=pltpu.make_async_copy(feat,ft_v,sem_f); cf.start()
    lists_v[...]=make_lists(blk_l[...],blk_c[...],lb,NB,L)
    cl=pltpu.make_async_copy(lists_v,lists_s,sem_l.at[0]); cl.start()
    co=pltpu.make_async_copy(lists_v,lists_out,sem_l.at[1]); co.start()
    S[BLK]=jnp.zeros((128,128),BF)
    acc[...]=jnp.zeros(acc.shape,F32)
    cf.wait()
    per=CH*NB//BLK
    def conv(i,_):
        slot=lax.rem(i,NBUF)
        chunk_in(i,slot).wait()
        for k in range(CH):
            S[i*CH+k]=buf[slot,k].T.astype(BF)
        for k in range(per):
            b=i*per+k
            x=ft_v[:,pl.ds(pl.multiple_of(b*128,128),128)]
            x=jnp.concatenate([x,jnp.zeros((128-FIN,128),F32)],axis=0).T
            h,l=split(x); fth[b]=h; ftl[b]=l
        @pl.when(i+NBUF<nch)
        def _(): chunk_in(i+NBUF,slot).start()
        chunk_out(i).start()
        return 0
    lax.fori_loop(0,nch,conv,0)
    c1=pltpu.make_async_copy(fth,fth_out,sem_o.at[0]); c1.start()
    c2=pltpu.make_async_copy(ftl,ftl_out,sem_o.at[1]); c2.start()
    cl.wait()
    agg_nodes(lists_s,0,S,fth,acc)
    def fin(b,_):
        af[b]=acc[b].astype(BF); return 0
    lax.fori_loop(0,nb,fin,0)
    c3=pltpu.make_async_copy(af,af_out,sem_o.at[2]); c3.start()
    lax.fori_loop(0,nch,lambda i,_:(chunk_out(i).wait(),0)[1],0)
    c1.wait();c2.wait();c3.wait();co.wait()

def call_k0(sizes, blk, feat, vals, CH=16, NBUF=12):
    FIN,N=feat.shape; NB=N//128; BLK=vals.shape[0]; L=pl.cdiv(BLK+NB,128)*128
    CH=min(CH,BLK)
    sds=jax.ShapeDtypeStruct
    ANY=pl.BlockSpec(memory_space=pl.ANY); VM=pl.BlockSpec(memory_space=pltpu.VMEM); SM=pl.BlockSpec(memory_space=pltpu.SMEM)
    return pl.pallas_call(functools.partial(k0,CH=CH,NBUF=NBUF),
        out_shape=(sds((BLK,128,128),BF),sds((8,L),I32),sds((NB,128,128),BF),sds((NB,128,128),BF),sds((NB,128,128),BF)),
        in_specs=[SM,VM,VM,ANY,ANY],out_specs=[ANY]*5,
        scratch_shapes=[pltpu.VMEM((BLK+1,128,128),BF),pltpu.VMEM((8,L),I32),pltpu.SMEM((8,L),I32),pltpu.VMEM((FIN,N),F32),
            pltpu.VMEM((NB,128,128),BF),pltpu.VMEM((NB,128,128),BF),pltpu.VMEM((NB+1,128,128),F32),pltpu.VMEM((NB,128,128),BF),
            pltpu.VMEM((NBUF,CH,128,128),F32),
            pltpu.SemaphoreType.DMA((NBUF,)),pltpu.SemaphoreType.DMA(()),pltpu.SemaphoreType.DMA((2,)),pltpu.SemaphoreType.DMA((3,)),pltpu.SemaphoreType.DMA((pl.cdiv(BLK,CH),))],
        compiler_params=pltpu.CompilerParams(vmem_limit_bytes=VLIM))(sizes,blk,blk.T,feat,vals)
G0=0.7978845608; G1=0.044715
EPS=1e-5
def for_blocks(nb,U,fn):
    full=nb//U
    def many(s,_): fn(s*U,U); return 0
    def one(b,_): fn(b,1); return 0
    lax.fori_loop(0,full,many,0)
    if U>1: lax.fori_loop(full*U,nb,one,0)
def rows8(x): return jnp.sum(x.reshape(x.shape[0]//8,8,x.shape[1]),axis=0)
def blk(ref,b0,U):
    x=ref[pl.ds(b0,U)]; return x.reshape(U*x.shape[1],x.shape[2])
def put_blk(ref,b0,U,x): ref[pl.ds(b0,U)]=x.reshape((U,)+ref.shape[1:])
def gelu(u):
    return (0.5*u)*(1.0+jnp.tanh(u*(G0+(G0*G1)*(u*u))))

def norm_stats(pre,nb,count,sums,st,row):
    mean=jnp.sum(sums[0],axis=0,keepdims=True)/count
    sums[1]=jnp.zeros_like(sums[1])
    def var(b0,U):
        x=blk(pre,b0,U)-mean
        sums[1]+=rows8(x*x)
    for_blocks(nb,4,var)
    v=jnp.sum(sums[1],axis=0,keepdims=True)/count
    inv=lax.rsqrt(v+EPS)
    st[row:row+1,:]=mean; st[row+1:row+2,:]=inv
    return mean,inv

def kb(sizes,lists,S_in,fth_in,ftl_in,af_in,w1,w2,wh,npar,pairs,
       h1h_out,h1l_out,ah_out,pre_out,st_out,h2t_out,lg_out,own_out,
       S,fth,ftl,af,h1h,h1l,acc,pre,zz,acc2,lg,h2t,sums,st,sem_i,sem_o):
    nb=sizes[0]; NB=fth.shape[0]; BLK=S_in.shape[0]; KC=lg.shape[1]; MY=h2t.shape[1]//2
    count=(nb*128).astype(F32)
    cs=[pltpu.make_async_copy(a,b,sem_i.at[i]) for i,(a,b) in enumerate(((fth_in,fth),(ftl_in,ftl),(af_in,af),(S_in,S.at[pl.ds(0,BLK)])))]
    for c in cs: c.start()
    S[BLK]=jnp.zeros((128,128),BF)
    sums[...]=jnp.zeros_like(sums)
    for c in cs[:3]: c.wait()
    def p1(b0,U):
        h=blk(fth,b0,U)
        x=jnp.concatenate([h,blk(ftl,b0,U),h,blk(af,b0,U)],axis=1)
        y=dot(x,w1[...])
        put_blk(pre,b0,U,y)
        sums[0]+=rows8(y)
    for_blocks(nb,4,p1)
    mean,inv=norm_stats(pre,nb,count,sums,st,0)
    a=npar[0:1,:]*inv; c=npar[1:2,:]-mean*a
    def n1(b0,U):
        h,l=split(gelu(blk(pre,b0,U)*a+c))
        put_blk(h1h,b0,U,h); put_blk(h1l,b0,U,l)
        put_blk(acc,b0,U,jnp.zeros((U*128,acc.shape[2]),F32))
    for_blocks(nb,4,n1)
    acc[NB]=jnp.zeros(acc.shape[1:],F32)
    oh=[pltpu.make_async_copy(h1h,h1h_out,sem_o.at[0]),pltpu.make_async_copy(h1l,h1l_out,sem_o.at[1])]
    for o in oh: o.start()
    cs[3].wait()
    agg_nodes(lists,0,S,h1h,acc)
    oa=pltpu.make_async_copy(acc.at[pl.ds(0,NB)],ah_out,sem_o.at[2]); oa.start()
    sums[...]=jnp.zeros_like(sums)
    def p2(b0,U):
        h=blk(h1h,b0,U); l=blk(h1l,b0,U); ah,al=split(blk(acc,b0,U))
        y=dot(jnp.concatenate([h,l,h,ah,al,ah],axis=1),w2[...])
        put_blk(pre,b0,U,y)
        sums[0]+=rows8(y)
    for_blocks(nb,2,p2)
    op=pltpu.make_async_copy(pre,pre_out,sem_o.at[3]); op.start()
    mean2,inv2=norm_stats(pre,nb,count,sums,st,2)
    a2=npar[2:3,:]*inv2; c2=npar[3:4,:]-mean2*a2
    def n2(b0,U):
        h,l=split(gelu(blk(pre,b0,U)*a2+c2))
        r=dot_nt(wh[...],h); r2=dot_nt(wh[0:KC,:],l)
        d=r[0:KC]+r[2*KC:3*KC]+r2
        zh,zl=split(r[KC:2*KC]+r[3*KC:4*KC])
        t=jnp.concatenate([h[:,:MY],l[:,:MY]],axis=1)
        for k in range(U):
            w=slice(k*128,k*128+128)
            lg[b0+k]=d[:,w]
            zz[b0+k]=jnp.concatenate([zh[:,w],zl[:,w]],axis=0)
            h2t[b0+k]=t[w].T
            acc2[b0+k]=jnp.zeros(acc2.shape[1:],F32)
    for_blocks(nb,2,n2)
    acc2[NB]=jnp.zeros(acc2.shape[1:],F32)
    ot=pltpu.make_async_copy(h2t,h2t_out,sem_o.at[4]); ot.start()
    agg_rows(lists,0,S,zz,acc2,True)
    own_out[...]=jnp.zeros_like(own_out)
    def fin(b0,U):
        parts=[]; hot=[]
        for k in range(U):
            x=acc2[b0+k]; y=lg[b0+k]+x[:KC]+x[KC:]; lg[b0+k]=y
            h,l=split(y); parts.append(jnp.concatenate([h,l],axis=0)); hot.append(one_hot(pairs,b0+k))
        r=dot_nt(jnp.concatenate(parts,axis=1),jnp.concatenate(hot,axis=1))
        own_out[...]+=r[:KC]+r[KC:]
    for_blocks(nb,4,fin)
    ol=pltpu.make_async_copy(lg,lg_out,sem_o.at[5]); ol.start()
    st_out[...]=st[...]
    for o in (*oh,oa,op,ot,ol): o.wait()

def one_hot(pairs,b):
    return jnp.where(pairs[...]==lax.broadcasted_iota(I32,(1,128),1)+b*128,1.0,0.0).astype(BF)

def agg_rows(lists,which,S,v,acc,nt):
    n=lists[2+which,0]//2
    def step(s,_):
        for u in range(GROUP):
            r,c0,c1,b0,b1=pair_fields(lists,which,s*GROUP+u)
            lhs=jnp.concatenate([v[c0],v[c1]],axis=1)
            if nt: acc[r]+=dot_nt(lhs,jnp.concatenate([S[b0],S[b1]],axis=1))
            else: acc[r]+=dot(lhs,jnp.concatenate([S[b0],S[b1]],axis=0))
        return 0
    lax.fori_loop(0,pl.cdiv(n,GROUP),step,0)

def call_kb(sizes,lists,S,fth,ftl,af,w1,w2,wh,npar,pairs,MY):
    NB=fth.shape[0]; BLK=S.shape[0]; H=w2.shape[1]; KC=wh.shape[0]//4
    sds=jax.ShapeDtypeStruct
    ANY=pl.BlockSpec(memory_space=pl.ANY); VM=pl.BlockSpec(memory_space=pltpu.VMEM); SM=pl.BlockSpec(memory_space=pltpu.SMEM)
    V=pltpu.VMEM
    return pl.pallas_call(kb,
        out_shape=(sds((NB,128,H),BF),sds((NB,128,H),BF),sds((NB,128,H),F32),sds((NB,128,H),F32),sds((8,H),F32),sds((NB,2*MY,128),BF),sds((NB,KC,128),F32),sds((KC,pairs.shape[0]),F32)),
        in_specs=[SM,SM]+[ANY]*4+[VM]*5,out_specs=[ANY]*4+[VM]+[ANY]*2+[VM],
        scratch_shapes=[V((BLK+1,128,128),BF)]+[V((NB,128,128),BF)]*3+[V((NB,128,H),BF)]*2+[V((NB+1,128,H),F32),V((NB,128,H),F32),
            V((NB,2*KC,128),BF),V((NB+1,2*KC,128),F32),V((NB,KC,128),F32),V((NB,2*MY,128),BF),V((2,8,H),F32),V((8,H),F32),
            pltpu.SemaphoreType.DMA((4,)),pltpu.SemaphoreType.DMA((6,))],
        compiler_params=pltpu.CompilerParams(vmem_limit_bytes=VLIM))(sizes,lists,S,fth,ftl,af,w1,w2,wh,npar,pairs)

def split_x(x):
    h=lax.reduce_precision(x,8,7); return h.astype(BF),(x-h).astype(BF)
def prep_weights(wf,ws,wh,npar,MY):
    FIN=wf.shape[1]; C=wh.shape[2]; CP=-(-C//16)*16
    def padk(w): return jnp.pad(w,((0,128-FIN),(0,0)))
    f0h,f0l=split_x(padk(wf[0])); f1h=padk(wf[1]).astype(BF)
    w1=jnp.concatenate([f0h,f0h,f0l,f1h],axis=0)
    (ah,al),(bh,bl)=split_x(ws[0]),split_x(ws[1])
    w2=jnp.concatenate([ah,ah,al,bh,bh,bl],axis=0)
    hp=jnp.pad(wh,((0,0),(0,0),(0,CP-C))).transpose(0,2,1)
    (ch,cl),(dh,dl)=split_x(hp[0]),split_x(hp[1])
    whc=jnp.concatenate([ch,dh,cl,dl],axis=0)
    n8=jnp.concatenate([npar.reshape(4,-1),jnp.zeros((4,npar.shape[2]),F32)],axis=0)
    m0h=f0h[:,:MY].T; m0l=f0l[:,:MY].T
    w1m=jnp.concatenate([m0h,m0h,m0l,f1h[:,:MY].T],axis=1)
    z=jnp.zeros((128-2*CP,hp.shape[2]),BF)
    th=jnp.concatenate([ch,dh,z],axis=0); tl=jnp.concatenate([cl,dl,z],axis=0)
    wt=jnp.concatenate([th,th,tl],axis=0)
    w2m=jnp.concatenate([ah[:MY],al[:MY],bh[:MY],bl[:MY]],axis=0)
    nc=n8[:,:MY].T
    return (w1,w2,whc,n8),(w1m,wt,w2m,n8,nc)
def dgelu(u):
    q=u*u
    t=jnp.tanh(u*(G0+(G0*G1)*q))
    return 0.5*(1.0+t)+(0.5*u)*(1.0-t*t)*(G0+(3.0*G0*G1)*q)

def kc(sizes,lists,S_in,fth_in,ftl_in,af_in,h1h_in,h1l_in,ah_in,pre_in,h2t_in,lg_in,st,own,recv,labels,pairs,w1m,wt,w2m,npar,ncol,
       g_out,
       S,fth,ftl,af,rh,rl,ra,pre,du,h2t,lg,gz,acc3,d0,t1,pre1,sums,cross,RH,RS,RL,R1,R2,colsum,sem_i,sem_r,CLS):
    nb=sizes[0]; BLK=S_in.shape[0]; NB=fth.shape[0]; CP=lg.shape[1]; MY=t1.shape[1]; P2=own.shape[1]; H=pre.shape[2]; NS=rh.shape[0]
    count=(nb*128).astype(F32); total=sizes[2].astype(F32)
    ins=((lg_in,lg),(S_in,S.at[pl.ds(0,BLK)]),(pre_in,pre),(h2t_in,h2t),(fth_in,fth),(ftl_in,ftl),(af_in,af))
    cs=[pltpu.make_async_copy(a,b,sem_i.at[i]) for i,(a,b) in enumerate(ins)]
    for c in cs: c.start()
    nch=pl.cdiv(nb,2)
    def ring(i):
        s=lax.rem(i,NS)
        return [pltpu.make_async_copy(a.at[pl.ds(i*2,2)],b.at[s],sem_r.at[s,k]) for k,(a,b) in enumerate(((h1h_in,rh),(h1l_in,rl),(ah_in,ra)))]
    for i in range(NS):
        @pl.when(i<nch)
        def _():
            for c in ring(i): c.start()
    S[BLK]=jnp.zeros((128,128),BF)
    for r in (sums,cross,RH,RS,RL,R1,R2,colsum): r[...]=jnp.zeros_like(r)
    acc3[NB]=jnp.zeros(acc3.shape[1:],F32)
    half=P2//2
    o=own[...]; r=recv[...]
    D=o-jnp.concatenate([r[:,half:],r[:,:half]],axis=1)
    pair_loss=0.5*jnp.sum(D[:,half:]*D[:,half:])
    Dh,Dl=split(D/total); D2=jnp.concatenate([Dh,Dl],axis=0)
    cs[0].wait()
    def soft(b0,U):
        hot=jnp.concatenate([one_hot(pairs,b0+k) for k in range(U)],axis=1)
        add=dot(D2,hot); add=add[:CP]+add[CP:]
        x=jnp.concatenate([lg[b0+k] for k in range(U)],axis=1)
        lab=jnp.concatenate([labels[b0+k] for k in range(U)],axis=1)
        row=lax.broadcasted_iota(I32,(CP,1),0)
        xm=jnp.where(row<CLS,x,-1e30)
        mx=jnp.max(xm,axis=0,keepdims=True)
        e=jnp.exp(xm-mx); s=jnp.sum(e,axis=0,keepdims=True)
        hit=jnp.where(row==lab,1.0,0.0)
        c=mx+jnp.log(s)-jnp.sum(hit*x,axis=0,keepdims=True)
        g=(e/s-hit)/total+add
        h,l=split(g)
        for k in range(U):
            w=slice(k*128,k*128+128)
            cross[...]+=c[:,w]
            lg[b0+k]=g[:,w]
            gz[b0+k]=jnp.concatenate([h[:,w],l[:,w]],axis=0)
            acc3[b0+k]=jnp.zeros(acc3.shape[1:],F32)
    for_blocks(nb,4,soft)
    cs[1].wait()
    agg_rows(lists,1,S,gz,acc3,False)
    for c in cs[2:]: c.wait()
    mean2=st[2:3,:]; inv2=st[3:4,:]
    gain2=npar[2:3,:]; a2=gain2*inv2; c2=npar[3:4,:]-mean2*a2
    def back2(b0,U):
        T=[];ads=[]
        for k in range(U):
            ad=acc3[b0+k]; ad=ad[:CP]+ad[CP:]
            T.append(jnp.concatenate([lg[b0+k],ad,jnp.zeros((128-2*CP,128),F32)],axis=0).T)
            ads.append(ad.astype(BF))
        th,tl=split(jnp.concatenate(T,axis=0))
        gh=dot(jnp.concatenate([th,tl,th],axis=1),wt[...])
        hh=jnp.concatenate([h2t[b0+k] for k in range(U)],axis=1)
        gg=jnp.concatenate([jnp.concatenate([gz[b0+k] for k in range(U)],axis=1),jnp.concatenate(ads,axis=1)],axis=0)
        RH[...]+=dot_nt(hh,gg)
        y=blk(pre,b0,U)
        d=gh*dgelu(y*a2+c2)
        put_blk(du,b0,U,d)
        sums[0]+=rows8(d); sums[1]+=rows8(d*((y-mean2)*inv2))
    for_blocks(nb,2,back2)
    sb2=jnp.sum(sums[0],axis=0,keepdims=True); sg2=jnp.sum(sums[1],axis=0,keepdims=True)
    A2=-a2*inv2*sg2/count; C2=-a2*sb2/count-A2*mean2
    def proj(b0,U):
        i=b0//2; s=lax.rem(i,NS)
        for c in ring(i): c.wait()
        gp=blk(du,b0,U)*a2+blk(pre,b0,U)*A2+C2
        h,l=split(gp)
        r=dot_nt(w2m[...],h); rl2=dot_nt(w2m[0:MY,:],l)
        d=r[:MY]+r[MY:2*MY]+rl2; t=(r[2*MY:3*MY]+r[3*MY:]).astype(BF)
        for k in range(U):
            w=slice(k*128,k*128+128)
            d0[b0+k]=d[:,w]; t1[b0+k]=t[:,w]
        gt=jnp.concatenate([h[:,:MY],l[:,:MY]],axis=1)
        gt=jnp.concatenate([gt[k*128:k*128+128].T for k in range(U)],axis=1)
        f=lambda ref: ref[s,0:U].reshape(U*128,H)
        ah,al=split(f(ra))
        RS[...]+=dot(gt,jnp.concatenate([f(rh),ah],axis=1))
        RL[...]+=dot(gt[:MY],jnp.concatenate([f(rl),al],axis=1))
        @pl.when(i+NS<nch)
        def _():
            for c in ring(i+NS): c.start()
    for_blocks(nb,2,proj)
    d0[NB]=jnp.zeros(d0.shape[1:],F32)
    agg_rows(lists,1,S,t1,d0,False)
    def pre_one(b0,U):
        h=blk(fth,b0,U)
        y=dot_nt(w1m[...],jnp.concatenate([h,blk(ftl,b0,U),h,blk(af,b0,U)],axis=1))
        for k in range(U):
            p=y[:,k*128:k*128+128]
            pre1[b0+k]=p; colsum[0]+=p
    for_blocks(nb,2,pre_one)
    lane=lambda x: jnp.sum(x,axis=1,keepdims=True)
    mean1=lane(colsum[0])/count
    def var1(b0,U):
        for k in range(U):
            p=pre1[b0+k]-mean1; colsum[1]+=p*p
    for_blocks(nb,4,var1)
    inv1=lax.rsqrt(lane(colsum[1])/count+EPS)
    a1=ncol[:,0:1]*inv1; c1=ncol[:,1:2]-mean1*a1
    def back1(b0,U):
        for k in range(U):
            p=pre1[b0+k]
            d=d0[b0+k]*dgelu(p*a1+c1)
            d0[b0+k]=d
            colsum[2]+=d; colsum[3]+=d*((p-mean1)*inv1)
    for_blocks(nb,4,back1)
    sb1=lane(colsum[2]); sg1=lane(colsum[3])
    A1=-a1*inv1*sg1/count; C1=-a1*sb1/count-A1*mean1
    def first(b0,U):
        h,l=split(jnp.concatenate([d0[b0+k]*a1+pre1[b0+k]*A1+C1 for k in range(U)],axis=1))
        R1[...]+=dot(jnp.concatenate([h,l],axis=0),blk(fth,b0,U))
        R2[...]+=dot(h,jnp.concatenate([blk(ftl,b0,U),blk(af,b0,U)],axis=1))
    for_blocks(nb,2,first)
    RSv=RS[...]; gs=RSv[:MY]+RSv[MY:]+RL[...]
    nh=2*H//128
    for k in range(nh): g_out[k*MY:(k+1)*MY,:]=gs[:,k*128:k*128+128]
    R1v=R1[...]; R2v=R2[...]
    q=nh*MY
    g_out[q:q+MY,:]=R1v[:MY]+R1v[MY:]+R2v[:,:128]
    g_out[q+MY:q+2*MY,:]=R2v[:,128:]
    RHv=RH[...]; gh=RHv[:MY]+RHv[MY:]
    gh=jnp.concatenate([RHv[:MY,:CP]+RHv[:MY,CP:2*CP]+RHv[MY:,:CP],gh[:,2*CP:3*CP],sg1,sb1,jnp.zeros((MY,128-2*CP-2),F32)],axis=1)
    g_out[q+2*MY:q+3*MY,:]=gh
    loss=jnp.sum(cross[...])+pair_loss
    tail=jnp.concatenate([jnp.concatenate([sg2[:,:MY],sb2[:,:MY]]+([jnp.zeros((1,128-2*MY),F32)] if MY<64 else []),axis=1),jnp.broadcast_to(loss,(1,128)),jnp.zeros((6,128),F32)],axis=0)
    g_out[q+3*MY:,:]=tail

def call_kc(sizes,lists,S,fth,ftl,af,h1h,h1l,ah,pre,h2t,lg,st,own,recv,labels,pairs,w1m,wt,w2m,npar,ncol,CLS):
    NB=fth.shape[0]; BLK=S.shape[0]; H=pre.shape[2]; CP=lg.shape[1]; MY=ncol.shape[0]; NS=min(8,NB//2)
    sds=jax.ShapeDtypeStruct
    ANY=pl.BlockSpec(memory_space=pl.ANY); VM=pl.BlockSpec(memory_space=pltpu.VMEM); SM=pl.BlockSpec(memory_space=pltpu.SMEM)
    V=pltpu.VMEM
    rows=2*H//128*MY+3*MY+8
    return pl.pallas_call(functools.partial(kc,CLS=CLS),out_shape=sds((rows,128),F32),
        in_specs=[SM,SM]+[ANY]*10+[VM]*10,out_specs=VM,
        scratch_shapes=[V((BLK+1,128,128),BF)]+[V((NB,128,128),BF)]*3+[V((NS,2,128,H),BF)]*2+[V((NS,2,128,H),F32),
            V((NB,128,H),F32),V((NB,128,H),F32),V((NB,2*MY,128),BF),V((NB,CP,128),F32),V((NB,2*CP,128),BF),V((NB+1,2*CP,128),F32),
            V((NB+1,MY,128),F32),V((NB,MY,128),BF),V((NB,MY,128),F32),
            V((2,8,H),F32),V((1,128),F32),V((2*MY,3*CP),F32),V((2*MY,2*H),F32),V((MY,2*H),F32),V((2*MY,128),F32),V((MY,256),F32),V((4,MY,128),F32),
            pltpu.SemaphoreType.DMA((7,)),pltpu.SemaphoreType.DMA((NS,3))],
        compiler_params=pltpu.CompilerParams(vmem_limit_bytes=VLIM))(sizes,lists,S,fth,ftl,af,h1h,h1l,ah,pre,h2t,lg,st,own,recv,labels,pairs,w1m,wt,w2m,npar,ncol)

MOMENTUM=0.9; STEP_RATE=2.0; AVERAGE_KEEP=0.9

def renew(weight, momentum, average, gradient):
    momentum_new = MOMENTUM * momentum + gradient
    weight_new = weight - STEP_RATE * (gradient + MOMENTUM * momentum_new)
    average_new = AVERAGE_KEEP * average + (1.0 - AVERAGE_KEEP) * weight_new
    return momentum_new, average_new, weight_new

def turn(x, axis, by):
    return lax.dynamic_slice_in_dim(jnp.concatenate([x,x],axis=axis),by,x.shape[axis],axis)

def per_device(n_col, features, blocks, block_values, group_sizes, labels, pair_nodes, weight_first, weight_second, weight_head,
               norm_params, momentum_first, momentum_second, momentum_head, momentum_norms, average_first, average_second,
               average_head, average_norms):
    col=lax.axis_index("col")
    MY=weight_first.shape[2]; H=MY*n_col; FIN=weight_first.shape[1]; CLS=weight_head.shape[2]; CP=-(-CLS//16)*16
    G=group_sizes.shape[0]; N=features.shape[2]; NB=N//128
    shards=(weight_first,weight_second,weight_head,norm_params)
    flat=jnp.concatenate([x.reshape(-1) for x in shards])
    parts=[flat]+[lax.ppermute(flat,"col",[((j+k)%n_col,j) for j in range(n_col)]) for k in range(1,n_col)]
    own_sizes=lax.dynamic_slice_in_dim(group_sizes,lax.axis_index("graph"),1,0)[0]
    total=jnp.sum(group_sizes[:,0])
    sizes=jnp.stack([own_sizes[0]//128,own_sizes[1],total])
    S,lists,fth,ftl,af=call_k0(sizes,blocks[0],features[0],block_values[0])
    def whole(i,axis):
        start=sum(x.size for x in shards[:i]); x=shards[i]
        return jnp.concatenate([p[start:start+x.size].reshape(x.shape) for p in parts],axis=axis)
    wf=whole(0,2); ws=turn(whole(1,2),1,col*MY); wh=whole(2,1); npar=whole(3,2)
    wb,wc=prep_weights(wf,ws,wh,npar,MY)
    pairs=pair_nodes[0].reshape(-1,1)
    h1h,h1l,ah,pre,st,h2t,lg,own=call_kb(sizes,lists,S,fth,ftl,af,*wb,pairs,MY=MY)
    P2=own.shape[1]
    recv=lax.all_to_all(own.reshape(CP,2,G,P2//2//G),"graph",split_axis=2,concat_axis=2,tiled=True).reshape(CP,P2)
    g=call_kc(sizes,lists,S,fth,ftl,af,h1h,h1l,ah,pre,h2t,lg,st,own,recv,labels[0].reshape(NB,1,128),pairs,*wc,CLS=CLS)
    g=lax.psum(g,"graph")
    nh=2*H//128; q=nh*MY
    gs=g[:q].reshape(2,H//128,MY,128).transpose(0,1,3,2).reshape(2,H,MY)
    gs=turn(gs,1,(n_col-col)%n_col*MY)
    gf=g[q:q+2*MY].reshape(2,MY,128)[:,:,:FIN].transpose(0,2,1)
    hd=g[q+2*MY:q+3*MY]; tail=g[q+3*MY:]
    gh=jnp.stack([hd[:,:CLS],hd[:,CP:CP+CLS]])
    gn=jnp.stack([hd[:,2*CP:2*CP+2].T,tail[0,:2*MY].reshape(2,MY)])
    first=renew(weight_first,momentum_first,average_first,gf)
    second=renew(weight_second,momentum_second,average_second,gs)
    head=renew(weight_head,momentum_head,average_head,gh)
    norms=renew(norm_params,momentum_norms,average_norms,gn)
    return (tail[1,0],total.astype(F32),*first,*second,*head,*norms)

def solution(mesh):
    P=jax.sharding.PartitionSpec
    unit=P(None,None,"col"); head=P(None,"col",None)
    weights=(unit,unit,head,unit)
    in_specs=(P("graph",None,None),P("graph",None,None),P("graph",None,None,None),P(),P("graph",None),P("graph",None,None,None))+weights*3
    out_specs=(P(),P())+(unit,)*6+(head,)*3+(unit,)*3
    return jax.shard_map(functools.partial(per_device,mesh.shape["col"]),mesh=mesh,in_specs=in_specs,out_specs=out_specs,check_vma=False)
```

time: 1480 us -> 273 us (0.18)
  waiting for transfers between devices: 970 us -> 89.9 us
  matrix products: 276 us -> 0 us
  local copies, waits for them, and re-layouts: 106 us -> 30.3 us
  Pallas kernels: 0 us -> 60 us
  starting transfers between devices: 8.7 us -> 63.7 us
  other arithmetic: 58.4 us -> 8.46 us
  blocking collectives: 23.5 us -> 0 us
    all_gather x2 -> x0, waiting for transfers between devices: 410 us -> none  [the longest x1 269 us: per_device(): lax.all_gather(hidden_one, 'col', axis=0, tiled=True)]
    dot_general x56 -> x0, matrix products: 276 us -> none  [the longest x20 67.9 us: one_slab(): jnp.einsum('cbi,br->cri', product * alive_here[None, :, None], onehot, pr...]
    unnamed x7 -> x1, waiting for transfers between devices: 250 us -> 0.02 us
    psum x2 -> x1, waiting for transfers between devices: 215 us -> 86.6 us  [per_device(): g = lax.psum(g, 'graph')]
    reduce_scatter x1 -> x0, waiting for transfers between devices: 94.1 us -> none  [per_device(): lax.psum_scatter(back_project(weight_second[0], grad_pre_two), 'col', sca...]
    pallas_call x0 -> x3, Pallas kernels: none -> 60 us  [the longest x1 25.5 us: call_kc(): pl.pallas_call(functools.partial(kc, CLS=CLS), out_shape=sds((rows, 128),...]
    gather x22 -> x0, local copies, waits for them, and re-layouts: 51.9 us -> none  [the longest x12 28.1 us: one_slab(): shaped[:, cols_here, :]]
    all_to_all x2 -> x1, starting transfers between devices: 7.86 us -> 56.5 us  [per_device(): lax.all_to_all(own.reshape(CP, 2, G, P2 // 2 // G), 'graph', split_axis=2...]
  transfers between devices with their start and end apart: 8 -> 5, of which waited for: 6 -> 2; matrix products, arithmetic and copies ran while one was open for 13% -> 6% of each run, Pallas kernels for 0% -> 4%
where the time goes in v1:
time: 273 us; the launch traced here: 272 us
  waiting for transfers between devices  89.9 us (33%)
  starting transfers between devices  63.7 us (23%)
  Pallas kernels  60 us (22%)
  local copies, waits for them, and re-layouts  30.3 us (11%)
  between operations  19.1 us (7%)
  other arithmetic  8.46 us (3%)
    psum x1, waiting for transfers between devices, per_device(): g = lax.psum(g, 'graph')  86.6 us
    all_to_all x1, starting transfers between devices, per_device(): lax.all_to_all(own.reshape(CP, 2, G, P2 // 2 // G), 'graph', split_axis=2...  56.5 us
    pallas_call x1, Pallas kernels, call_kc(): pl.pallas_call(functools.partial(kc, CLS=CLS), out_shape=sds((rows, 128),...  25.5 us
    pallas_call x1, Pallas kernels, call_kb(): pl.pallas_call(kb, out_shape=(sds((NB, 128, H), BF), sds((NB, 128, H), BF...  24.1 us
    unnamed x53, local copies, waits for them, and re-layouts  13.9 us
    pallas_call x1, Pallas kernels, call_k0(): pl.pallas_call(functools.partial(k0, CH=CH, NBUF=NBUF), out_shape=(sds((B...  10.4 us
    ppermute x3, starting transfers between devices, per_device(): lax.ppermute(flat, 'col', [((j + k) % n_col, j) for j in range(n_col)])  7.01 us
  transfers between devices with their start and end apart: 5, of which 2 were waited for; matrix products, arithmetic and copies ran while one was open for 6% of the time, Pallas kernels for 4%

profile of v1, /device:TPU:0, one launch (start us, length us, event | category | flops | bytes accessed | tf_op | source)
XLA Modules:
  0.0 271.5 jit_solution(4912407056915012631)
XLA Ops:
  7.2 0.8 reshape.123
  8.0 0.9 copy.86
  8.8 0.2 reshape.122
  9.0 0.9 copy.84
  10.1 1.0 copy.85
  11.1 0.1 reshape.121
  11.3 3.1 %collective-permute-start.2 = (f32[51840]{0:T(1024)S(1)}, f32[51840]{0:T(1024)S(1)}, u32[]{:S(2)}, u32[]{:S(2)}) collective-permute-start(f32[51840]{0:T(1024)S(1)} %constant_dynamic-update-slice_fusion.16), channel_id=1, source_target_pairs={{3,0},{0,1},{1,2},{2,3},{7,4},{4,5},{5,6},{6,7},{11,8},{8,9},{9,10... | collective-permute-start | bytes 622088 | tf_op jit(solution)/shard_map/ppermute | solution.py:427
  14.4 2.6 collective-permute-start.1
  17.0 1.3 collective-permute-start
  18.3 0.7 constant_dynamic-slice_fusion
  19.1 0.5 fusion.19
  21.5 0.8 copy.91
  23.0 1.4 reshape_squeeze.8.pairs
  24.4 0.8 copy.82
  25.2 0.7 copy.83.blk_l
  26.0 6.0 %copy.119 = f32[1,100,8192]{2,1,0:T(8,128)} copy(f32[1,100,8192]{2,0,1:T(1,128)} %param.18) | data formatting | bytes 6553600
  32.0 0.6 slice_reduce_fusion.1
  32.6 1.9 pad_add_fusion.sizes
  34.5 10.4 %shard_map.281 = (bf16[512,128,128]{2,1,0:T(8,128)(2,1)}, s32[8,640]{1,0:T(8,128)}, bf16[64,128,128]{2,1,0:T(8,128)(2,1)}, bf16[64,128,128]{2,1,0:T(8,128)(2,1)}, bf16[64,128,128]{2,1,0:T(8,128)(2,1)}) custom-call(s32[3]{0:T(128)} %pad_add_fusion.sizes, s32[2,512]{1,0:T(2,128)} %copy.83.blk_l, s32[512,2]{1,0:T(8,128)} %bitcast.94, f32[100,8192]{1,0:T(8,128)} %bitcast.92, ...), custom_call_target="tpu_custom_call" | custom-call | tf_op jit(solution)/shard_map/pallas_call | solution.py:103
  45.7 0.1 concatenate.63
  45.9 0.1 copy.95
  46.2 0.6 slice_bitcast_fusion.9.ncol
  46.8 0.2 reshape.132
  47.0 0.1 copy.94
  47.1 0.1 reshape.129
  47.2 0.2 reshape.131
  47.4 0.1 copy.93
  47.6 0.1 reshape.128
  47.7 0.2 reshape.130
  47.9 0.1 copy.92
  48.1 0.8 copy.96.w1
  49.0 0.1 reshape.127
  49.1 0.1 fusion.11
  49.3 0.6 fusion.3
  50.2 0.7 concatenate.66.clone.npar
  50.8 0.6 pad_maximum_fusion.3.wh
  51.5 24.1 %shard_map.282 = (bf16[64,128,256]{2,1,0:T(8,128)(2,1)}, bf16[64,128,256]{2,1,0:T(8,128)(2,1)}, f32[64,128,256]{2,1,0:T(8,128)}, f32[64,128,256]{2,1,0:T(8,128)}...) custom-call(s32[3]{0:T(128)} %pad_add_fusion.sizes, ...), custom_call_target="tpu_custom_call" | custom-call | tf_op jit(solution)/shard_map/pallas_call | solution.py:226
  75.6 0.8 copy.99
  76.4 0.7 reshape.145
  77.1 56.5 %all-to-all-start = ((f32[8,1,768]{2,1,0:T(1,128)}), f32[8,1,768]{2,1,0:T(1,128)S(1)}, u32[]{:S(2)}, u32[]{:S(2)}) async-start(f32[8,1,768]{2,1,0:T(1,128)} %reshape.145), calls=%async_computation | async-start | bytes 49152 | tf_op jit(solution)/shard_map/all_to_all | solution.py:440
  133.6 0.2 all-reduce.6.cloned.1.call-start
  133.9 0.6 pad_maximum_fusion.4.w1m
  134.5 0.7 pad_maximum_fusion.2.w2m
  135.2 3.3 %all-to-all-done = f32[8,1,768]{2,1,0:T(1,128)S(1)} async-done(((f32[8,1,768]{2,1,0:T(1,128)}), f32[8,1,768]{2,1,0:T(1,128)S(1)}, u32[]{:S(2)}, u32[]{:S(2)}) %all-to-all-start) | async-done | bytes 24608 | tf_op jit(solution)/shard_map/all_to_all | solution.py:440
  138.4 0.5 broadcast.60
  139.0 0.7 reduce.5
  139.8 0.7 copy.102.recv
  140.5 25.5 %shard_map.283 = f32[456,128]{1,0:T(8,128)} custom-call(s32[3]{0:T(128)} %pad_add_fusion.sizes, s32[8,640]{1,0:T(8,128)} %get-tuple-element.27.lists, bf16[512,128,128]{2,1,0:T(8,128)(2,1)} %get-tuple-element.28.S_in, bf16[64,128,128]{2,1,0:T(8,128)(2,1)} %get-tuple-element.29.fth_in, bf16[64,128,128]{2,1,0:T(8,128)(2,1)} %get-tuple-element.30.ftl_in, ...), custom_call_target="tpu_custom_call" | custom-call | tf_op jit(solution)/shard_map/pallas_call | solution.py:399
  166.7 0.1 copy.106
  166.8 0.1 copy.107
  166.9 86.6 %all-reduce.6.cloned.1.call-done = f32[456,128]{1,0:T(8,128)} async-done(((f32[456,128]{1,0:T(8,128)}), f32[456,128]{1,0:T(8,128)}) %all-reduce.6.cloned.1.call-update) | async-done | bytes 233488 | tf_op jit(solution)/shard_map/psum | solution.py:442
  253.5 0.7 slice_reduce_fusion
  254.2 0.1 stack_reshape_squeeze.3
  254.3 0.8 slice_bitcast_fusion.6
  255.2 0.9 slice.212
  256.2 0.9 slice_bitcast_fusion.8
  257.1 0.7 copy.111
  257.8 0.7 copy.112
  258.5 0.7 copy.110
  259.3 0.8 slice.210
  260.1 0.7 multiply_add_fusion.4
  260.8 0.6 multiply_add_fusion.6
  261.4 0.9 multiply_add_fusion
  262.3 1.2 slice.209
  (95 shorter events, 1.7 us)
Async XLA Ops:
  11.3 33.6 %collective-permute-start.2 = (f32[51840]{0:T(1024)S(1)}, f32[51840]{0:T(1024)S(1)}, u32[]{:S(2)}, u32[]{:S(2)}) collective-permute-start(f32[51840]{0:T(1024)S(1)} %constant_dynamic-update-slice_fusion.16), channel_id=1, source_target_pairs={{3,0},{0,1},{1,2},{2,3},{7,4},{4,5},{5,6},{6,7},{11,8},{8,9},{9,10... | collective-permute-start | bytes 622088 | tf_op jit(solution)/shard_map/ppermute | solution.py:427
  14.4 30.8 %collective-permute-start.1 = (f32[51840]{0:T(1024)S(1)}, f32[51840]{0:T(1024)S(1)}, u32[]{:S(2)}, u32[]{:S(2)}) collective-permute-start(f32[51840]{0:T(1024)S(1)} %constant_dynamic-update-slice_fusion.16), channel_id=1, source_target_pairs={{2,0},{3,1},{0,2},{1,3},{6,4},{7,5},{4,6},{5,7},{10,8},{11,9},{8,1... | collective-permute-start | bytes 622088 | tf_op jit(solution)/shard_map/ppermute | solution.py:427
  17.0 28.4 %collective-permute-start = (f32[51840]{0:T(1024)S(1)}, f32[51840]{0:T(1024)S(1)}, u32[]{:S(2)}, u32[]{:S(2)}) collective-permute-start(f32[51840]{0:T(1024)S(1)} %constant_dynamic-update-slice_fusion.16), channel_id=1, source_target_pairs={{1,0},{2,1},{3,2},{0,3},{5,4},{6,5},{7,6},{4,7},{9,8},{10,9},{11,1... | collective-permute-start | bytes 622088 | tf_op jit(solution)/shard_map/ppermute | solution.py:427
  25.2 6.8 %copy-start = (s32[1,2,512]{1,2,0:T(8,128)}, s32[1,2,512]{1,2,0:T(8,128)S(1)}, u32[]{:S(2)}) copy-start(s32[1,2,512]{1,2,0:T(8,128)S(1)} %copy.82) | copy-start | bytes 12292
  26.0 6.0 %copy-start.14 = (s32[8,2]{0,1:T(2,128)S(1)}, s32[8,2]{0,1:T(2,128)}, u32[]{:S(2)}) copy-start(s32[8,2]{0,1:T(2,128)} %param.21) | copy-start | bytes 196
  34.5 11.0 %copy-start.2 = (f32[2,100,64]{1,2,0:T(8,128)S(1)}, f32[2,100,64]{1,2,0:T(8,128)}, u32[]{:S(2)}) copy-start(f32[2,100,64]{1,2,0:T(8,128)} %param.24) | copy-start | bytes 153604
  34.5 11.3 %copy-start.11 = (f32[2,2,64]{2,1,0:T(2,128)S(1)}, f32[2,2,64]{2,1,0:T(2,128)}, u32[]{:S(2)}) copy-start(f32[2,2,64]{2,1,0:T(2,128)} %param.27) | copy-start | bytes 3076
  50.2 1.3 copy-start.1
  77.1 61.3 %all-to-all-start = ((f32[8,1,768]{2,1,0:T(1,128)}), f32[8,1,768]{2,1,0:T(1,128)S(1)}, u32[]{:S(2)}, u32[]{:S(2)}) async-start(f32[8,1,768]{2,1,0:T(1,128)} %reshape.145), calls=%async_computation | async-start | bytes 49152 | tf_op jit(solution)/shard_map/all_to_all | solution.py:440
  133.6 119.9 %all-reduce.6.cloned.1.call-start = ((), (), s32[]{:S(2)}) async-start(), calls=%async_computation.1 | async-start | bytes 466944 | tf_op jit(solution)/shard_map/psum | solution.py:442
  135.2 5.3 %copy-start.4 = (bf16[384,256]{1,0:T(8,128)(2,1)}, bf16[384,256]{1,0:T(8,128)(2,1)S(1)}, u32[]{:S(2)}) copy-start(bf16[384,256]{1,0:T(8,128)(2,1)S(1)} %constant_dynamic-update-slice_fusion.7.wt) | copy-start | bytes 589828
  140.5 26.2 %copy-start.9 = (f32[2,64,47]{1,0,2:T(2,128)S(1)}, f32[2,64,47]{1,0,2:T(2,128)}, u32[]{:S(2)}) copy-start(f32[2,64,47]{1,0,2:T(2,128)} %param.30) | copy-start | bytes 72196
  140.5 26.3 %copy-start.10 = (f32[2,64,47]{1,0,2:T(2,128)S(1)}, f32[2,64,47]{1,0,2:T(2,128)}, u32[]{:S(2)}) copy-start(f32[2,64,47]{1,0,2:T(2,128)} %param.34) | copy-start | bytes 72196
  140.5 119.6 %copy-start.7 = (f32[2,100,64]{1,2,0:T(8,128)S(1)}, f32[2,100,64]{1,2,0:T(8,128)}, u32[]{:S(2)}) copy-start(f32[2,100,64]{1,2,0:T(8,128)} %param.32) | copy-start | bytes 153604
  140.5 119.6 %copy-start.8 = (f32[2,100,64]{1,2,0:T(8,128)S(1)}, f32[2,100,64]{1,2,0:T(8,128)}, u32[]{:S(2)}) copy-start(f32[2,100,64]{1,2,0:T(8,128)} %param.28) | copy-start | bytes 153604
  140.5 120.3 %copy-start.12 = (f32[2,2,64]{2,1,0:T(2,128)S(1)}, f32[2,2,64]{2,1,0:T(2,128)}, u32[]{:S(2)}) copy-start(f32[2,2,64]{2,1,0:T(2,128)} %param.35) | copy-start | bytes 3076
  140.5 120.3 %copy-start.13 = (f32[2,2,64]{2,1,0:T(2,128)S(1)}, f32[2,2,64]{2,1,0:T(2,128)}, u32[]{:S(2)}) copy-start(f32[2,2,64]{2,1,0:T(2,128)} %param.31) | copy-start | bytes 3076
  140.5 120.9 %copy-start.3 = (f32[2,256,64]{1,2,0:T(8,128)S(1)}, f32[2,256,64]{1,2,0:T(8,128)}, u32[]{:S(2)}) copy-start(f32[2,256,64]{1,2,0:T(8,128)} %param.25) | copy-start | bytes 393220
  140.5 120.9 %copy-start.5 = (f32[2,256,64]{1,2,0:T(8,128)S(1)}, f32[2,256,64]{1,2,0:T(8,128)}, u32[]{:S(2)}) copy-start(f32[2,256,64]{1,2,0:T(8,128)} %param.33) | copy-start | bytes 393220
  140.5 120.9 %copy-start.6 = (f32[2,256,64]{1,2,0:T(8,128)S(1)}, f32[2,256,64]{1,2,0:T(8,128)}, u32[]{:S(2)}) copy-start(f32[2,256,64]{1,2,0:T(8,128)} %param.29) | copy-start | bytes 393220
Sparse Core Ops, SparseCore 0:
  166.2 87.3 all-reduce.5

commit v2 on v1

--- a/solution.py
+++ b/solution.py
@@ -10,6 +10,12 @@
 def split(x):
     h=x.astype(BF); return h,(x-h.astype(F32)).astype(BF)
 GROUP=16
+
+def my_sizes(sizes):
+    me=lax.axis_index("graph")
+    total=sizes[0,0]
+    for g in range(1,sizes.shape[1]): total+=sizes[0,g]
+    return sizes[0,me]>>7, sizes[1,me], total
 
 def make_lists(blk_l, blk_c, lb, NB, L):
     BLK=blk_l.shape[1]
@@ -50,9 +56,9 @@
         return 0
     lax.fori_loop(0,pl.cdiv(n,GROUP),step,0)
 
-def k0(sizes, blk_l, blk_c, feat, vals, S_out, lists_out, fth_out, ftl_out, af_out,
+def k0(sizes, blk_l, feat, vals, S_out, lists_out, fth_out, ftl_out, af_out,
        S, lists_v, lists_s, ft_v, fth, ftl, acc, af, buf, sem_in, sem_f, sem_l, sem_o, sem_S, CH, NBUF):
-    nb=sizes[0]; lb=sizes[1]
+    nb,lb,_=my_sizes(sizes)
     NB=acc.shape[0]-1; BLK=vals.shape[0]; FIN=feat.shape[0]
     L=lists_v.shape[1]
     nch=pl.cdiv(lb,CH)
@@ -61,8 +67,10 @@
     for i in range(NBUF):
         @pl.when(i<nch)
         def _(): chunk_in(i,i).start()
-    cf=pltpu.make_async_copy(feat,ft_v,sem_f); cf.start()
-    lists_v[...]=make_lists(blk_l[...],blk_c[...],lb,NB,L)
+    cf=pltpu.make_async_copy(feat.at[:,0],ft_v,sem_f); cf.start()
+    ids=blk_l[...]
+    columns=jnp.concatenate([ids.astype(F32),jnp.zeros((6,BLK),F32)],axis=0).T.astype(I32)
+    lists_v[...]=make_lists(ids,columns,lb,NB,L)
     cl=pltpu.make_async_copy(lists_v,lists_s,sem_l.at[0]); cl.start()
     co=pltpu.make_async_copy(lists_v,lists_out,sem_l.at[1]); co.start()
     S[BLK]=jnp.zeros((128,128),BF)
@@ -96,18 +104,18 @@
     c1.wait();c2.wait();c3.wait();co.wait()
 
 def call_k0(sizes, blk, feat, vals, CH=16, NBUF=12):
-    FIN,N=feat.shape; NB=N//128; BLK=vals.shape[0]; L=pl.cdiv(BLK+NB,128)*128
+    FIN,_,N=feat.shape; NB=N//128; BLK=vals.shape[0]; L=pl.cdiv(BLK+NB,128)*128
     CH=min(CH,BLK)
     sds=jax.ShapeDtypeStruct
     ANY=pl.BlockSpec(memory_space=pl.ANY); VM=pl.BlockSpec(memory_space=pltpu.VMEM); SM=pl.BlockSpec(memory_space=pltpu.SMEM)
     return pl.pallas_call(functools.partial(k0,CH=CH,NBUF=NBUF),
         out_shape=(sds((BLK,128,128),BF),sds((8,L),I32),sds((NB,128,128),BF),sds((NB,128,128),BF),sds((NB,128,128),BF)),
-        in_specs=[SM,VM,VM,ANY,ANY],out_specs=[ANY]*5,
+        in_specs=[SM,VM,ANY,ANY],out_specs=[ANY]*5,
         scratch_shapes=[pltpu.VMEM((BLK+1,128,128),BF),pltpu.VMEM((8,L),I32),pltpu.SMEM((8,L),I32),pltpu.VMEM((FIN,N),F32),
             pltpu.VMEM((NB,128,128),BF),pltpu.VMEM((NB,128,128),BF),pltpu.VMEM((NB+1,128,128),F32),pltpu.VMEM((NB,128,128),BF),
             pltpu.VMEM((NBUF,CH,128,128),F32),
             pltpu.SemaphoreType.DMA((NBUF,)),pltpu.SemaphoreType.DMA(()),pltpu.SemaphoreType.DMA((2,)),pltpu.SemaphoreType.DMA((3,)),pltpu.SemaphoreType.DMA((pl.cdiv(BLK,CH),))],
-        compiler_params=pltpu.CompilerParams(vmem_limit_bytes=VLIM))(sizes,blk,blk.T,feat,vals)
+        compiler_params=pltpu.CompilerParams(vmem_limit_bytes=VLIM))(sizes,blk,feat,vals)
 G0=0.7978845608; G1=0.044715
 EPS=1e-5
 def for_blocks(nb,U,fn):
@@ -138,7 +146,7 @@
 def kb(sizes,lists,S_in,fth_in,ftl_in,af_in,w1,w2,wh,npar,pairs,
        h1h_out,h1l_out,ah_out,pre_out,st_out,h2t_out,lg_out,own_out,
        S,fth,ftl,af,h1h,h1l,acc,pre,zz,acc2,lg,h2t,sums,st,sem_i,sem_o):
-    nb=sizes[0]; NB=fth.shape[0]; BLK=S_in.shape[0]; KC=lg.shape[1]; MY=h2t.shape[1]//2
+    nb,_,_=my_sizes(sizes); NB=fth.shape[0]; BLK=S_in.shape[0]; KC=lg.shape[1]; MY=h2t.shape[1]//2
     count=(nb*128).astype(F32)
     cs=[pltpu.make_async_copy(a,b,sem_i.at[i]) for i,(a,b) in enumerate(((fth_in,fth),(ftl_in,ftl),(af_in,af),(S_in,S.at[pl.ds(0,BLK)])))]
     for c in cs: c.start()
@@ -148,7 +156,7 @@
     def p1(b0,U):
         h=blk(fth,b0,U)
         x=jnp.concatenate([h,blk(ftl,b0,U),h,blk(af,b0,U)],axis=1)
-        y=dot(x,w1[...])
+        y=dot_nt(x,w1[...])
         put_blk(pre,b0,U,y)
         sums[0]+=rows8(y)
     for_blocks(nb,4,p1)
@@ -168,7 +176,7 @@
     sums[...]=jnp.zeros_like(sums)
     def p2(b0,U):
         h=blk(h1h,b0,U); l=blk(h1l,b0,U); ah,al=split(blk(acc,b0,U))
-        y=dot(jnp.concatenate([h,l,h,ah,al,ah],axis=1),w2[...])
+        y=dot_nt(jnp.concatenate([h,l,h,ah,al,ah],axis=1),w2[...])
         put_blk(pre,b0,U,y)
         sums[0]+=rows8(y)
     for_blocks(nb,2,p2)
@@ -192,20 +200,27 @@
     ot=pltpu.make_async_copy(h2t,h2t_out,sem_o.at[4]); ot.start()
     agg_rows(lists,0,S,zz,acc2,True)
     own_out[...]=jnp.zeros_like(own_out)
+    slots=slot_nodes(pairs)
     def fin(b0,U):
         parts=[]; hot=[]
         for k in range(U):
             x=acc2[b0+k]; y=lg[b0+k]+x[:KC]+x[KC:]; lg[b0+k]=y
-            h,l=split(y); parts.append(jnp.concatenate([h,l],axis=0)); hot.append(one_hot(pairs,b0+k))
-        r=dot_nt(jnp.concatenate(parts,axis=1),jnp.concatenate(hot,axis=1))
-        own_out[...]+=r[:KC]+r[KC:]
+            h,l=split(y); parts.append(jnp.concatenate([h,l],axis=0)); hot.append(one_hot(slots,b0+k))
+        r=dot_nt(jnp.concatenate(hot,axis=1),jnp.concatenate(parts,axis=1))
+        own_out[:,:KC]+=r[:,:KC]+r[:,KC:]
     for_blocks(nb,4,fin)
     ol=pltpu.make_async_copy(lg,lg_out,sem_o.at[5]); ol.start()
     st_out[...]=st[...]
     for o in (*oh,oa,op,ot,ol): o.wait()
 
-def one_hot(pairs,b):
-    return jnp.where(pairs[...]==lax.broadcasted_iota(I32,(1,128),1)+b*128,1.0,0.0).astype(BF)
+def slot_nodes(pairs):
+    R,K=pairs.shape; G=R//2
+    x=jnp.concatenate([pairs[...].astype(F32),jnp.zeros((R,128-K),F32)],axis=1)
+    if R%128: x=jnp.concatenate([x,jnp.zeros((128-R%128,128),F32)],axis=0)
+    x=x.T[:K].astype(I32)
+    return jnp.concatenate([x[:,t*G+g:t*G+g+1] for g in range(G) for t in range(2)],axis=0)
+def one_hot(slots,b):
+    return jnp.where(slots==lax.broadcasted_iota(I32,(1,128),1)+b*128,1.0,0.0).astype(BF)
 
 def agg_rows(lists,which,S,v,acc,nt):
     n=lists[2+which,0]//2
@@ -219,39 +234,18 @@
     lax.fori_loop(0,pl.cdiv(n,GROUP),step,0)
 
 def call_kb(sizes,lists,S,fth,ftl,af,w1,w2,wh,npar,pairs,MY):
-    NB=fth.shape[0]; BLK=S.shape[0]; H=w2.shape[1]; KC=wh.shape[0]//4
+    NB=fth.shape[0]; BLK=S.shape[0]; H=w2.shape[0]; KC=wh.shape[0]//4
     sds=jax.ShapeDtypeStruct
     ANY=pl.BlockSpec(memory_space=pl.ANY); VM=pl.BlockSpec(memory_space=pltpu.VMEM); SM=pl.BlockSpec(memory_space=pltpu.SMEM)
     V=pltpu.VMEM
     return pl.pallas_call(kb,
-        out_shape=(sds((NB,128,H),BF),sds((NB,128,H),BF),sds((NB,128,H),F32),sds((NB,128,H),F32),sds((8,H),F32),sds((NB,2*MY,128),BF),sds((NB,KC,128),F32),sds((KC,pairs.shape[0]),F32)),
+        out_shape=(sds((NB,128,H),BF),sds((NB,128,H),BF),sds((NB,128,H),F32),sds((NB,128,H),F32),sds((8,H),F32),sds((NB,2*MY,128),BF),sds((NB,KC,128),F32),sds((pairs.size,128),F32)),
         in_specs=[SM,SM]+[ANY]*4+[VM]*5,out_specs=[ANY]*4+[VM]+[ANY]*2+[VM],
         scratch_shapes=[V((BLK+1,128,128),BF)]+[V((NB,128,128),BF)]*3+[V((NB,128,H),BF)]*2+[V((NB+1,128,H),F32),V((NB,128,H),F32),
             V((NB,2*KC,128),BF),V((NB+1,2*KC,128),F32),V((NB,KC,128),F32),V((NB,2*MY,128),BF),V((2,8,H),F32),V((8,H),F32),
             pltpu.SemaphoreType.DMA((4,)),pltpu.SemaphoreType.DMA((6,))],
         compiler_params=pltpu.CompilerParams(vmem_limit_bytes=VLIM))(sizes,lists,S,fth,ftl,af,w1,w2,wh,npar,pairs)
 
-def split_x(x):
-    h=lax.reduce_precision(x,8,7); return h.astype(BF),(x-h).astype(BF)
-def prep_weights(wf,ws,wh,npar,MY):
-    FIN=wf.shape[1]; C=wh.shape[2]; CP=-(-C//16)*16
-    def padk(w): return jnp.pad(w,((0,128-FIN),(0,0)))
-    f0h,f0l=split_x(padk(wf[0])); f1h=padk(wf[1]).astype(BF)
-    w1=jnp.concatenate([f0h,f0h,f0l,f1h],axis=0)
-    (ah,al),(bh,bl)=split_x(ws[0]),split_x(ws[1])
-    w2=jnp.concatenate([ah,ah,al,bh,bh,bl],axis=0)
-    hp=jnp.pad(wh,((0,0),(0,0),(0,CP-C))).transpose(0,2,1)
-    (ch,cl),(dh,dl)=split_x(hp[0]),split_x(hp[1])
-    whc=jnp.concatenate([ch,dh,cl,dl],axis=0)
-    n8=jnp.concatenate([npar.reshape(4,-1),jnp.zeros((4,npar.shape[2]),F32)],axis=0)
-    m0h=f0h[:,:MY].T; m0l=f0l[:,:MY].T
-    w1m=jnp.concatenate([m0h,m0h,m0l,f1h[:,:MY].T],axis=1)
-    z=jnp.zeros((128-2*CP,hp.shape[2]),BF)
-    th=jnp.concatenate([ch,dh,z],axis=0); tl=jnp.concatenate([cl,dl,z],axis=0)
-    wt=jnp.concatenate([th,th,tl],axis=0)
-    w2m=jnp.concatenate([ah[:MY],al[:MY],bh[:MY],bl[:MY]],axis=0)
-    nc=n8[:,:MY].T
-    return (w1,w2,whc,n8),(w1m,wt,w2m,n8,nc)
 def dgelu(u):
     q=u*u
     t=jnp.tanh(u*(G0+(G0*G1)*q))
@@ -260,8 +254,8 @@
 def kc(sizes,lists,S_in,fth_in,ftl_in,af_in,h1h_in,h1l_in,ah_in,pre_in,h2t_in,lg_in,st,own,recv,labels,pairs,w1m,wt,w2m,npar,ncol,
        g_out,
        S,fth,ftl,af,rh,rl,ra,pre,du,h2t,lg,gz,acc3,d0,t1,pre1,sums,cross,RH,RS,RL,R1,R2,colsum,sem_i,sem_r,CLS):
-    nb=sizes[0]; BLK=S_in.shape[0]; NB=fth.shape[0]; CP=lg.shape[1]; MY=t1.shape[1]; P2=own.shape[1]; H=pre.shape[2]; NS=rh.shape[0]
-    count=(nb*128).astype(F32); total=sizes[2].astype(F32)
+    nb,_,nodes=my_sizes(sizes); BLK=S_in.shape[0]; NB=fth.shape[0]; CP=lg.shape[1]; MY=t1.shape[1]; H=pre.shape[2]; NS=rh.shape[0]
+    count=(nb*128).astype(F32); total=nodes.astype(F32)
     ins=((lg_in,lg),(S_in,S.at[pl.ds(0,BLK)]),(pre_in,pre),(h2t_in,h2t),(fth_in,fth),(ftl_in,ftl),(af_in,af))
     cs=[pltpu.make_async_copy(a,b,sem_i.at[i]) for i,(a,b) in enumerate(ins)]
     for c in cs: c.start()
@@ -276,14 +270,16 @@
     S[BLK]=jnp.zeros((128,128),BF)
     for r in (sums,cross,RH,RS,RL,R1,R2,colsum): r[...]=jnp.zeros_like(r)
     acc3[NB]=jnp.zeros(acc3.shape[1:],F32)
-    half=P2//2
-    o=own[...]; r=recv[...]
-    D=o-jnp.concatenate([r[:,half:],r[:,:half]],axis=1)
+    half=pairs.shape[1]
+    G=pairs.shape[0]//2
+    r=recv[...]
+    D=own[...].reshape(G,2*half,128)-jnp.concatenate([r[:,half:],r[:,:half]],axis=1)
     pair_loss=0.5*jnp.sum(D[:,half:]*D[:,half:])
-    Dh,Dl=split(D/total); D2=jnp.concatenate([Dh,Dl],axis=0)
+    Dh,Dl=split((D.reshape(2*G*half,128).T)[:CP]/total); D2=jnp.concatenate([Dh,Dl],axis=0)
+    slots=slot_nodes(pairs)
     cs[0].wait()
     def soft(b0,U):
-        hot=jnp.concatenate([one_hot(pairs,b0+k) for k in range(U)],axis=1)
+        hot=jnp.concatenate([one_hot(slots,b0+k) for k in range(U)],axis=1)
         add=dot(D2,hot); add=add[:CP]+add[CP:]
         x=jnp.concatenate([lg[b0+k] for k in range(U)],axis=1)
         lab=jnp.concatenate([labels[b0+k] for k in range(U)],axis=1)
@@ -349,7 +345,7 @@
     agg_rows(lists,1,S,t1,d0,False)
     def pre_one(b0,U):
         h=blk(fth,b0,U)
-        y=dot_nt(w1m[...],jnp.concatenate([h,blk(ftl,b0,U),h,blk(af,b0,U)],axis=1))
+        y=dot_nt(w1m[0:MY,:],jnp.concatenate([h,blk(ftl,b0,U),h,blk(af,b0,U)],axis=1))
         for k in range(U):
             p=y[:,k*128:k*128+128]
             pre1[b0+k]=p; colsum[0]+=p
@@ -387,15 +383,15 @@
     gh=jnp.concatenate([RHv[:MY,:CP]+RHv[:MY,CP:2*CP]+RHv[MY:,:CP],gh[:,2*CP:3*CP],sg1,sb1,jnp.zeros((MY,128-2*CP-2),F32)],axis=1)
     g_out[q+2*MY:q+3*MY,:]=gh
     loss=jnp.sum(cross[...])+pair_loss
-    tail=jnp.concatenate([jnp.concatenate([sg2[:,:MY],sb2[:,:MY]]+([jnp.zeros((1,128-2*MY),F32)] if MY<64 else []),axis=1),jnp.broadcast_to(loss,(1,128)),jnp.zeros((6,128),F32)],axis=0)
-    g_out[q+3*MY:,:]=tail
-
-def call_kc(sizes,lists,S,fth,ftl,af,h1h,h1l,ah,pre,h2t,lg,st,own,recv,labels,pairs,w1m,wt,w2m,npar,ncol,CLS):
+    pad=[jnp.zeros((1,128-MY),F32)]
+    g_out[q+3*MY:,:]=jnp.zeros((g_out.shape[0]-q-3*MY,128),F32)
+    g_out[q+3*MY:q+3*MY+8,:]=jnp.concatenate([jnp.concatenate([sg2[:,:MY]]+pad,axis=1),jnp.concatenate([sb2[:,:MY]]+pad,axis=1),jnp.broadcast_to(loss,(1,128)),jnp.zeros((5,128),F32)],axis=0)
+
+def call_kc(sizes,lists,S,fth,ftl,af,h1h,h1l,ah,pre,h2t,lg,st,own,recv,labels,pairs,w1m,wt,w2m,npar,ncol,CLS,rows):
     NB=fth.shape[0]; BLK=S.shape[0]; H=pre.shape[2]; CP=lg.shape[1]; MY=ncol.shape[0]; NS=min(8,NB//2)
     sds=jax.ShapeDtypeStruct
     ANY=pl.BlockSpec(memory_space=pl.ANY); VM=pl.BlockSpec(memory_space=pltpu.VMEM); SM=pl.BlockSpec(memory_space=pltpu.SMEM)
     V=pltpu.VMEM
-    rows=2*H//128*MY+3*MY+8
     return pl.pallas_call(functools.partial(kc,CLS=CLS),out_shape=sds((rows,128),F32),
         in_specs=[SM,SM]+[ANY]*10+[VM]*10,out_specs=VM,
         scratch_shapes=[V((BLK+1,128,128),BF)]+[V((NB,128,128),BF)]*3+[V((NS,2,128,H),BF)]*2+[V((NS,2,128,H),F32),
@@ -405,7 +401,114 @@
             pltpu.SemaphoreType.DMA((7,)),pltpu.SemaphoreType.DMA((NS,3))],
         compiler_params=pltpu.CompilerParams(vmem_limit_bytes=VLIM))(sizes,lists,S,fth,ftl,af,h1h,h1l,ah,pre,h2t,lg,st,own,recv,labels,pairs,w1m,wt,w2m,npar,ncol)
 
-MOMENTUM=0.9; STEP_RATE=2.0; AVERAGE_KEEP=0.9
+def at(index): return {"graph": index}
+def meet(n):
+    me=lax.axis_index("graph")
+    barrier=pltpu.get_barrier_semaphore()
+    for k in range(1,n):
+        pl.semaphore_signal(barrier,inc=1,device_id=at(lax.rem(me+k,n)),device_id_type=pl.DeviceIdType.MESH)
+    pl.semaphore_wait(barrier,n-1)
+
+def kx(own,out,send,recv,n):
+    me=lax.axis_index("graph")
+    meet(n)
+    copies=[]
+    for k in range(1,n):
+        peer=lax.rem(me+k,n)
+        c=pltpu.make_async_remote_copy(src_ref=own.at[peer],dst_ref=out.at[me],send_sem=send.at[k-1],recv_sem=recv.at[k-1],
+            device_id=at(peer),device_id_type=pl.DeviceIdType.MESH)
+        c.start(); copies.append(c)
+    out[me]=own[me]
+    for c in copies: c.wait()
+
+def call_kx(own,n):
+    VM=pl.BlockSpec(memory_space=pltpu.VMEM)
+    return pl.pallas_call(functools.partial(kx,n=n),out_shape=jax.ShapeDtypeStruct(own.shape,own.dtype),in_specs=[VM],out_specs=VM,
+        scratch_shapes=[pltpu.SemaphoreType.DMA((n-1,)),pltpu.SemaphoreType.DMA((n-1,))],
+        compiler_params=pltpu.CompilerParams(collective_id=1,has_side_effects=True))(own)
+
+def kr(g,out,parts,send1,recv1,send2,recv2,n):
+    me=lax.axis_index("graph")
+    piece=g.shape[0]//n
+    def rows(i): return pl.ds(pl.multiple_of(i*piece,8),piece)
+    meet(n)
+    copies=[]
+    for k in range(1,n):
+        peer=lax.rem(me+k,n)
+        c=pltpu.make_async_remote_copy(src_ref=g.at[rows(peer)],dst_ref=parts.at[k-1],send_sem=send1.at[k-1],recv_sem=recv1.at[k-1],
+            device_id=at(peer),device_id_type=pl.DeviceIdType.MESH)
+        c.start(); copies.append(c)
+    total=g[rows(me),:]
+    for k,c in enumerate(copies):
+        c.wait_recv(); total+=parts[k]
+    out[rows(me),:]=total
+    back=[]
+    for k in range(1,n):
+        peer=lax.rem(me+k,n)
+        c=pltpu.make_async_remote_copy(src_ref=out.at[rows(me)],dst_ref=out.at[rows(me)],send_sem=send2.at[k-1],recv_sem=recv2.at[k-1],
+            device_id=at(peer),device_id_type=pl.DeviceIdType.MESH)
+        c.start(); back.append(c)
+    for c in copies: c.wait_send()
+    for c in back: c.wait()
+
+def call_kr(g,n):
+    VM=pl.BlockSpec(memory_space=pltpu.VMEM); D=pltpu.SemaphoreType.DMA((n-1,))
+    return pl.pallas_call(functools.partial(kr,n=n),out_shape=jax.ShapeDtypeStruct(g.shape,g.dtype),in_specs=[VM],out_specs=VM,
+        scratch_shapes=[pltpu.VMEM((n-1,g.shape[0]//n,128),F32),D,D,D,D],
+        compiler_params=pltpu.CompilerParams(collective_id=2,has_side_effects=True))(g)
+
+def kp(wf,ws,wh,npar,out):
+    _,MY,FIN=wf.shape; H=ws.shape[2]; CLS=wh.shape[0]; CP=-(-CLS//16)*16; nk=H//128
+    out[...]=jnp.zeros_like(out)
+    for h in range(2):
+        for k in range(nk):
+            r=(h*nk+k)*MY; out[r:r+MY,:]=ws[h,:,k*128:k*128+128]
+        r=2*nk*MY+h*MY; out[r:r+MY,:FIN]=wf[h]
+        r=2*nk*MY+2*MY+h*CP; out[r:r+CLS,:MY]=wh[:,h,:]
+        r=2*nk*MY+2*MY+2*CP+2*h; out[r:r+2,:MY]=npar[h]
+
+def call_kp(wf,ws,wh,npar,n_col):
+    _,MY,FIN=wf.shape; H=ws.shape[2]; CP=-(-wh.shape[0]//16)*16
+    rows=max(2*H//128*MY+2*MY+2*CP+8,2048//n_col)
+    VM=pl.BlockSpec(memory_space=pltpu.VMEM)
+    return pl.pallas_call(kp,out_shape=jax.ShapeDtypeStruct((rows,128),F32),in_specs=[VM]*4,out_specs=VM)(wf,ws,wh,npar)
+
+def kw(x,w1_out,w2_out,wh_out,npar_out,wt_out,w2m_out,ncol_out,n_col):
+    H=w1_out.shape[0]; MY=H//n_col; CP=wh_out.shape[0]//4; nk=H//128
+    col=lax.axis_index("col")
+    back=lax.rem(H-col*MY,H)
+    heads=([],[]); norms=[]; mine=([],[])
+    for k in range(n_col):
+        j=lax.rem(col+k,n_col); r=slice(k*MY,k*MY+MY)
+        q=2*nk*MY
+        h,l=split(x[j,q:q+MY,:])
+        w1_out[r,:]=jnp.concatenate([h,h,l,x[j,q+MY:q+2*MY,:].astype(BF)],axis=1)
+        two=[]
+        for half in range(2):
+            w=jnp.concatenate([x[j,(half*nk+i)*MY:(half*nk+i+1)*MY,:] for i in range(nk)],axis=1)
+            w=pltpu.roll(w,back,1)
+            mine[half].append(w[:,:128])
+            h,l=split(w); two+=[h,h,l]
+            heads[half].append(x[j,q+2*MY+half*CP:q+2*MY+(half+1)*CP,:MY])
+        w2_out[r,:]=jnp.concatenate(two,axis=1)
+        norms.append(x[j,q+2*MY+2*CP:q+2*MY+2*CP+8,:MY])
+    npar=jnp.concatenate(norms,axis=1)
+    npar_out[...]=npar
+    ncol_out[...]=npar[:,:128].T[:MY]
+    (ch,cl),(dh,dl)=[split(jnp.concatenate(p,axis=1)) for p in heads]
+    wh_out[...]=jnp.concatenate([ch,dh,cl,dl],axis=0)
+    z=jnp.zeros((128-2*CP,H),BF)
+    th=jnp.concatenate([ch,dh,z],axis=0); tl=jnp.concatenate([cl,dl,z],axis=0)
+    wt_out[...]=jnp.concatenate([th,th,tl],axis=0)
+    for half in range(2):
+        h,l=split(jnp.concatenate(mine[half],axis=0).T[:MY])
+        w2m_out[2*half*MY:(2*half+2)*MY,:]=jnp.concatenate([h,l],axis=0)
+
+def call_kw(x,n_col,H,CP):
+    MY=H//n_col; sds=jax.ShapeDtypeStruct; VM=pl.BlockSpec(memory_space=pltpu.VMEM)
+    return pl.pallas_call(functools.partial(kw,n_col=n_col),
+        out_shape=(sds((H,512),BF),sds((H,6*H),BF),sds((4*CP,H),BF),sds((8,H),F32),sds((384,H),BF),sds((4*MY,H),BF),sds((MY,8),F32)),
+        in_specs=[VM],out_specs=[VM]*7)(x)
 
 def renew(weight, momentum, average, gradient):
     momentum_new = MOMENTUM * momentum + gradient
@@ -413,45 +516,55 @@
     average_new = AVERAGE_KEEP * average + (1.0 - AVERAGE_KEEP) * weight_new
     return momentum_new, average_new, weight_new
 
-def turn(x, axis, by):
-    return lax.dynamic_slice_in_dim(jnp.concatenate([x,x],axis=axis),by,x.shape[axis],axis)
-
-def per_device(n_col, features, blocks, block_values, group_sizes, labels, pair_nodes, weight_first, weight_second, weight_head,
+def ku(g,*refs):
+    weights,momenta,averages,outs,loss=refs[:4],refs[4:8],refs[8:12],refs[12:24],refs[24]
+    _,MY,FIN=weights[0].shape; H=weights[1].shape[2]; CLS=weights[2].shape[0]; CP=-(-CLS//16)*16; nk=H//128
+    q=2*nk*MY
+    shift=lax.axis_index("col")*MY
+    def store(i,where,grad):
+        for o,v in zip(outs[3*i:3*i+3],renew(weights[i][where],momenta[i][where],averages[i][where],grad)): o[where]=v
+    head=g[q+2*MY:q+3*MY,:].T
+    for h in range(2):
+        x=jnp.concatenate([g[(h*nk+k)*MY:(h*nk+k+1)*MY,:] for k in range(nk)],axis=1)
+        store(1,(h,),pltpu.roll(x,shift,1))
+        store(0,(h,),g[q+h*MY:q+h*MY+MY,:FIN])
+        store(2,(slice(None),h,slice(None)),head[h*CP:h*CP+CLS,:MY])
+    store(3,(0,),head[2*CP:2*CP+2,:MY])
+    store(3,(1,),g[q+3*MY:q+3*MY+2,:MY])
+    loss[0,0]=g[q+3*MY+2,0]
+
+def call_ku(g,weights,momenta,averages):
+    VM=pl.BlockSpec(memory_space=pltpu.VMEM); SM=pl.BlockSpec(memory_space=pltpu.SMEM)
+    shapes=[jax.ShapeDtypeStruct(w.shape,F32) for w in weights for _ in range(3)]
+    return pl.pallas_call(ku,out_shape=(*shapes,jax.ShapeDtypeStruct((1,1),F32)),in_specs=[VM]*13,out_specs=[VM]*12+[SM])(g,*weights,*momenta,*averages)
+
+MOMENTUM=0.9; STEP_RATE=2.0; AVERAGE_KEEP=0.9
+
+def per_device(n_graph, n_col, features, blocks, block_values, group_sizes, labels, pair_nodes, weight_first, weight_second, weight_head,
                norm_params, momentum_first, momentum_second, momentum_head, momentum_norms, average_first, average_second,
                average_head, average_norms):
-    col=lax.axis_index("col")
-    MY=weight_first.shape[2]; H=MY*n_col; FIN=weight_first.shape[1]; CLS=weight_head.shape[2]; CP=-(-CLS//16)*16
-    G=group_sizes.shape[0]; N=features.shape[2]; NB=N//128
-    shards=(weight_first,weight_second,weight_head,norm_params)
-    flat=jnp.concatenate([x.reshape(-1) for x in shards])
-    parts=[flat]+[lax.ppermute(flat,"col",[((j+k)%n_col,j) for j in range(n_col)]) for k in range(1,n_col)]
-    own_sizes=lax.dynamic_slice_in_dim(group_sizes,lax.axis_index("graph"),1,0)[0]
-    total=jnp.sum(group_sizes[:,0])
-    sizes=jnp.stack([own_sizes[0]//128,own_sizes[1],total])
-    S,lists,fth,ftl,af=call_k0(sizes,blocks[0],features[0],block_values[0])
-    def whole(i,axis):
-        start=sum(x.size for x in shards[:i]); x=shards[i]
-        return jnp.concatenate([p[start:start+x.size].reshape(x.shape) for p in parts],axis=axis)
-    wf=whole(0,2); ws=turn(whole(1,2),1,col*MY); wh=whole(2,1); npar=whole(3,2)
-    wb,wc=prep_weights(wf,ws,wh,npar,MY)
-    pairs=pair_nodes[0].reshape(-1,1)
-    h1h,h1l,ah,pre,st,h2t,lg,own=call_kb(sizes,lists,S,fth,ftl,af,*wb,pairs,MY=MY)
-    P2=own.shape[1]
-    recv=lax.all_to_all(own.reshape(CP,2,G,P2//2//G),"graph",split_axis=2,concat_axis=2,tiled=True).reshape(CP,P2)
-    g=call_kc(sizes,lists,S,fth,ftl,af,h1h,h1l,ah,pre,h2t,lg,st,own,recv,labels[0].reshape(NB,1,128),pairs,*wc,CLS=CLS)
-    g=lax.psum(g,"graph")
-    nh=2*H//128; q=nh*MY
-    gs=g[:q].reshape(2,H//128,MY,128).transpose(0,1,3,2).reshape(2,H,MY)
-    gs=turn(gs,1,(n_col-col)%n_col*MY)
-    gf=g[q:q+2*MY].reshape(2,MY,128)[:,:,:FIN].transpose(0,2,1)
-    hd=g[q+2*MY:q+3*MY]; tail=g[q+3*MY:]
-    gh=jnp.stack([hd[:,:CLS],hd[:,CP:CP+CLS]])
-    gn=jnp.stack([hd[:,2*CP:2*CP+2].T,tail[0,:2*MY].reshape(2,MY)])
-    first=renew(weight_first,momentum_first,average_first,gf)
-    second=renew(weight_second,momentum_second,average_second,gs)
-    head=renew(weight_head,momentum_head,average_head,gh)
-    norms=renew(norm_params,momentum_norms,average_norms,gn)
-    return (tail[1,0],total.astype(F32),*first,*second,*head,*norms)
+    MY=weight_first.shape[2]; H=MY*n_col; CLS=weight_head.shape[2]; CP=-(-CLS//16)*16
+    G=group_sizes.shape[0]; N=features.shape[2]; NB=N//128; PEER=pair_nodes.shape[3]
+    def native(first,second,head,norms):
+        return first.transpose(0,2,1),second.transpose(0,2,1),head.transpose(2,0,1),norms
+    weights=native(weight_first,weight_second,weight_head,norm_params)
+    momenta=native(momentum_first,momentum_second,momentum_head,momentum_norms)
+    averages=native(average_first,average_second,average_head,average_norms)
+    packed=lax.all_gather(call_kp(*weights,n_col),"col")
+    sizes=group_sizes.T
+    S,lists,fth,ftl,af=call_k0(sizes,blocks[0],features.transpose(1,0,2),block_values[0])
+    w1,w2,wh,npar,wt,w2m,ncol=call_kw(packed,n_col,H,CP)
+    pairs=pair_nodes[0].reshape(2*G,PEER)
+    h1h,h1l,ah,pre,st,h2t,lg,own=call_kb(sizes,lists,S,fth,ftl,af,w1,w2,wh,npar,pairs,MY=MY)
+    recv=call_kx(own.reshape(G,2*PEER,128),n_graph)
+    unit=8*n_graph; rows=-(-(2*H//128*MY+3*MY+8)//unit)*unit
+    g=call_kc(sizes,lists,S,fth,ftl,af,h1h,h1l,ah,pre,h2t,lg,st,own,recv,labels[0].reshape(NB,1,128),pairs,w1,wt,w2m,npar,ncol,CLS=CLS,rows=rows)
+    g=call_kr(g,n_graph)
+    *new,loss=call_ku(g,weights,momenta,averages)
+    first=[x.transpose(0,2,1) for x in new[0:3]]
+    second=[x.transpose(0,2,1) for x in new[3:6]]
+    head=[x.transpose(1,2,0) for x in new[6:9]]
+    return (loss[0,0],jnp.sum(group_sizes[:,0]).astype(F32),*first,*second,*head,*new[9:12])
 
 def solution(mesh):
     P=jax.sharding.PartitionSpec
@@ -459,4 +572,4 @@
     weights=(unit,unit,head,unit)
     in_specs=(P("graph",None,None),P("graph",None,None),P("graph",None,None,None),P(),P("graph",None),P("graph",None,None,None))+weights*3
     out_specs=(P(),P())+(unit,)*6+(head,)*3+(unit,)*3
-    return jax.shard_map(functools.partial(per_device,mesh.shape["col"]),mesh=mesh,in_specs=in_specs,out_specs=out_specs,check_vma=False)
+    return jax.shard_map(functools.partial(per_device,mesh.shape["graph"],mesh.shape["col"]),mesh=mesh,in_specs=in_specs,out_specs=out_specs,check_vma=False)

time: 273 us -> 203 us (0.74)
  Pallas kernels: 60 us -> 184 us
  waiting for transfers between devices: 89.9 us -> 0.04 us
  starting transfers between devices: 63.7 us -> 0.04 us
  local copies, waits for them, and re-layouts: 30.3 us -> 0 us
  other arithmetic: 8.46 us -> 1.32 us
  between operations: 19.1 us -> 15.9 us
    psum x1 -> x0, waiting for transfers between devices: 86.6 us -> none  [per_device(): g = lax.psum(g, 'graph')]
    all_to_all x1 -> x0, starting transfers between devices: 56.5 us -> none  [per_device(): lax.all_to_all(own.reshape(CP, 2, G, P2 // 2 // G), 'graph', split_axis=2...]
    pallas_call x1, Pallas kernels: 24.1 us -> 63.8 us  [call_kb(): pl.pallas_call(kb, out_shape=(sds((NB, 128, H), BF), sds((NB, 128, H), BF...]
    pallas_call x1, Pallas kernels: 25.5 us -> 64 us  [call_kc(): pl.pallas_call(functools.partial(kc, CLS=CLS), out_shape=sds((rows, 128),...]
    pallas_call x0 -> x5, Pallas kernels: none -> 26.3 us  [the longest x1 13.2 us: call_kr(): pl.pallas_call(functools.partial(kr, n=n), out_shape=jax.ShapeDtypeStruct...]
    pallas_call x1, Pallas kernels: 10.4 us -> 29.7 us  [call_k0(): pl.pallas_call(functools.partial(k0, CH=CH, NBUF=NBUF), out_shape=(sds((B...]
    unnamed x53 -> x0, local copies, waits for them, and re-layouts: 13.9 us -> none
    ppermute x3 -> x0, starting transfers between devices: 7.01 us -> none  [per_device(): lax.ppermute(flat, 'col', [((j + k) % n_col, j) for j in range(n_col)])]
  transfers between devices with their start and end apart: 5 -> 1, of which waited for: 2 -> 0; matrix products, arithmetic and copies ran while one was open for 6% -> 1% of each run, Pallas kernels for 4% -> 15%
where the time goes in v2:
time: 203 us; the launch traced here: 201 us
  Pallas kernels  184 us (91%)
  between operations  15.9 us (8%)
    pallas_call x1, Pallas kernels, call_kc(): pl.pallas_call(functools.partial(kc, CLS=CLS), out_shape=sds((rows, 128),...  64 us
    pallas_call x1, Pallas kernels, call_kb(): pl.pallas_call(kb, out_shape=(sds((NB, 128, H), BF), sds((NB, 128, H), BF...  63.8 us
    pallas_call x1, Pallas kernels, call_k0(): pl.pallas_call(functools.partial(k0, CH=CH, NBUF=NBUF), out_shape=(sds((B...  29.7 us
    pallas_call x1, Pallas kernels, call_kr(): pl.pallas_call(functools.partial(kr, n=n), out_shape=jax.ShapeDtypeStruct...  13.2 us
    pallas_call x1, Pallas kernels, call_kx(): pl.pallas_call(functools.partial(kx, n=n), out_shape=jax.ShapeDtypeStruct...  6.45 us
  transfers between devices with their start and end apart: 1, of which 0 were waited for; matrix products, arithmetic and copies ran while one was open for 1% of the time, Pallas kernels for 15%

profile of v2, /device:TPU:0, one launch (start us, length us, event | category | flops | bytes accessed | tf_op | source)
XLA Modules:
  0.0 201.1 jit_solution(16420224895000291865)
XLA Ops:
  7.2 0.0 all-gather.3.cloned.1.call-start
  7.2 1.7 shard_map.282
  8.9 0.0 all-gather.3.cloned.1.call-update
  8.9 1.3 slice_reduce_fusion
  10.9 29.7 %shard_map.281 = (bf16[512,128,128]{2,1,0:T(8,128)(2,1)}, s32[8,640]{1,0:T(8,128)}, bf16[64,128,128]{2,1,0:T(8,128)(2,1)}, bf16[64,128,128]{2,1,0:T(8,128)(2,1)}, bf16[64,128,128]{2,1,0:T(8,128)(2,1)}) custom-call(s32[2,8]{1,0:T(2,128)} %bitcast.46, s32[2,512]{1,0:T(2,128)} %bitcast.49, f32[100,1,8192]{2,1,0:T(1,128)} %bitcast.28, f32[512,128,128]{2,1,0:T(8,128)} %bitcast.27), custom_call_target="tpu_custom_call" | custom-call | tf_op jit(solution)/shard_map/pallas_call | solution.py:111
  40.6 0.0 all-gather.3.cloned.1.call-done
  40.7 2.5 %shard_map.283 = (bf16[256,512]{1,0:T(8,128)(2,1)}, bf16[256,1536]{1,0:T(8,128)(2,1)}, bf16[192,256]{1,0:T(8,128)(2,1)}, f32[8,256]{1,0:T(8,128)}, bf16[384,256]...) custom-call(f32[4,512,128]{2,1,0:T(8,128)} %bitcast.29), custom_call_target="tpu_custom_call" | custom-call | tf_op jit(solution)/shard_map/pallas_call | solution.py:509
  43.2 63.8 %shard_map.284 = (bf16[64,128,256]{2,1,0:T(8,128)(2,1)}, bf16[64,128,256]{2,1,0:T(8,128)(2,1)}, f32[64,128,256]{2,1,0:T(8,128)}, f32[64,128,256]{2,1,0:T(8,128)}...) custom-call(s32[2,8]{1,0:T(2,128)} %bitcast.47, ...), custom_call_target="tpu_custom_call" | custom-call | tf_op jit(solution)/shard_map/pallas_call | solution.py:241
  107.0 6.4 %shard_map.285.recv = f32[8,16,128]{2,1,0:T(8,128)} custom-call(f32[8,16,128]{2,1,0:T(8,128)} %bitcast.32), custom_call_target="tpu_custom_call" | custom-call | tf_op jit(solution)/shard_map/pallas_call | solution.py:426
  113.5 64.0 %shard_map.286.g = f32[512,128]{1,0:T(8,128)} custom-call(s32[2,8]{1,0:T(2,128)} %bitcast.48, s32[8,640]{1,0:T(8,128)} %get-tuple-element.47.lists, bf16[512,128,128]{2,1,0:T(8,128)(2,1)} %get-tuple-element.48.S_in, bf16[64,128,128]{2,1,0:T(8,128)(2,1)} %get-tuple-element.49.fth_in, bf16[64,128,128]{2,1,0:T(8,128)(2,1)} %get-tuple-element.50.ftl_in, ...), custom_call_target="tpu_custom_call" | custom-call | tf_op jit(solution)/shard_map/pallas_call | solution.py:395
  177.5 13.2 %shard_map.287.g = f32[512,128]{1,0:T(8,128)} custom-call(f32[512,128]{1,0:T(8,128)} %shard_map.286.g), custom_call_target="tpu_custom_call" | custom-call | tf_op jit(solution)/shard_map/pallas_call | solution.py:456
  190.7 2.4 %shard_map.288 = (f32[2,64,100]{2,1,0:T(8,128)}, f32[2,64,100]{2,1,0:T(8,128)}, f32[2,64,100]{2,1,0:T(8,128)}, f32[2,64,256]{2,1,0:T(8,128)}, f32[2,64,256]{2,1,...) custom-call(f32[512,128]{1,0:T(8,128)} %shard_map.287.g, ...), custom_call_target="tpu_custom_call" | custom-call | tf_op jit(solution)/shard_map/pallas_call | solution.py:539
Async XLA Ops:
  7.2 33.5 %all-gather.3.cloned.1.call-start = ((), (), s32[]{:S(2)}) async-start(), calls=%async_computation | async-start | bytes 1310720 | tf_op jit(solution)/shard_map/all_gather | solution.py:553
Sparse Core Ops, SparseCore 0:
  9.6 30.6 all-gather.2

commit v3 on v2

v3 whole, which is shorter than its diff:
```python
import functools
import jax, jax.numpy as jnp
from jax import lax
from jax.experimental import pallas as pl
from jax.experimental.pallas import tpu as pltpu
BF=jnp.bfloat16; F32=jnp.float32; I32=jnp.int32
VLIM=60<<20
def dot(a,b): return jnp.dot(a,b,preferred_element_type=F32)
def dot_nt(a,b): return lax.dot_general(a,b,(((1,),(1,)),((),())),preferred_element_type=F32)
def split(x):
    h=x.astype(BF); return h,(x-h.astype(F32)).astype(BF)
GROUP=32

def my_sizes(sizes):
    me=lax.axis_index("graph")
    total=sizes[0,0]
    for g in range(1,sizes.shape[1]): total+=sizes[0,g]
    return sizes[0,me]>>7, sizes[1,me], total

def make_lists(blk_l, blk_c, lb, NB, L):
    BLK=blk_l.shape[1]
    b_c=lax.broadcasted_iota(I32,(BLK,1),0); b_l=lax.broadcasted_iota(I32,(1,BLK),1)
    live=b_c<lb
    r_l=lax.broadcasted_iota(I32,(1,128),1)
    p_l=lax.broadcasted_iota(I32,(1,L),1)
    outs=[];counts=[]
    for k in range(2):
        kc=blk_c[:,k:k+1]; oc=blk_c[:,1-k:2-k]; kl=blk_l[k:k+1,:]
        before=jnp.where((kl==kc)&(b_l<b_c),1.0,0.0)
        rank=jnp.sum(before,axis=1,keepdims=True)
        cnt=jnp.sum(jnp.where((kc==r_l)&live,1.0,0.0),axis=0,keepdims=True)
        half=jnp.floor(cnt*0.5)
        pc=cnt+(cnt-2.0*half)
        start=jnp.sum(jnp.where(r_l<kc,pc,0.0),axis=1,keepdims=True)
        pos=jnp.where(live,(start+rank).astype(I32),-1)
        null=BLK+NB*(1<<20)
        enc=b_c+oc*(1<<12)+kc*(1<<20)-null
        lo=jnp.where(pos==p_l,(enc&0xfff).astype(F32),0.0); hi=jnp.where(pos==p_l,(enc>>12).astype(F32),0.0)
        lo=jnp.sum(lo,axis=0,keepdims=True).astype(I32); hi=jnp.sum(hi,axis=0,keepdims=True).astype(I32)
        outs.append(hi*4096+lo+null)
        counts.append(jnp.broadcast_to(jnp.sum(pc,axis=1,keepdims=True).astype(I32),(1,L)))
    return jnp.concatenate(outs+counts+[jnp.zeros((4,L),I32)],axis=0)

def pair_fields(lists, which, q):
    e0=lists[which,2*q]; e1=lists[which,2*q+1]
    return e0>>20, (e0>>12)&0xff, (e1>>12)&0xff, e0&0xfff, e1&0xfff

def agg_nodes(lists, which, S, v, acc, lanes=slice(None)):
    n=lists[2+which,0]//2
    def step(s,_):
        for u in range(GROUP):
            r,c0,c1,b0,b1=pair_fields(lists,which,s*GROUP+u)
            lhs=jnp.concatenate([S[b0],S[b1]],axis=1)
            rhs=jnp.concatenate([v[c0],v[c1]],axis=0)
            acc[r,:,lanes]+=dot(lhs,rhs)
        return 0
    lax.fori_loop(0,pl.cdiv(n,GROUP),step,0)

def agg_rows(lists, which, S, v, acc, rows=slice(None)):
    n=lists[2+which,0]//2
    def step(s,_):
        for u in range(GROUP):
            r,c0,c1,b0,b1=pair_fields(lists,which,s*GROUP+u)
            lhs=jnp.concatenate([v[c0],v[c1]],axis=1)
            acc[r,rows]+=dot(lhs,jnp.concatenate([S[b0],S[b1]],axis=0))
        return 0
    lax.fori_loop(0,pl.cdiv(n,GROUP),step,0)

def k0(sizes, blk_l, feat, vals, S_out, lists_out, fth_out, ftl_out, af_out,
       S, lists_v, lists_s, ft_v, fth, ftl, acc, af, buf, sem_in, sem_f, sem_l, sem_o, sem_S, CH, NBUF):
    nb,lb,_=my_sizes(sizes)
    NB=acc.shape[0]-1; BLK=vals.shape[0]; FIN=feat.shape[0]
    L=lists_v.shape[1]
    nch=pl.cdiv(lb,CH)
    def chunk_in(i,slot): return pltpu.make_async_copy(vals.at[pl.ds(i*CH,CH)],buf.at[slot],sem_in.at[slot])
    def chunk_out(i): return pltpu.make_async_copy(S.at[pl.ds(i*CH,CH)],S_out.at[pl.ds(i*CH,CH)],sem_S.at[i])
    for i in range(NBUF):
        @pl.when(i<nch)
        def _(): chunk_in(i,i).start()
    cf=pltpu.make_async_copy(feat.at[:,0],ft_v,sem_f); cf.start()
    ids=blk_l[...]
    columns=jnp.concatenate([ids.astype(F32),jnp.zeros((6,BLK),F32)],axis=0).T.astype(I32)
    lists_v[...]=make_lists(ids,columns,lb,NB,L)
    cl=pltpu.make_async_copy(lists_v,lists_s,sem_l.at[0]); cl.start()
    co=pltpu.make_async_copy(lists_v,lists_out,sem_l.at[1]); co.start()
    S[BLK]=jnp.zeros((128,128),BF)
    acc[...]=jnp.zeros(acc.shape,F32)
    cf.wait()
    per=CH*NB//BLK
    def conv(i,_):
        slot=lax.rem(i,NBUF)
        chunk_in(i,slot).wait()
        for k in range(CH):
            S[i*CH+k]=buf[slot,k].T.astype(BF)
        for k in range(per):
            b=i*per+k
            x=ft_v[:,pl.ds(pl.multiple_of(b*128,128),128)]
            x=jnp.concatenate([x,jnp.zeros((128-FIN,128),F32)],axis=0).T
            h,l=split(x); fth[b]=h; ftl[b]=l
        @pl.when(i+NBUF<nch)
        def _(): chunk_in(i+NBUF,slot).start()
        chunk_out(i).start()
        return 0
    lax.fori_loop(0,nch,conv,0)
    c1=pltpu.make_async_copy(fth,fth_out,sem_o.at[0]); c1.start()
    c2=pltpu.make_async_copy(ftl,ftl_out,sem_o.at[1]); c2.start()
    cl.wait()
    agg_nodes(lists_s,0,S,fth,acc)
    def fin(b,_):
        af[b]=acc[b].astype(BF); return 0
    lax.fori_loop(0,nb,fin,0)
    c3=pltpu.make_async_copy(af,af_out,sem_o.at[2]); c3.start()
    lax.fori_loop(0,nch,lambda i,_:(chunk_out(i).wait(),0)[1],0)
    c1.wait();c2.wait();c3.wait();co.wait()

def call_k0(sizes, blk, feat, vals, CH=16, NBUF=12):
    FIN,_,N=feat.shape; NB=N//128; BLK=vals.shape[0]; L=pl.cdiv(BLK+NB,128)*128
    CH=min(CH,BLK)
    sds=jax.ShapeDtypeStruct
    ANY=pl.BlockSpec(memory_space=pl.ANY); VM=pl.BlockSpec(memory_space=pltpu.VMEM); SM=pl.BlockSpec(memory_space=pltpu.SMEM)
    return pl.pallas_call(functools.partial(k0,CH=CH,NBUF=NBUF),
        out_shape=(sds((BLK,128,128),BF),sds((8,L),I32),sds((NB,128,128),BF),sds((NB,128,128),BF),sds((NB,128,128),BF)),
        in_specs=[SM,VM,ANY,ANY],out_specs=[ANY]*5,
        scratch_shapes=[pltpu.VMEM((BLK+1,128,128),BF),pltpu.VMEM((8,L),I32),pltpu.SMEM((8,L),I32),pltpu.VMEM((FIN,N),F32),
            pltpu.VMEM((NB,128,128),BF),pltpu.VMEM((NB,128,128),BF),pltpu.VMEM((NB+1,128,128),F32),pltpu.VMEM((NB,128,128),BF),
            pltpu.VMEM((NBUF,CH,128,128),F32),
            pltpu.SemaphoreType.DMA((NBUF,)),pltpu.SemaphoreType.DMA(()),pltpu.SemaphoreType.DMA((2,)),pltpu.SemaphoreType.DMA((3,)),pltpu.SemaphoreType.DMA((pl.cdiv(BLK,CH),))],
        compiler_params=pltpu.CompilerParams(vmem_limit_bytes=VLIM))(sizes,blk,feat,vals)
G0=0.7978845608; G1=0.044715
EPS=1e-5
HP=64
def for_blocks(nb,U,fn,start=0):
    full=nb//U
    def many(s,_): fn(s*U,U); return 0
    def one(b,_): fn(b,1); return 0
    lax.fori_loop(start,full,many,0)
    if U>1: lax.fori_loop(full*U,nb,one,0)
def rows8(x): return jnp.sum(x.reshape(x.shape[0]//8,8,x.shape[1]),axis=0)
def blk(ref,b0,U):
    x=ref[pl.ds(b0,U)]; return x.reshape(U*x.shape[1],x.shape[2])
def put_blk(ref,b0,U,x): ref[pl.ds(b0,U)]=x.reshape((U,)+ref.shape[1:])
def gelu_half(w):
    return w+w*jnp.tanh(w*(2.0*G0+(8.0*G0*G1)*(w*w)))
def dgelu_half(w):
    q=w*w
    t=jnp.tanh(w*(2.0*G0+(8.0*G0*G1)*q))
    return (1.0+t)*(0.5+(w*(G0+(12.0*G0*G1)*q))*(1.0-t))

def moments(sums,shift,count):
    d=jnp.sum(sums[0],axis=0,keepdims=True)/count
    v=jnp.sum(sums[1],axis=0,keepdims=True)/count-d*d
    return shift+d,lax.rsqrt(v+EPS)

def slot_nodes(pairs):
    R,K=pairs.shape; G=R//2
    x=jnp.concatenate([pairs[...].astype(F32),jnp.zeros((R,128-K),F32)],axis=1)
    if R%128: x=jnp.concatenate([x,jnp.zeros((128-R%128,128),F32)],axis=0)
    x=x.T[:K].astype(I32)
    return jnp.concatenate([x[:,t*G+g:t*G+g+1] for g in range(G) for t in range(2)],axis=0)
def one_hot(slots,b):
    return jnp.where(slots==lax.broadcasted_iota(I32,(1,128),1)+b*128,1.0,0.0).astype(BF)

def kb(sizes,lists,pairs,S_in,fth_in,ftl_in,af_in,w1,w2,wh,npar,
       h1h_out,h1l_out,pre_out,pre1_out,st_out,h2t_out,lg_out,own_out,
       S,fth,ftl,af,h1h,h1l,acc,pre,zz,lg,h2t,pre1,sums,st,sem_i,sem_o):
    nb,_,_=my_sizes(sizes); NB=fth.shape[0]; BLK=S_in.shape[0]; CP=lg.shape[1]; MY=pre1.shape[1]
    count=(nb*128).astype(F32)
    cs=[pltpu.make_async_copy(a,b,sem_i.at[i]) for i,(a,b) in enumerate(((fth_in,fth),(ftl_in,ftl),(af_in,af),(S_in,S.at[pl.ds(0,BLK)])))]
    for c in cs: c.start()
    S[BLK]=jnp.zeros((128,128),BF)
    st[...]=jnp.zeros_like(st)
    for c in cs[:3]: c.wait()
    def first(b0,U):
        h=blk(fth,b0,U)
        x=jnp.concatenate([h,blk(ftl,b0,U),h,blk(af,b0,U)],axis=1)
        return dot_nt(x,w1[...])
    def second(b0,U):
        h=blk(h1h,b0,U); l=blk(h1l,b0,U); ah,al=split(blk(acc,b0,U))
        return dot_nt(jnp.concatenate([h,l,h,ah,al,ah],axis=1),w2[...])
    def layer(fn,mine):
        shift=jnp.sum(fn(0,1),axis=0,keepdims=True)/128.0
        sums[...]=jnp.zeros_like(sums)
        def tile(b0,U):
            y=fn(b0,U)
            put_blk(pre,b0,U,y)
            if mine:
                for k in range(U): pre1[b0+k]=y[k*128:k*128+128,:MY].T
            d=y-shift
            sums[0]+=rows8(d); sums[1]+=rows8(d*d)
        for_blocks(nb,8,tile)
        return moments(sums,shift,count)
    mean,inv=layer(first,True)
    st[0:1,:]=mean; st[1:2,:]=inv
    a=npar[0:1,:]*inv; c=npar[1:2,:]-mean*a
    a=0.5*a; c=0.5*c
    def n1(b0,U):
        h,l=split(gelu_half(blk(pre,b0,U)*a+c))
        put_blk(h1h,b0,U,h); put_blk(h1l,b0,U,l)
        put_blk(acc,b0,U,jnp.zeros((U*128,acc.shape[2]),F32))
    for_blocks(nb,4,n1)
    acc[NB]=jnp.zeros(acc.shape[1:],F32)
    outs=[pltpu.make_async_copy(x,y,sem_o.at[i]) for i,(x,y) in enumerate(((h1h,h1h_out),(h1l,h1l_out),(pre1,pre1_out)))]
    for o in outs: o.start()
    cs[3].wait()
    agg_nodes(lists,0,S,h1h,acc)
    mean2,inv2=layer(second,False)
    st[2:3,:]=mean2; st[3:4,:]=inv2
    outs.append(pltpu.make_async_copy(pre,pre_out,sem_o.at[3])); outs[-1].start()
    a2=npar[2:3,:]*inv2; c2=npar[3:4,:]-mean2*a2
    a2=0.5*a2; c2=0.5*c2
    def n2(b0,U):
        h,l=split(gelu_half(blk(pre,b0,U)*a2+c2))
        r=dot_nt(h,wh[...])
        dz=r[:,:2*HP]+r[:,2*HP:]+dot_nt(l,wh[0:2*HP,:])
        zh,zl=split(dz)
        put_blk(zz,b0,U,jnp.concatenate([zh[:,HP:],zl[:,HP:]],axis=1))
        put_blk(acc,b0,U,jnp.concatenate([dz,jnp.zeros_like(dz)],axis=1))
        t=jnp.concatenate([h[:,:MY],l[:,:MY]],axis=1)
        for k in range(U): h2t[b0+k]=t[k*128:k*128+128].T
    for_blocks(nb,8,n2)
    outs.append(pltpu.make_async_copy(h2t,h2t_out,sem_o.at[4])); outs[-1].start()
    agg_nodes(lists,0,S,zz,acc,slice(2*HP,4*HP))
    def fin(b0,U):
        for k in range(U):
            x=acc[b0+k]; s=x[:,2*HP:]
            y=x[:,:2*HP]+s+pltpu.roll(s,HP,1)
            acc[b0+k,:,:2*HP]=y
            lg[b0+k]=y.T[:CP]
    for_blocks(nb,8,fin)
    outs.append(pltpu.make_async_copy(lg,lg_out,sem_o.at[5])); outs[-1].start()
    G=pairs.shape[0]//2; K=pairs.shape[1]
    lane=lax.broadcasted_iota(I32,(1,128),1); sub=lax.broadcasted_iota(I32,(8,1),0)
    def slot(g,_):
        for t in range(2):
            for k0 in range(0,K,8):
                o=jnp.zeros((8,128),F32)
                for k in range(8):
                    n=pairs[t*G+g,k0+k]
                    x=acc[n>>7,pl.ds(pl.multiple_of(((n>>3)&15)*8,8),8),:2*HP]
                    o=jnp.where(sub==k,jnp.sum(jnp.where(sub==(n&7),x,0.0),axis=0,keepdims=True),o)
                own_out[pl.ds(pl.multiple_of((g*2+t)*K+k0,8),8),:]=jnp.where(lane<CP,o,0.0)
        return 0
    lax.fori_loop(0,G,slot,0)
    st_out[...]=st[...]
    for o in outs: o.wait()

def call_kb(sizes,lists,S,fth,ftl,af,w1,w2,wh,npar,pairs,MY,CP):
    NB=fth.shape[0]; BLK=S.shape[0]; H=w2.shape[0]
    sds=jax.ShapeDtypeStruct
    ANY=pl.BlockSpec(memory_space=pl.ANY); VM=pl.BlockSpec(memory_space=pltpu.VMEM); SM=pl.BlockSpec(memory_space=pltpu.SMEM)
    V=pltpu.VMEM
    return pl.pallas_call(kb,
        out_shape=(sds((NB,128,H),BF),sds((NB,128,H),BF),sds((NB,128,H),F32),sds((NB,MY,128),F32),sds((8,H),F32),sds((NB,2*MY,128),BF),sds((NB,CP,128),F32),sds((pairs.size,128),F32)),
        in_specs=[SM]*3+[ANY]*4+[VM]*4,out_specs=[ANY]*4+[VM]+[ANY]*2+[VM],
        scratch_shapes=[V((BLK+1,128,128),BF)]+[V((NB,128,128),BF)]*3+[V((NB,128,H),BF)]*2+[V((NB+1,128,H),F32),V((NB,128,H),F32),
            V((NB,128,2*HP),BF),V((NB,CP,128),F32),V((NB,2*MY,128),BF),V((NB,MY,128),F32),V((2,8,H),F32),V((8,H),F32),
            pltpu.SemaphoreType.DMA((4,)),pltpu.SemaphoreType.DMA((6,))],
        compiler_params=pltpu.CompilerParams(vmem_limit_bytes=VLIM))(sizes,lists,pairs,S,fth,ftl,af,w1,w2,wh,npar)


def kc(sizes,lists,S_in,fth_in,ftl_in,af_in,h1h_in,h1l_in,pre_in,pre1_in,h2t_in,lg_in,st,own,recv,labels,pairs,wt,w2m,npar,ncol,
       g_out,
       S,rfh,rfl,raf,rh,rl,pre,du,h2t,lg,gz,acc,v4,pre1,sums,cross,RH,RS,RL,R1,R2,colsum,sem_i,sem_r,CLS):
    nb,_,nodes=my_sizes(sizes); BLK=S_in.shape[0]; NB=pre.shape[0]; CP=lg.shape[1]; MY=ncol.shape[0]; H=pre.shape[2]; NS=rh.shape[0]; U8=rh.shape[1]
    count=(nb*128).astype(F32); total=nodes.astype(F32)
    ins=((lg_in,lg),(S_in,S.at[pl.ds(0,BLK)]),(pre_in,pre),(h2t_in,h2t),(pre1_in,pre1))
    cs=[pltpu.make_async_copy(a,b,sem_i.at[i]) for i,(a,b) in enumerate(ins)]
    for c in cs[:2]: c.start()
    nch=pl.cdiv(nb,U8)
    def ring(i):
        s=lax.rem(i,NS)
        return [pltpu.make_async_copy(a.at[pl.ds(i*U8,U8)],b.at[s],sem_r.at[s,k]) for k,(a,b) in enumerate(((h1h_in,rh),(h1l_in,rl),(fth_in,rfh),(ftl_in,rfl),(af_in,raf)))]
    S[BLK]=jnp.zeros((128,128),BF)
    for r in (sums,cross,RH,RS,RL,R1,R2,colsum): r[...]=jnp.zeros_like(r)
    acc[NB]=jnp.zeros(acc.shape[1:],F32)
    half=pairs.shape[1]
    G=pairs.shape[0]//2
    r=recv[...]
    D=own[...].reshape(G,2*half,128)-jnp.concatenate([r[:,half:],r[:,:half]],axis=1)
    pair_loss=0.5*jnp.sum(D[:,half:]*D[:,half:])
    Dh,Dl=split((D.reshape(2*G*half,128).T)[:CP]/total); D2=jnp.concatenate([Dh,Dl],axis=0)
    slots=slot_nodes(pairs)
    cs[0].wait()
    def soft(b0,U):
        hot=jnp.concatenate([one_hot(slots,b0+k) for k in range(U)],axis=1)
        add=dot(D2,hot); add=add[:CP]+add[CP:]
        x=jnp.concatenate([lg[b0+k] for k in range(U)],axis=1)
        lab=jnp.concatenate([labels[b0+k] for k in range(U)],axis=1)
        row=lax.broadcasted_iota(I32,(CP,1),0)
        xm=jnp.where(row<CLS,x,-1e30)
        mx=jnp.max(xm,axis=0,keepdims=True)
        e=jnp.exp(xm-mx); s=jnp.sum(e,axis=0,keepdims=True)
        hit=jnp.where(row==lab,1.0,0.0)
        c=mx+jnp.log(s)-jnp.sum(hit*x,axis=0,keepdims=True)
        g=(e/s-hit)/total+add
        h,l=split(g)
        for k in range(U):
            w=slice(k*128,k*128+128)
            cross[...]+=c[:,w]
            gz[b0+k]=jnp.concatenate([h[:,w],l[:,w]],axis=0)
            acc[b0+k,:2*CP]=jnp.zeros((2*CP,128),F32)
    for_blocks(nb,4,soft)
    cs[1].wait()
    for c in cs[2:]: c.start()
    agg_rows(lists,1,S,gz,acc,slice(0,2*CP))
    for i in range(NS):
        @pl.when(i<nch)
        def _():
            for c in ring(i): c.start()
    for c in cs[2:]: c.wait()
    mean2=st[2:3,:]; inv2=st[3:4,:]
    a2=npar[2:3,:]*inv2; c2=npar[3:4,:]-mean2*a2
    ha2=0.5*a2; hc2=0.5*c2
    def back2(b0,U):
        th=[];tl=[];ads=[]
        z=jnp.zeros((128-2*CP,128),BF)
        for k in range(U):
            ad=acc[b0+k,:2*CP]; ah,al=split(ad[:CP]+ad[CP:]); gk=gz[b0+k]
            th.append(jnp.concatenate([gk[:CP],ah,z],axis=0).T); tl.append(jnp.concatenate([gk[CP:],al,z],axis=0).T)
            ads.append(ah)
        th=jnp.concatenate(th,axis=0); tl=jnp.concatenate(tl,axis=0)
        gh=dot(jnp.concatenate([th,tl,th],axis=1),wt[...])
        hh=jnp.concatenate([h2t[b0+k] for k in range(U)],axis=1)
        gg=jnp.concatenate([jnp.concatenate([gz[b0+k] for k in range(U)],axis=1),jnp.concatenate(ads,axis=1)],axis=0)
        RH[...]+=dot_nt(hh,gg)
        y=blk(pre,b0,U)
        d=gh*dgelu_half(y*ha2+hc2)
        put_blk(du,b0,U,d)
        sums[0]+=rows8(d); sums[1]+=rows8(d*(y-mean2))
    for_blocks(nb,8,back2)
    sb2=jnp.sum(sums[0],axis=0,keepdims=True); sg2=jnp.sum(sums[1],axis=0,keepdims=True)*inv2
    A2=-a2*inv2*sg2/count; C2=-a2*sb2/count-A2*mean2
    def proj(b0,U):
        h,l=split(blk(du,b0,U)*a2+blk(pre,b0,U)*A2+C2)
        r=dot_nt(w2m[...],h); rl2=dot_nt(w2m[0:MY,:],l)
        d=r[:MY]+r[MY:2*MY]+rl2; t=(r[2*MY:3*MY]+r[3*MY:]).astype(BF)
        gt=jnp.concatenate([h[:,:MY],l[:,:MY]],axis=1)
        for k in range(U):
            w=slice(k*128,k*128+128)
            acc[b0+k]=jnp.concatenate([d[:,w],jnp.zeros((2*MY,128),F32)],axis=0)
            v4[b0+k]=jnp.concatenate([t[:,w],gt[w].T],axis=0)
    for_blocks(nb,8,proj)
    acc[NB]=jnp.zeros(acc.shape[1:],F32)
    agg_rows(lists,1,S,v4,acc)
    lane=lambda x: jnp.sum(x,axis=1,keepdims=True)
    stc=st[:,:128].T[:MY]
    mean1=stc[:,0:1]; inv1=stc[:,1:2]
    a1=ncol[:,0:1]*inv1; c1=ncol[:,1:2]-mean1*a1
    ha1=0.5*a1; hc1=0.5*c1
    def back1(b0,U):
        for k in range(U):
            p=pre1[b0+k]
            d=acc[b0+k,:MY]*dgelu_half(p*ha1+hc1)
            acc[b0+k,:MY]=d
            colsum[0]+=d; colsum[1]+=d*(p-mean1)
    for_blocks(nb,4,back1)
    sb1=lane(colsum[0]); sg1=lane(colsum[1])*inv1
    A1=-a1*inv1*sg1/count; C1=-a1*sb1/count-A1*mean1
    def last(i,_):
        s=lax.rem(i,NS)
        for c in ring(i): c.wait()
        def part(b0,off,U):
            f=lambda ref: ref[s,pl.ds(off,U)].reshape(U*128,ref.shape[3])
            x=[acc[b0+k] for k in range(U)]
            gh,gl=split(jnp.concatenate([x[k][:MY]*a1+pre1[b0+k]*A1+C1 for k in range(U)],axis=1))
            R1[...]+=dot(jnp.concatenate([gh,gl],axis=0),f(rfh))
            R2[...]+=dot(gh,jnp.concatenate([f(rfl),f(raf)],axis=1))
            ah,al=split(jnp.concatenate([x[k][MY:2*MY]+x[k][2*MY:] for k in range(U)],axis=1))
            gt=jnp.concatenate([v4[b0+k,MY:] for k in range(U)],axis=1)
            RS[...]+=dot(jnp.concatenate([gt,ah,al],axis=0),f(rh))
            RL[...]+=dot(jnp.concatenate([gt[:MY],ah],axis=0),f(rl))
        @pl.when((i+1)*U8<=nb)
        def _(): part(i*U8,0,U8)
        @pl.when((i+1)*U8>nb)
        def _():
            lax.fori_loop(0,nb-i*U8,lambda k,_:(part(i*U8+k,k,1),0)[1],0)
        @pl.when(i+NS<nch)
        def _():
            for c in ring(i+NS): c.start()
        return 0
    lax.fori_loop(0,nch,last,0)
    RSv=RS[...]; RLv=RL[...]; nk=H//128
    for h in range(2):
        gs=RSv[2*h*MY:(2*h+1)*MY]+RSv[(2*h+1)*MY:(2*h+2)*MY]+RLv[h*MY:(h+1)*MY]
        for k in range(nk): g_out[(h*nk+k)*MY:(h*nk+k+1)*MY,:]=gs[:,k*128:k*128+128]
    R1v=R1[...]; R2v=R2[...]
    q=2*nk*MY
    g_out[q:q+MY,:]=R1v[:MY]+R1v[MY:]+R2v[:,:128]
    g_out[q+MY:q+2*MY,:]=R2v[:,128:]
    RHv=RH[...]; gh=RHv[:MY]+RHv[MY:]
    gh=jnp.concatenate([RHv[:MY,:CP]+RHv[:MY,CP:2*CP]+RHv[MY:,:CP],gh[:,2*CP:3*CP],sg1,sb1,jnp.zeros((MY,128-2*CP-2),F32)],axis=1)
    g_out[q+2*MY:q+3*MY,:]=gh
    loss=jnp.sum(cross[...])+pair_loss
    pad=[jnp.zeros((1,128-MY),F32)]
    g_out[q+3*MY:,:]=jnp.zeros((g_out.shape[0]-q-3*MY,128),F32)
    g_out[q+3*MY:q+3*MY+8,:]=jnp.concatenate([jnp.concatenate([sg2[:,:MY]]+pad,axis=1),jnp.concatenate([sb2[:,:MY]]+pad,axis=1),jnp.broadcast_to(loss,(1,128)),jnp.zeros((5,128),F32)],axis=0)

def call_kc(sizes,lists,S,fth,ftl,af,h1h,h1l,pre,pre1,h2t,lg,st,own,recv,labels,pairs,wt,w2m,npar,ncol,CLS,rows):
    NB=fth.shape[0]; BLK=S.shape[0]; H=pre.shape[2]; CP=lg.shape[1]; MY=ncol.shape[0]; NS=3; U8=8
    sds=jax.ShapeDtypeStruct
    ANY=pl.BlockSpec(memory_space=pl.ANY); VM=pl.BlockSpec(memory_space=pltpu.VMEM); SM=pl.BlockSpec(memory_space=pltpu.SMEM)
    V=pltpu.VMEM
    return pl.pallas_call(functools.partial(kc,CLS=CLS),out_shape=sds((rows,128),F32),
        in_specs=[SM,SM]+[ANY]*10+[VM]*9,out_specs=VM,
        scratch_shapes=[V((BLK+1,128,128),BF)]+[V((NS,U8,128,128),BF)]*3+[V((NS,U8,128,H),BF)]*2+[
            V((NB,128,H),F32),V((NB,128,H),F32),V((NB,2*MY,128),BF),V((NB,CP,128),F32),V((NB,2*CP,128),BF),V((NB+1,max(3*MY,2*CP),128),F32),
            V((NB,3*MY,128),BF),V((NB,MY,128),F32),
            V((2,8,H),F32),V((1,128),F32),V((2*MY,3*CP),F32),V((4*MY,H),F32),V((2*MY,H),F32),V((2*MY,128),F32),V((MY,256),F32),V((2,MY,128),F32),
            pltpu.SemaphoreType.DMA((5,)),pltpu.SemaphoreType.DMA((NS,5))],
        compiler_params=pltpu.CompilerParams(vmem_limit_bytes=VLIM))(sizes,lists,S,fth,ftl,af,h1h,h1l,pre,pre1,h2t,lg,st,own,recv,labels,pairs,wt,w2m,npar,ncol)

def at(index): return {"graph": index}
def meet(n):
    me=lax.axis_index("graph")
    barrier=pltpu.get_barrier_semaphore()
    for k in range(1,n):
        pl.semaphore_signal(barrier,inc=1,device_id=at(lax.rem(me+k,n)),device_id_type=pl.DeviceIdType.MESH)
    pl.semaphore_wait(barrier,n-1)

def kx(own,out,send,recv,n):
    me=lax.axis_index("graph")
    meet(n)
    copies=[]
    for k in range(1,n):
        peer=lax.rem(me+k,n)
        c=pltpu.make_async_remote_copy(src_ref=own.at[peer],dst_ref=out.at[me],send_sem=send.at[k-1],recv_sem=recv.at[k-1],
            device_id=at(peer),device_id_type=pl.DeviceIdType.MESH)
        c.start(); copies.append(c)
    out[me]=own[me]
    for c in copies: c.wait()

def call_kx(own,n):
    VM=pl.BlockSpec(memory_space=pltpu.VMEM)
    return pl.pallas_call(functools.partial(kx,n=n),out_shape=jax.ShapeDtypeStruct(own.shape,own.dtype),in_specs=[VM],out_specs=VM,
        scratch_shapes=[pltpu.SemaphoreType.DMA((n-1,)),pltpu.SemaphoreType.DMA((n-1,))],
        compiler_params=pltpu.CompilerParams(collective_id=1,has_side_effects=True))(own)

def kr(g,out,parts,send1,recv1,send2,recv2,n):
    me=lax.axis_index("graph")
    piece=g.shape[0]//n
    def rows(i): return pl.ds(pl.multiple_of(i*piece,8),piece)
    meet(n)
    copies=[]
    for k in range(1,n):
        peer=lax.rem(me+k,n)
        c=pltpu.make_async_remote_copy(src_ref=g.at[rows(peer)],dst_ref=parts.at[k-1],send_sem=send1.at[k-1],recv_sem=recv1.at[k-1],
            device_id=at(peer),device_id_type=pl.DeviceIdType.MESH)
        c.start(); copies.append(c)
    total=g[rows(me),:]
    for k,c in enumerate(copies):
        c.wait_recv(); total+=parts[k]
    out[rows(me),:]=total
    back=[]
    for k in range(1,n):
        peer=lax.rem(me+k,n)
        c=pltpu.make_async_remote_copy(src_ref=out.at[rows(me)],dst_ref=out.at[rows(me)],send_sem=send2.at[k-1],recv_sem=recv2.at[k-1],
            device_id=at(peer),device_id_type=pl.DeviceIdType.MESH)
        c.start(); back.append(c)
    for c in copies: c.wait_send()
    for c in back: c.wait()

def call_kr(g,n):
    VM=pl.BlockSpec(memory_space=pltpu.VMEM); D=pltpu.SemaphoreType.DMA((n-1,))
    return pl.pallas_call(functools.partial(kr,n=n),out_shape=jax.ShapeDtypeStruct(g.shape,g.dtype),in_specs=[VM],out_specs=VM,
        scratch_shapes=[pltpu.VMEM((n-1,g.shape[0]//n,128),F32),D,D,D,D],
        compiler_params=pltpu.CompilerParams(collective_id=2,has_side_effects=True))(g)

def kp(wf,ws,wh,npar,out,half):
    _,MY,FIN=wf.shape; H=ws.shape[2]; CLS=wh.shape[0]; CP=-(-CLS//16)*16; nk=H//128
    out[...]=jnp.zeros_like(out)
    for h in range(2):
        for k in range(nk):
            r=(h*nk+k)*MY; out[r:r+MY,:]=ws[h,:,k*128:k*128+128]
        r=2*nk*MY+h*MY; out[r:r+MY,:FIN]=wf[h]
        r=2*nk*MY+2*MY+h*CP; out[r:r+CLS,:MY]=wh[:,h,:]
        r=2*nk*MY+2*MY+2*CP+2*h; out[r:r+2,:MY]=npar[h]
    core=lax.rem(lax.axis_index("graph"),2); n=half.shape[0]
    half[...]=out[pl.ds(pl.multiple_of(core*n,8),n),:]

def call_kp(wf,ws,wh,npar):
    _,MY,FIN=wf.shape; H=ws.shape[2]; CP=-(-wh.shape[0]//16)*16
    rows=-(-(2*H//128*MY+2*MY+2*CP+8)//16)*16
    VM=pl.BlockSpec(memory_space=pltpu.VMEM)
    return pl.pallas_call(kp,out_shape=(jax.ShapeDtypeStruct((rows,128),F32),jax.ShapeDtypeStruct((rows//2,128),F32)),in_specs=[VM]*4,out_specs=[VM]*2)(wf,ws,wh,npar)

def kw(own,*refs,n_col,CP):
    halves=refs[:n_col-1]; w1_out,w2_out,wh_out,npar_out,wt_out,w2m_out,ncol_out,x,send,recv=refs[n_col-1:]
    me=lax.axis_index("graph"); core=lax.rem(me,2); twin=me+1-2*core
    barrier=pltpu.get_barrier_semaphore()
    pl.semaphore_signal(barrier,inc=1,device_id=at(twin),device_id_type=pl.DeviceIdType.MESH)
    n=own.shape[0]//2; rows=pl.ds(pl.multiple_of(core*n,8),n)
    pl.semaphore_wait(barrier,1)
    copies=[]
    for k in range(1,n_col):
        c=pltpu.make_async_remote_copy(src_ref=halves[k-1],dst_ref=x.at[k,rows],send_sem=send.at[k-1],recv_sem=recv.at[k-1],
            device_id=at(twin),device_id_type=pl.DeviceIdType.MESH)
        c.start(); copies.append(c)
    x[0]=own[...]
    for k in range(1,n_col): x[k,rows,:]=halves[k-1][...]
    for c in copies: c.wait()
    H=w1_out.shape[0]; MY=H//n_col; nk=H//128
    col=lax.axis_index("col")
    back=lax.rem(H-col*MY,H)
    heads=([],[]); norms=[]; mine=([],[])
    for k in range(n_col):
        j=k; r=slice(k*MY,k*MY+MY)
        q=2*nk*MY
        h,l=split(x[j,q:q+MY,:])
        w1_out[r,:]=jnp.concatenate([h,h,l,x[j,q+MY:q+2*MY,:].astype(BF)],axis=1)
        two=[]
        for half in range(2):
            w=jnp.concatenate([x[j,(half*nk+i)*MY:(half*nk+i+1)*MY,:] for i in range(nk)],axis=1)
            w=pltpu.roll(w,back,1)
            mine[half].append(w[:,:128])
            h,l=split(w); two+=[h,h,l]
            heads[half].append(x[j,q+2*MY+half*CP:q+2*MY+(half+1)*CP,:MY])
        w2_out[r,:]=jnp.concatenate(two,axis=1)
        norms.append(x[j,q+2*MY+2*CP:q+2*MY+2*CP+8,:MY])
    npar=jnp.concatenate(norms,axis=1)
    npar_out[...]=npar
    ncol_out[...]=npar[:,:128].T[:MY]
    (ch,cl),(dh,dl)=[split(jnp.concatenate(p,axis=1)) for p in heads]
    z=jnp.zeros((HP-CP,H),BF)
    wh_out[...]=jnp.concatenate([ch,z,dh,z,cl,z,dl,z],axis=0)
    z=jnp.zeros((128-2*CP,H),BF)
    th=jnp.concatenate([ch,dh,z],axis=0); tl=jnp.concatenate([cl,dl,z],axis=0)
    wt_out[...]=jnp.concatenate([th,th,tl],axis=0)
    for half in range(2):
        h,l=split(jnp.concatenate(mine[half],axis=0).T[:MY])
        w2m_out[2*half*MY:(2*half+2)*MY,:]=jnp.concatenate([h,l],axis=0)

def call_kw(own,halves,H,CP):
    n_col=1+len(halves); MY=H//n_col; sds=jax.ShapeDtypeStruct; VM=pl.BlockSpec(memory_space=pltpu.VMEM)
    return pl.pallas_call(functools.partial(kw,n_col=n_col,CP=CP),
        out_shape=(sds((H,512),BF),sds((H,6*H),BF),sds((4*HP,H),BF),sds((8,H),F32),sds((384,H),BF),sds((4*MY,H),BF),sds((MY,8),F32)),
        in_specs=[VM]*n_col,out_specs=[VM]*7,
        scratch_shapes=[pltpu.VMEM((n_col,)+own.shape,F32),pltpu.SemaphoreType.DMA((n_col-1,)),pltpu.SemaphoreType.DMA((n_col-1,))],
        compiler_params=pltpu.CompilerParams(collective_id=3,has_side_effects=True))(own,*halves)

def renew(weight, momentum, average, gradient):
    momentum_new = MOMENTUM * momentum + gradient
    weight_new = weight - STEP_RATE * (gradient + MOMENTUM * momentum_new)
    average_new = AVERAGE_KEEP * average + (1.0 - AVERAGE_KEEP) * weight_new
    return momentum_new, average_new, weight_new

def ku(sizes,g,*refs):
    weights,momenta,averages,outs,loss,count=refs[:4],refs[4:8],refs[8:12],refs[12:24],refs[24],refs[25]
    _,MY,FIN=weights[0].shape; H=weights[1].shape[2]; CLS=weights[2].shape[0]; CP=-(-CLS//16)*16; nk=H//128
    q=2*nk*MY
    shift=lax.axis_index("col")*MY
    def store(i,where,grad):
        for o,v in zip(outs[3*i:3*i+3],renew(weights[i][where],momenta[i][where],averages[i][where],grad)): o[where]=v
    head=g[q+2*MY:q+3*MY,:].T
    for h in range(2):
        x=jnp.concatenate([g[(h*nk+k)*MY:(h*nk+k+1)*MY,:] for k in range(nk)],axis=1)
        store(1,(h,),pltpu.roll(x,shift,1))
        store(0,(h,),g[q+h*MY:q+h*MY+MY,:FIN])
        store(2,(slice(None),h,slice(None)),head[h*CP:h*CP+CLS,:MY])
    store(3,(0,),head[2*CP:2*CP+2,:MY])
    store(3,(1,),g[q+3*MY:q+3*MY+2,:MY])
    loss[0,0]=g[q+3*MY+2,0]
    count[0,0]=my_sizes(sizes)[2].astype(F32)

def call_ku(sizes,g,weights,momenta,averages):
    VM=pl.BlockSpec(memory_space=pltpu.VMEM); SM=pl.BlockSpec(memory_space=pltpu.SMEM)
    shapes=[jax.ShapeDtypeStruct(w.shape,F32) for w in weights for _ in range(3)]
    return pl.pallas_call(ku,out_shape=(*shapes,*[jax.ShapeDtypeStruct((1,1),F32)]*2),in_specs=[SM]+[VM]*13,out_specs=[VM]*12+[SM]*2)(sizes,g,*weights,*momenta,*averages)

MOMENTUM=0.9; STEP_RATE=2.0; AVERAGE_KEEP=0.9

def per_device(n_graph, n_col, features, blocks, block_values, group_sizes, labels, pair_nodes, weight_first, weight_second, weight_head,
               norm_params, momentum_first, momentum_second, momentum_head, momentum_norms, average_first, average_second,
               average_head, average_norms):
    MY=weight_first.shape[2]; H=MY*n_col; CLS=weight_head.shape[2]; CP=-(-CLS//16)*16
    G=group_sizes.shape[0]; N=features.shape[2]; NB=N//128; PEER=pair_nodes.shape[3]
    def native(first,second,head,norms):
        return first.transpose(0,2,1),second.transpose(0,2,1),head.transpose(2,0,1),norms
    weights=native(weight_first,weight_second,weight_head,norm_params)
    momenta=native(momentum_first,momentum_second,momentum_head,momentum_norms)
    averages=native(average_first,average_second,average_head,average_norms)
    packed,half=call_kp(*weights)
    halves=[lax.ppermute(half,"col",[((j+k)%n_col,j) for j in range(n_col)]) for k in range(1,n_col)]
    sizes=group_sizes.T
    S,lists,fth,ftl,af=call_k0(sizes,blocks[0],features.transpose(1,0,2),block_values[0])
    w1,w2,wh,npar,wt,w2m,ncol=call_kw(packed,halves,H,CP)
    pairs=pair_nodes[0].reshape(2*G,PEER)
    h1h,h1l,pre,pre1,st,h2t,lg,own=call_kb(sizes,lists,S,fth,ftl,af,w1,w2,wh,npar,pairs,MY=MY,CP=CP)
    recv=call_kx(own.reshape(G,2*PEER,128),n_graph)
    unit=8*n_graph; rows=-(-(2*H//128*MY+3*MY+8)//unit)*unit
    g=call_kc(sizes,lists,S,fth,ftl,af,h1h,h1l,pre,pre1,h2t,lg,st,own,recv,labels[0].reshape(NB,1,128),pairs,wt,w2m,npar,ncol,CLS=CLS,rows=rows)
    g=call_kr(g,n_graph)
    *new,loss,count=call_ku(sizes,g,weights,momenta,averages)
    first=[x.transpose(0,2,1) for x in new[0:3]]
    second=[x.transpose(0,2,1) for x in new[3:6]]
    head=[x.transpose(1,2,0) for x in new[6:9]]
    return (loss[0,0],count[0,0],*first,*second,*head,*new[9:12])

def solution(mesh):
    P=jax.sharding.PartitionSpec
    unit=P(None,None,"col"); head=P(None,"col",None)
    weights=(unit,unit,head,unit)
    in_specs=(P("graph",None,None),P("graph",None,None),P("graph",None,None,None),P(),P("graph",None),P("graph",None,None,None))+weights*3
    out_specs=(P(),P())+(unit,)*6+(head,)*3+(unit,)*3
    return jax.shard_map(functools.partial(per_device,mesh.shape["graph"],mesh.shape["col"]),mesh=mesh,in_specs=in_specs,out_specs=out_specs,check_vma=False)
```

time: 203 us -> 155 us (0.76)
  Pallas kernels: 184 us -> 146 us
  between operations: 15.9 us -> 0.9 us
  starting transfers between devices: 0.04 us -> 6.96 us
    pallas_call x1, Pallas kernels: 64 us -> 43.2 us  [call_kc(): pl.pallas_call(functools.partial(kc, CLS=CLS), out_shape=sds((rows, 128),...]
    pallas_call x1, Pallas kernels: 63.8 us -> 47.8 us  [call_kb(): pl.pallas_call(kb, out_shape=(sds((NB, 128, H), BF), sds((NB, 128, H), BF...]
    ppermute x0 -> x3, starting transfers between devices: none -> 6.96 us  [per_device(): lax.ppermute(half, 'col', [((j + k) % n_col, j) for j in range(n_col)])]
  transfers between devices with their start and end apart: 1 -> 3, of which waited for: 0 -> 0; matrix products, arithmetic and copies ran while one was open for 1% -> 0% of each run, Pallas kernels for 15% -> 18%
where the time goes in v3:
time: 155 us
  Pallas kernels  146 us (94%)
  starting transfers between devices  6.96 us (4%)
    pallas_call x1, Pallas kernels, call_kb(): pl.pallas_call(kb, out_shape=(sds((NB, 128, H), BF), sds((NB, 128, H), BF...  47.8 us
    pallas_call x1, Pallas kernels, call_kc(): pl.pallas_call(functools.partial(kc, CLS=CLS), out_shape=sds((rows, 128),...  43.2 us
    pallas_call x1, Pallas kernels, call_k0(): pl.pallas_call(functools.partial(k0, CH=CH, NBUF=NBUF), out_shape=(sds((B...  28.6 us
    pallas_call x1, Pallas kernels, call_kr(): pl.pallas_call(functools.partial(kr, n=n), out_shape=jax.ShapeDtypeStruct...  12.4 us
    ppermute x3, starting transfers between devices, per_device(): lax.ppermute(half, 'col', [((j + k) % n_col, j) for j in range(n_col)])  6.96 us
    pallas_call x1, Pallas kernels, call_kx(): pl.pallas_call(functools.partial(kx, n=n), out_shape=jax.ShapeDtypeStruct...  6.17 us
    pallas_call x1, Pallas kernels, call_kw(): pl.pallas_call(functools.partial(kw, n_col=n_col, CP=CP), out_shape=(sds(...  4.28 us
  transfers between devices with their start and end apart: 3, of which 0 were waited for; matrix products, arithmetic and copies ran while one was open for 0% of the time, Pallas kernels for 18%

profile of v3, /device:TPU:0, one launch (start us, length us, event | category | flops | bytes accessed | tf_op | source)
XLA Modules:
  0.0 155.0 jit_solution(8190626537191815656)
XLA Ops:
  0.6 1.7 %shard_map.282 = (f32[496,128]{1,0:T(8,128)}, f32[248,128]{1,0:T(8,128)}) custom-call(f32[2,64,100]{2,1,0:T(8,128)} %bitcast.32, f32[2,64,256]{2,1,0:T(8,128)} %bitcast.29, f32[47,2,64]{2,1,0:T(2,128)} %bitcast.34, f32[2,2,64]{2,1,0:T(2,128)} %refs_3_.1), custom_call_target="tpu_custom_call" | custom-call | tf_op jit(solution)/shard_map/pallas_call | solution.py:484
  2.3 3.0 %collective-permute-start.2 = (f32[248,128]{1,0:T(8,128)}, f32[248,128]{1,0:T(8,128)S(1)}, u32[]{:S(2)}, u32[]{:S(2)}) collective-permute-start(f32[248,128]{1,0:T(8,128)} %get-tuple-element.56), channel_id=1, source_target_pairs={{3,0},{0,1},{1,2},{2,3},{7,4},{4,5},{5,6},{6,7},{11,8},{8,9},{9,10... | collective-permute-start | bytes 380936 | tf_op jit(solution)/shard_map/ppermute | solution.py:582
  5.4 2.6 %collective-permute-start.1 = (f32[248,128]{1,0:T(8,128)}, f32[248,128]{1,0:T(8,128)S(1)}, u32[]{:S(2)}, u32[]{:S(2)}) collective-permute-start(f32[248,128]{1,0:T(8,128)} %get-tuple-element.56), channel_id=1, source_target_pairs={{2,0},{3,1},{0,2},{1,3},{6,4},{7,5},{4,6},{5,7},{10,8},{11,9},{8,1... | collective-permute-start | bytes 380936 | tf_op jit(solution)/shard_map/ppermute | solution.py:582
  8.0 1.3 collective-permute-start
  9.3 28.6 %shard_map.281 = (bf16[512,128,128]{2,1,0:T(8,128)(2,1)}, s32[8,640]{1,0:T(8,128)}, bf16[64,128,128]{2,1,0:T(8,128)(2,1)}, bf16[64,128,128]{2,1,0:T(8,128)(2,1)}, bf16[64,128,128]{2,1,0:T(8,128)(2,1)}) custom-call(s32[2,8]{1,0:T(2,128)} %bitcast.45, s32[2,512]{1,0:T(2,128)} %bitcast.49, f32[100,1,8192]{2,1,0:T(1,128)} %bitcast.28, f32[512,128,128]{2,1,0:T(8,128)} %bitcast.27), custom_call_target="tpu_custom_call" | custom-call | tf_op jit(solution)/shard_map/pallas_call | solution.py:121
  37.9 0.0 collective-permute-done.2.refs_2_
  37.9 0.0 copy-start
  37.9 0.0 collective-permute-done.1.refs_1_
  37.9 0.0 copy-start.1
  37.9 0.0 collective-permute-done.refs_0_
  37.9 0.0 copy-start.2
  37.9 0.6 copy-done
  38.5 0.0 copy-done.1
  38.6 0.0 copy-done.2
  38.6 4.3 %shard_map.283 = (bf16[256,512]{1,0:T(8,128)(2,1)}, bf16[256,1536]{1,0:T(8,128)(2,1)}, bf16[256,256]{1,0:T(8,128)(2,1)}, f32[8,256]{1,0:T(8,128)}, bf16[384,256]...) custom-call(f32[496,128]{1,0:T(8,128)} %get-tuple-element.55.own, f32[248,128]{1,0:T(8,128)} %copy-done.2, ...), custom_call_target="tpu_custom_call" | custom-call | tf_op jit(solution)/shard_map/pallas_call | solution.py:534
  42.9 47.8 %shard_map.284 = (bf16[64,128,256]{2,1,0:T(8,128)(2,1)}, bf16[64,128,256]{2,1,0:T(8,128)(2,1)}, f32[64,128,256]{2,1,0:T(8,128)}, f32[64,64,128]{2,1,0:T(8,128)},...) custom-call(s32[2,8]{1,0:T(2,128)} %bitcast.46, ...), custom_call_target="tpu_custom_call" | custom-call | tf_op jit(solution)/shard_map/pallas_call | solution.py:252
  90.7 6.2 %shard_map.285.recv = f32[8,16,128]{2,1,0:T(8,128)} custom-call(f32[8,16,128]{2,1,0:T(8,128)} %bitcast.31), custom_call_target="tpu_custom_call" | custom-call | tf_op jit(solution)/shard_map/pallas_call | solution.py:434
  96.9 43.2 %shard_map.286.g = f32[512,128]{1,0:T(8,128)} custom-call(s32[2,8]{1,0:T(2,128)} %bitcast.47, s32[8,640]{1,0:T(8,128)} %get-tuple-element.50.lists, bf16[512,128,128]{2,1,0:T(8,128)(2,1)} %get-tuple-element.51.S_in, bf16[64,128,128]{2,1,0:T(8,128)(2,1)} %get-tuple-element.52.fth_in, bf16[64,128,128]{2,1,0:T(8,128)(2,1)} %get-tuple-element.53.ftl_in, ...), custom_call_target="tpu_custom_call" | custom-call | tf_op jit(solution)/shard_map/pallas_call | solution.py:403
  140.0 12.4 %shard_map.287.g = f32[512,128]{1,0:T(8,128)} custom-call(f32[512,128]{1,0:T(8,128)} %shard_map.286.g), custom_call_target="tpu_custom_call" | custom-call | tf_op jit(solution)/shard_map/pallas_call | solution.py:464
  152.4 2.4 %shard_map.288 = (f32[2,64,100]{2,1,0:T(8,128)}, f32[2,64,100]{2,1,0:T(8,128)}, f32[2,64,100]{2,1,0:T(8,128)}, f32[2,64,256]{2,1,0:T(8,128)}, f32[2,64,256]{2,1,...) custom-call(s32[2,8]{1,0:T(2,128)} %bitcast.48, ...), custom_call_target="tpu_custom_call" | custom-call | tf_op jit(solution)/shard_map/pallas_call | solution.py:567
Async XLA Ops:
  2.3 35.5 %collective-permute-start.2 = (f32[248,128]{1,0:T(8,128)}, f32[248,128]{1,0:T(8,128)S(1)}, u32[]{:S(2)}, u32[]{:S(2)}) collective-permute-start(f32[248,128]{1,0:T(8,128)} %get-tuple-element.56), channel_id=1, source_target_pairs={{3,0},{0,1},{1,2},{2,3},{7,4},{4,5},{5,6},{6,7},{11,8},{8,9},{9,10... | collective-permute-start | bytes 380936 | tf_op jit(solution)/shard_map/ppermute | solution.py:582
  5.4 32.5 %collective-permute-start.1 = (f32[248,128]{1,0:T(8,128)}, f32[248,128]{1,0:T(8,128)S(1)}, u32[]{:S(2)}, u32[]{:S(2)}) collective-permute-start(f32[248,128]{1,0:T(8,128)} %get-tuple-element.56), channel_id=1, source_target_pairs={{2,0},{3,1},{0,2},{1,3},{6,4},{7,5},{4,6},{5,7},{10,8},{11,9},{8,1... | collective-permute-start | bytes 380936 | tf_op jit(solution)/shard_map/ppermute | solution.py:582
  8.0 30.0 %collective-permute-start = (f32[248,128]{1,0:T(8,128)}, f32[248,128]{1,0:T(8,128)S(1)}, u32[]{:S(2)}, u32[]{:S(2)}) collective-permute-start(f32[248,128]{1,0:T(8,128)} %get-tuple-element.56), channel_id=1, source_target_pairs={{1,0},{2,1},{3,2},{0,3},{5,4},{6,5},{7,6},{4,7},{9,8},{10,9},{11,1... | collective-permute-start | bytes 380936 | tf_op jit(solution)/shard_map/ppermute | solution.py:582
  37.9 0.7 copy-start
  37.9 0.7 copy-start.1
  37.9 0.7 copy-start.2

commit v4 on v3

--- a/solution.py
+++ b/solution.py
@@ -4,12 +4,14 @@
 from jax.experimental import pallas as pl
 from jax.experimental.pallas import tpu as pltpu
 BF=jnp.bfloat16; F32=jnp.float32; I32=jnp.int32
-VLIM=60<<20
+VLIM0=58<<20
+VLIM=31<<20
 def dot(a,b): return jnp.dot(a,b,preferred_element_type=F32)
 def dot_nt(a,b): return lax.dot_general(a,b,(((1,),(1,)),((),())),preferred_element_type=F32)
 def split(x):
     h=x.astype(BF); return h,(x-h.astype(F32)).astype(BF)
 GROUP=32
+GP=16
 
 def my_sizes(sizes):
     me=lax.axis_index("graph")
@@ -17,115 +19,138 @@
     for g in range(1,sizes.shape[1]): total+=sizes[0,g]
     return sizes[0,me]>>7, sizes[1,me], total
 
-def make_lists(blk_l, blk_c, lb, NB, L):
-    BLK=blk_l.shape[1]
+def sort_list(keys_l, keys_c, enc, lb, null, L):
+    BLK=keys_l.shape[1]
     b_c=lax.broadcasted_iota(I32,(BLK,1),0); b_l=lax.broadcasted_iota(I32,(1,BLK),1)
     live=b_c<lb
-    r_l=lax.broadcasted_iota(I32,(1,128),1)
-    p_l=lax.broadcasted_iota(I32,(1,L),1)
-    outs=[];counts=[]
-    for k in range(2):
-        kc=blk_c[:,k:k+1]; oc=blk_c[:,1-k:2-k]; kl=blk_l[k:k+1,:]
-        before=jnp.where((kl==kc)&(b_l<b_c),1.0,0.0)
-        rank=jnp.sum(before,axis=1,keepdims=True)
-        cnt=jnp.sum(jnp.where((kc==r_l)&live,1.0,0.0),axis=0,keepdims=True)
-        half=jnp.floor(cnt*0.5)
-        pc=cnt+(cnt-2.0*half)
-        start=jnp.sum(jnp.where(r_l<kc,pc,0.0),axis=1,keepdims=True)
-        pos=jnp.where(live,(start+rank).astype(I32),-1)
-        null=BLK+NB*(1<<20)
-        enc=b_c+oc*(1<<12)+kc*(1<<20)-null
-        lo=jnp.where(pos==p_l,(enc&0xfff).astype(F32),0.0); hi=jnp.where(pos==p_l,(enc>>12).astype(F32),0.0)
-        lo=jnp.sum(lo,axis=0,keepdims=True).astype(I32); hi=jnp.sum(hi,axis=0,keepdims=True).astype(I32)
-        outs.append(hi*4096+lo+null)
-        counts.append(jnp.broadcast_to(jnp.sum(pc,axis=1,keepdims=True).astype(I32),(1,L)))
-    return jnp.concatenate(outs+counts+[jnp.zeros((4,L),I32)],axis=0)
+    r_l=lax.broadcasted_iota(I32,(1,128),1); p_l=lax.broadcasted_iota(I32,(1,L),1)
+    rank=jnp.sum(jnp.where((keys_l==keys_c)&(b_l<b_c),1.0,0.0),axis=1,keepdims=True)
+    cnt=jnp.sum(jnp.where((keys_c==r_l)&live,1.0,0.0),axis=0,keepdims=True)
+    even=2.0*jnp.floor(0.5*cnt+0.5)
+    start=jnp.sum(jnp.where(r_l<keys_c,even,0.0),axis=1,keepdims=True)
+    pos=jnp.where(live,(start+rank).astype(I32),-1)
+    enc=enc-null; here=pos==p_l
+    lo=jnp.sum(jnp.where(here,(enc&0xfff).astype(F32),0.0),axis=0,keepdims=True).astype(I32)
+    hi=jnp.sum(jnp.where(here,(enc>>12).astype(F32),0.0),axis=0,keepdims=True).astype(I32)
+    return hi*4096+lo+null,pos,jnp.sum(even,axis=1,keepdims=True).astype(I32)
 
 def pair_fields(lists, which, q):
     e0=lists[which,2*q]; e1=lists[which,2*q+1]
     return e0>>20, (e0>>12)&0xff, (e1>>12)&0xff, e0&0xfff, e1&0xfff
 
-def agg_nodes(lists, which, S, v, acc, lanes=slice(None)):
-    n=lists[2+which,0]//2
+def agg_nodes(lists, S, v, acc, lanes=slice(None)):
+    n=lists[2,0]//2
     def step(s,_):
         for u in range(GROUP):
-            r,c0,c1,b0,b1=pair_fields(lists,which,s*GROUP+u)
-            lhs=jnp.concatenate([S[b0],S[b1]],axis=1)
+            q=s*GROUP+u
+            r,c0,c1,_,_=pair_fields(lists,0,q)
             rhs=jnp.concatenate([v[c0],v[c1]],axis=0)
-            acc[r,:,lanes]+=dot(lhs,rhs)
+            acc[r,:,lanes]+=dot(jnp.concatenate([S[2*q],S[2*q+1]],axis=1),rhs)
         return 0
     lax.fori_loop(0,pl.cdiv(n,GROUP),step,0)
 
-def agg_rows(lists, which, S, v, acc, rows=slice(None)):
-    n=lists[2+which,0]//2
+def load_S(lists, S_in, S, sems):
+    n=2*pl.cdiv(lists[2,0],4*GP)
+    def one(i): return pltpu.make_async_copy(S_in.at[pl.ds(i*2*GP,2*GP)],S.at[pl.ds(i*2*GP,2*GP)],sems.at[i])
+    def start(): lax.fori_loop(0,n,lambda i,_:(one(i).start(),0)[1],0)
+    def wait(): lax.fori_loop(0,n,lambda i,_:(one(i).wait(),0)[1],0)
+    return start,wait
+
+def in_vmem(*arrays): return [pltpu.with_memory_space_constraint(x,pltpu.VMEM) for x in arrays]
+
+def agg_rows(lists, S, v, acc, rows=slice(None)):
+    n=lists[3,0]//2
     def step(s,_):
         for u in range(GROUP):
-            r,c0,c1,b0,b1=pair_fields(lists,which,s*GROUP+u)
+            r,c0,c1,b0,b1=pair_fields(lists,1,s*GROUP+u)
             lhs=jnp.concatenate([v[c0],v[c1]],axis=1)
             acc[r,rows]+=dot(lhs,jnp.concatenate([S[b0],S[b1]],axis=0))
         return 0
     lax.fori_loop(0,pl.cdiv(n,GROUP),step,0)
 
 def k0(sizes, blk_l, feat, vals, S_out, lists_out, fth_out, ftl_out, af_out,
-       S, lists_v, lists_s, ft_v, fth, ftl, acc, af, buf, sem_in, sem_f, sem_l, sem_o, sem_S, CH, NBUF):
+       lists_v, lists_s, ft_v, fth, ftl, af, acc, buf, even, odd, ring, sem_in, sem_f, sem_l, sem_o, sem_S):
     nb,lb,_=my_sizes(sizes)
-    NB=acc.shape[0]-1; BLK=vals.shape[0]; FIN=feat.shape[0]
-    L=lists_v.shape[1]
-    nch=pl.cdiv(lb,CH)
-    def chunk_in(i,slot): return pltpu.make_async_copy(vals.at[pl.ds(i*CH,CH)],buf.at[slot],sem_in.at[slot])
-    def chunk_out(i): return pltpu.make_async_copy(S.at[pl.ds(i*CH,CH)],S_out.at[pl.ds(i*CH,CH)],sem_S.at[i])
-    for i in range(NBUF):
-        @pl.when(i<nch)
-        def _(): chunk_in(i,i).start()
+    NB=acc.shape[0]-1; BLK=vals.shape[0]; FIN=feat.shape[0]; NBUF=buf.shape[0]; NOUT=ring.shape[0]; SL=S_out.shape[0]
+    L=lists_v.shape[1]; W=2*GP
     cf=pltpu.make_async_copy(feat.at[:,0],ft_v,sem_f); cf.start()
     ids=blk_l[...]
     columns=jnp.concatenate([ids.astype(F32),jnp.zeros((6,BLK),F32)],axis=0).T.astype(I32)
-    lists_v[...]=make_lists(ids,columns,lb,NB,L)
+    rows=columns[:,0:1]; cols=columns[:,1:2]
+    order=lax.broadcasted_iota(I32,(BLK,1),0)
+    l0,pos,n0=sort_list(ids[0:1],rows,order+cols*(1<<12)+rows*(1<<20),lb,BLK+(NB<<20),L)
+    lists_v[0:1,:]=l0; lists_v[2:3,:]=jnp.broadcast_to(n0,(1,L))
     cl=pltpu.make_async_copy(lists_v,lists_s,sem_l.at[0]); cl.start()
+    acc[...]=jnp.zeros(acc.shape,F32)
+    cl.wait()
+    n=2*pl.cdiv(lists_s[2,0],4*GP)
+    def chunk_start(i):
+        slot=lax.rem(i,NBUF)
+        for k in range(W):
+            b=lists_s[0,i*W+k]&0xfff
+            pltpu.make_async_copy(vals.at[jnp.where(b<BLK,b,0)],buf.at[slot,k],sem_in.at[slot]).start()
+    def chunk_wait(i):
+        slot=lax.rem(i,NBUF)
+        pltpu.make_async_copy(vals.at[pl.ds(0,W)],buf.at[slot],sem_in.at[slot]).wait()
+    lax.fori_loop(0,jnp.minimum(n,NBUF),lambda i,_:(chunk_start(i),0)[1],0)
+    l1,_,n1=sort_list(ids[1:2],cols,pos+rows*(1<<12)+cols*(1<<20),lb,SL+(NB<<20),L)
+    lists_v[1:2,:]=l1; lists_v[3:4,:]=jnp.broadcast_to(n1,(1,L))
     co=pltpu.make_async_copy(lists_v,lists_out,sem_l.at[1]); co.start()
-    S[BLK]=jnp.zeros((128,128),BF)
-    acc[...]=jnp.zeros(acc.shape,F32)
     cf.wait()
-    per=CH*NB//BLK
-    def conv(i,_):
-        slot=lax.rem(i,NBUF)
-        chunk_in(i,slot).wait()
-        for k in range(CH):
-            S[i*CH+k]=buf[slot,k].T.astype(BF)
-        for k in range(per):
-            b=i*per+k
+    def tr(i,_):
+        for k in range(4):
+            b=i*4+k
             x=ft_v[:,pl.ds(pl.multiple_of(b*128,128),128)]
             x=jnp.concatenate([x,jnp.zeros((128-FIN,128),F32)],axis=0).T
             h,l=split(x); fth[b]=h; ftl[b]=l
-        @pl.when(i+NBUF<nch)
-        def _(): chunk_in(i+NBUF,slot).start()
-        chunk_out(i).start()
         return 0
-    lax.fori_loop(0,nch,conv,0)
+    lax.fori_loop(0,pl.cdiv(nb,4),tr,0)
     c1=pltpu.make_async_copy(fth,fth_out,sem_o.at[0]); c1.start()
     c2=pltpu.make_async_copy(ftl,ftl_out,sem_o.at[1]); c2.start()
-    cl.wait()
-    agg_nodes(lists_s,0,S,fth,acc)
+    def chunk_out(i): return pltpu.make_async_copy(ring.at[lax.rem(i,NOUT)],S_out.at[pl.ds(i*W,W)],sem_S.at[lax.rem(i,NOUT)])
+    def convert(i,stage):
+        slot=lax.rem(i,NBUF); o=lax.rem(i,NOUT)
+        chunk_wait(i)
+        for k in range(W):
+            x=jnp.where(lists_s[0,i*W+k]&0xfff<BLK,buf[slot,k],0.0).T.astype(BF)
+            stage[k]=x; ring[o,k]=x
+    def dots(i,stage):
+        for u in range(GP):
+            r,f0,f1,_,_=pair_fields(lists_s,0,i*GP+u)
+            acc[r]+=dot(jnp.concatenate([stage[2*u],stage[2*u+1]],axis=1),jnp.concatenate([fth[f0],fth[f1]],axis=0))
+    def refill(i):
+        chunk_out(i).start()
+        @pl.when(i+NBUF<n)
+        def _(): chunk_start(i+NBUF)
+        @pl.when(i+1>=NOUT)
+        def _(): chunk_out(i+1-NOUT).wait()
+    convert(0,even); refill(0)
+    def step(j,_):
+        convert(2*j+1,odd); dots(2*j,even); refill(2*j+1)
+        convert(2*j+2,even); dots(2*j+1,odd); refill(2*j+2)
+        return 0
+    lax.fori_loop(0,n//2-1,step,0)
+    convert(n-1,odd); chunk_out(n-1).start(); dots(n-2,even); dots(n-1,odd)
     def fin(b,_):
-        af[b]=acc[b].astype(BF); return 0
-    lax.fori_loop(0,nb,fin,0)
+        for k in range(4): af[b*4+k]=acc[b*4+k].astype(BF)
+        return 0
+    lax.fori_loop(0,pl.cdiv(nb,4),fin,0)
     c3=pltpu.make_async_copy(af,af_out,sem_o.at[2]); c3.start()
-    lax.fori_loop(0,nch,lambda i,_:(chunk_out(i).wait(),0)[1],0)
+    lax.fori_loop(jnp.maximum(n-NOUT,0),n,lambda i,_:(chunk_out(i).wait(),0)[1],0)
     c1.wait();c2.wait();c3.wait();co.wait()
 
-def call_k0(sizes, blk, feat, vals, CH=16, NBUF=12):
-    FIN,_,N=feat.shape; NB=N//128; BLK=vals.shape[0]; L=pl.cdiv(BLK+NB,128)*128
-    CH=min(CH,BLK)
+def call_k0(sizes, blk, feat, vals, NBUF=8, NOUT=4):
+    FIN,_,N=feat.shape; NB=N//128; BLK=vals.shape[0]; L=pl.cdiv(BLK+NB,128)*128; W=2*GP; SL=pl.cdiv(BLK+NB,2*GROUP)*2*GROUP
     sds=jax.ShapeDtypeStruct
-    ANY=pl.BlockSpec(memory_space=pl.ANY); VM=pl.BlockSpec(memory_space=pltpu.VMEM); SM=pl.BlockSpec(memory_space=pltpu.SMEM)
-    return pl.pallas_call(functools.partial(k0,CH=CH,NBUF=NBUF),
-        out_shape=(sds((BLK,128,128),BF),sds((8,L),I32),sds((NB,128,128),BF),sds((NB,128,128),BF),sds((NB,128,128),BF)),
+    ANY=pl.BlockSpec(memory_space=pltpu.HBM); VM=pl.BlockSpec(memory_space=pltpu.VMEM); SM=pl.BlockSpec(memory_space=pltpu.SMEM)
+    V=pltpu.VMEM; D=pltpu.SemaphoreType.DMA
+    return pl.pallas_call(k0,
+        out_shape=(pltpu.HBM((SL,128,128),BF),pltpu.HBM((8,L),I32),*[pltpu.HBM((NB,128,128),BF)]*3),
         in_specs=[SM,VM,ANY,ANY],out_specs=[ANY]*5,
-        scratch_shapes=[pltpu.VMEM((BLK+1,128,128),BF),pltpu.VMEM((8,L),I32),pltpu.SMEM((8,L),I32),pltpu.VMEM((FIN,N),F32),
-            pltpu.VMEM((NB,128,128),BF),pltpu.VMEM((NB,128,128),BF),pltpu.VMEM((NB+1,128,128),F32),pltpu.VMEM((NB,128,128),BF),
-            pltpu.VMEM((NBUF,CH,128,128),F32),
-            pltpu.SemaphoreType.DMA((NBUF,)),pltpu.SemaphoreType.DMA(()),pltpu.SemaphoreType.DMA((2,)),pltpu.SemaphoreType.DMA((3,)),pltpu.SemaphoreType.DMA((pl.cdiv(BLK,CH),))],
-        compiler_params=pltpu.CompilerParams(vmem_limit_bytes=VLIM))(sizes,blk,feat,vals)
+        scratch_shapes=[V((8,L),I32),pltpu.SMEM((8,L),I32),V((FIN,N),F32),*[V((NB,128,128),BF)]*3,V((NB+1,128,128),F32),
+            V((NBUF,W,128,128),F32),V((W,128,128),BF),V((W,128,128),BF),V((NOUT,W,128,128),BF),
+            D((NBUF,)),D(()),D((2,)),D((3,)),D((NOUT,))],
+        compiler_params=pltpu.CompilerParams(vmem_limit_bytes=VLIM0))(sizes,blk,feat,vals)
 G0=0.7978845608; G1=0.044715
 EPS=1e-5
 HP=64
@@ -161,15 +186,16 @@
     return jnp.where(slots==lax.broadcasted_iota(I32,(1,128),1)+b*128,1.0,0.0).astype(BF)
 
 def kb(sizes,lists,pairs,S_in,fth_in,ftl_in,af_in,w1,w2,wh,npar,
-       h1h_out,h1l_out,pre_out,pre1_out,st_out,h2t_out,lg_out,own_out,
-       S,fth,ftl,af,h1h,h1l,acc,pre,zz,lg,h2t,pre1,sums,st,sem_i,sem_o):
-    nb,_,_=my_sizes(sizes); NB=fth.shape[0]; BLK=S_in.shape[0]; CP=lg.shape[1]; MY=pre1.shape[1]
+       h1h_out,h1l_out,pre,pre1,st,h2t,lg,own_out,S,
+       fth,ftl,af,h1h,h1l,acc,zz,sums,sem_i,sem_o,sem_S):
+    nb,_,_=my_sizes(sizes); NB=fth.shape[0]; CP=lg.shape[1]; MY=pre1.shape[1]
     count=(nb*128).astype(F32)
-    cs=[pltpu.make_async_copy(a,b,sem_i.at[i]) for i,(a,b) in enumerate(((fth_in,fth),(ftl_in,ftl),(af_in,af),(S_in,S.at[pl.ds(0,BLK)])))]
+    cs=[pltpu.make_async_copy(a,b,sem_i.at[i]) for i,(a,b) in enumerate(((fth_in,fth),(ftl_in,ftl),(af_in,af)))]
     for c in cs: c.start()
-    S[BLK]=jnp.zeros((128,128),BF)
+    S_start,S_wait=load_S(lists,S_in,S,sem_S); S_start()
+    S[S_in.shape[0]]=jnp.zeros((128,128),BF)
     st[...]=jnp.zeros_like(st)
-    for c in cs[:3]: c.wait()
+    for c in cs: c.wait()
     def first(b0,U):
         h=blk(fth,b0,U)
         x=jnp.concatenate([h,blk(ftl,b0,U),h,blk(af,b0,U)],axis=1)
@@ -199,13 +225,12 @@
         put_blk(acc,b0,U,jnp.zeros((U*128,acc.shape[2]),F32))
     for_blocks(nb,4,n1)
     acc[NB]=jnp.zeros(acc.shape[1:],F32)
-    outs=[pltpu.make_async_copy(x,y,sem_o.at[i]) for i,(x,y) in enumerate(((h1h,h1h_out),(h1l,h1l_out),(pre1,pre1_out)))]
+    outs=[pltpu.make_async_copy(x,y,sem_o.at[i]) for i,(x,y) in enumerate(((h1h,h1h_out),(h1l,h1l_out)))]
     for o in outs: o.start()
-    cs[3].wait()
-    agg_nodes(lists,0,S,h1h,acc)
+    S_wait()
+    agg_nodes(lists,S,h1h,acc)
     mean2,inv2=layer(second,False)
     st[2:3,:]=mean2; st[3:4,:]=inv2
-    outs.append(pltpu.make_async_copy(pre,pre_out,sem_o.at[3])); outs[-1].start()
     a2=npar[2:3,:]*inv2; c2=npar[3:4,:]-mean2*a2
     a2=0.5*a2; c2=0.5*c2
     def n2(b0,U):
@@ -218,8 +243,7 @@
         t=jnp.concatenate([h[:,:MY],l[:,:MY]],axis=1)
         for k in range(U): h2t[b0+k]=t[k*128:k*128+128].T
     for_blocks(nb,8,n2)
-    outs.append(pltpu.make_async_copy(h2t,h2t_out,sem_o.at[4])); outs[-1].start()
-    agg_nodes(lists,0,S,zz,acc,slice(2*HP,4*HP))
+    agg_nodes(lists,S,zz,acc,slice(2*HP,4*HP))
     def fin(b0,U):
         for k in range(U):
             x=acc[b0+k]; s=x[:,2*HP:]
@@ -227,7 +251,6 @@
             acc[b0+k,:,:2*HP]=y
             lg[b0+k]=y.T[:CP]
     for_blocks(nb,8,fin)
-    outs.append(pltpu.make_async_copy(lg,lg_out,sem_o.at[5])); outs[-1].start()
     G=pairs.shape[0]//2; K=pairs.shape[1]
     lane=lax.broadcasted_iota(I32,(1,128),1); sub=lax.broadcasted_iota(I32,(8,1),0)
     def slot(g,_):
@@ -238,49 +261,45 @@
                     n=pairs[t*G+g,k0+k]
                     x=acc[n>>7,pl.ds(pl.multiple_of(((n>>3)&15)*8,8),8),:2*HP]
                     o=jnp.where(sub==k,jnp.sum(jnp.where(sub==(n&7),x,0.0),axis=0,keepdims=True),o)
-                own_out[pl.ds(pl.multiple_of((g*2+t)*K+k0,8),8),:]=jnp.where(lane<CP,o,0.0)
+                own_out[g,pl.ds(pl.multiple_of(t*K+k0,8),8),:]=jnp.where(lane<CP,o,0.0)
         return 0
     lax.fori_loop(0,G,slot,0)
-    st_out[...]=st[...]
     for o in outs: o.wait()
 
 def call_kb(sizes,lists,S,fth,ftl,af,w1,w2,wh,npar,pairs,MY,CP):
-    NB=fth.shape[0]; BLK=S.shape[0]; H=w2.shape[0]
+    NB=fth.shape[0]; H=w2.shape[0]; SL=S.shape[0]; G=pairs.shape[0]//2; K=pairs.shape[1]
     sds=jax.ShapeDtypeStruct
-    ANY=pl.BlockSpec(memory_space=pl.ANY); VM=pl.BlockSpec(memory_space=pltpu.VMEM); SM=pl.BlockSpec(memory_space=pltpu.SMEM)
+    ANY=pl.BlockSpec(memory_space=pltpu.HBM); VM=pl.BlockSpec(memory_space=pltpu.VMEM); SM=pl.BlockSpec(memory_space=pltpu.SMEM)
     V=pltpu.VMEM
     return pl.pallas_call(kb,
-        out_shape=(sds((NB,128,H),BF),sds((NB,128,H),BF),sds((NB,128,H),F32),sds((NB,MY,128),F32),sds((8,H),F32),sds((NB,2*MY,128),BF),sds((NB,CP,128),F32),sds((pairs.size,128),F32)),
-        in_specs=[SM]*3+[ANY]*4+[VM]*4,out_specs=[ANY]*4+[VM]+[ANY]*2+[VM],
-        scratch_shapes=[V((BLK+1,128,128),BF)]+[V((NB,128,128),BF)]*3+[V((NB,128,H),BF)]*2+[V((NB+1,128,H),F32),V((NB,128,H),F32),
-            V((NB,128,2*HP),BF),V((NB,CP,128),F32),V((NB,2*MY,128),BF),V((NB,MY,128),F32),V((2,8,H),F32),V((8,H),F32),
-            pltpu.SemaphoreType.DMA((4,)),pltpu.SemaphoreType.DMA((6,))],
+        out_shape=(pltpu.HBM((NB,128,H),BF),pltpu.HBM((NB,128,H),BF),V((NB,128,H),F32),V((NB,MY,128),F32),sds((8,H),F32),V((NB,2*MY,128),BF),V((NB,CP,128),F32),V((G,2*K,128),F32),V((SL+1,128,128),BF)),
+        in_specs=[SM]*3+[ANY]*4+[VM]*4,out_specs=[ANY]*2+[VM]*7,
+        scratch_shapes=[V((NB,128,128),BF)]*3+[V((NB,128,H),BF)]*2+[V((NB+1,128,H),F32),V((NB,128,2*HP),BF),V((2,8,H),F32),pltpu.SemaphoreType.DMA((3,)),pltpu.SemaphoreType.DMA((2,)),pltpu.SemaphoreType.DMA((SL//(2*GP),))],
         compiler_params=pltpu.CompilerParams(vmem_limit_bytes=VLIM))(sizes,lists,pairs,S,fth,ftl,af,w1,w2,wh,npar)
 
 
-def kc(sizes,lists,S_in,fth_in,ftl_in,af_in,h1h_in,h1l_in,pre_in,pre1_in,h2t_in,lg_in,st,own,recv,labels,pairs,wt,w2m,npar,ncol,
+def kc(sizes,lists,S,pre,pre1,h2t,lg,h1h_in,h1l_in,fth_in,ftl_in,af_in,st,own,recv,labels,pairs,wt,w2m,npar,ncol,
        g_out,
-       S,rfh,rfl,raf,rh,rl,pre,du,h2t,lg,gz,acc,v4,pre1,sums,cross,RH,RS,RL,R1,R2,colsum,sem_i,sem_r,CLS):
-    nb,_,nodes=my_sizes(sizes); BLK=S_in.shape[0]; NB=pre.shape[0]; CP=lg.shape[1]; MY=ncol.shape[0]; H=pre.shape[2]; NS=rh.shape[0]; U8=rh.shape[1]
+       rh,rl,rfh,rfl,raf,du,gz,acc,v4,sums,cross,RH,RS,RL,R1,R2,colsum,sem_r,CLS):
+    nb,_,nodes=my_sizes(sizes); NB=pre.shape[0]; CP=lg.shape[1]; MY=ncol.shape[0]; H=pre.shape[2]; NS=rh.shape[0]; U8=rh.shape[1]
     count=(nb*128).astype(F32); total=nodes.astype(F32)
-    ins=((lg_in,lg),(S_in,S.at[pl.ds(0,BLK)]),(pre_in,pre),(h2t_in,h2t),(pre1_in,pre1))
-    cs=[pltpu.make_async_copy(a,b,sem_i.at[i]) for i,(a,b) in enumerate(ins)]
-    for c in cs[:2]: c.start()
     nch=pl.cdiv(nb,U8)
     def ring(i):
         s=lax.rem(i,NS)
         return [pltpu.make_async_copy(a.at[pl.ds(i*U8,U8)],b.at[s],sem_r.at[s,k]) for k,(a,b) in enumerate(((h1h_in,rh),(h1l_in,rl),(fth_in,rfh),(ftl_in,rfl),(af_in,raf)))]
-    S[BLK]=jnp.zeros((128,128),BF)
+    for i in range(NS):
+        @pl.when(i<nch)
+        def _():
+            for c in ring(i): c.start()
     for r in (sums,cross,RH,RS,RL,R1,R2,colsum): r[...]=jnp.zeros_like(r)
     acc[NB]=jnp.zeros(acc.shape[1:],F32)
     half=pairs.shape[1]
     G=pairs.shape[0]//2
     r=recv[...]
-    D=own[...].reshape(G,2*half,128)-jnp.concatenate([r[:,half:],r[:,:half]],axis=1)
+    D=own[...]-jnp.concatenate([r[:,half:],r[:,:half]],axis=1)
     pair_loss=0.5*jnp.sum(D[:,half:]*D[:,half:])
     Dh,Dl=split((D.reshape(2*G*half,128).T)[:CP]/total); D2=jnp.concatenate([Dh,Dl],axis=0)
     slots=slot_nodes(pairs)
-    cs[0].wait()
     def soft(b0,U):
         hot=jnp.concatenate([one_hot(slots,b0+k) for k in range(U)],axis=1)
         add=dot(D2,hot); add=add[:CP]+add[CP:]
@@ -300,14 +319,7 @@
             gz[b0+k]=jnp.concatenate([h[:,w],l[:,w]],axis=0)
             acc[b0+k,:2*CP]=jnp.zeros((2*CP,128),F32)
     for_blocks(nb,4,soft)
-    cs[1].wait()
-    for c in cs[2:]: c.start()
-    agg_rows(lists,1,S,gz,acc,slice(0,2*CP))
-    for i in range(NS):
-        @pl.when(i<nch)
-        def _():
-            for c in ring(i): c.start()
-    for c in cs[2:]: c.wait()
+    agg_rows(lists,S,gz,acc,slice(0,2*CP))
     mean2=st[2:3,:]; inv2=st[3:4,:]
     a2=npar[2:3,:]*inv2; c2=npar[3:4,:]-mean2*a2
     ha2=0.5*a2; hc2=0.5*c2
@@ -341,7 +353,7 @@
             v4[b0+k]=jnp.concatenate([t[:,w],gt[w].T],axis=0)
     for_blocks(nb,8,proj)
     acc[NB]=jnp.zeros(acc.shape[1:],F32)
-    agg_rows(lists,1,S,v4,acc)
+    agg_rows(lists,S,v4,acc)
     lane=lambda x: jnp.sum(x,axis=1,keepdims=True)
     stc=st[:,:128].T[:MY]
     mean1=stc[:,0:1]; inv1=stc[:,1:2]
@@ -396,18 +408,16 @@
     g_out[q+3*MY:q+3*MY+8,:]=jnp.concatenate([jnp.concatenate([sg2[:,:MY]]+pad,axis=1),jnp.concatenate([sb2[:,:MY]]+pad,axis=1),jnp.broadcast_to(loss,(1,128)),jnp.zeros((5,128),F32)],axis=0)
 
 def call_kc(sizes,lists,S,fth,ftl,af,h1h,h1l,pre,pre1,h2t,lg,st,own,recv,labels,pairs,wt,w2m,npar,ncol,CLS,rows):
-    NB=fth.shape[0]; BLK=S.shape[0]; H=pre.shape[2]; CP=lg.shape[1]; MY=ncol.shape[0]; NS=3; U8=8
-    sds=jax.ShapeDtypeStruct
-    ANY=pl.BlockSpec(memory_space=pl.ANY); VM=pl.BlockSpec(memory_space=pltpu.VMEM); SM=pl.BlockSpec(memory_space=pltpu.SMEM)
+    NB=fth.shape[0]; H=pre.shape[2]; CP=lg.shape[1]; MY=ncol.shape[0]; NS=3; U8=8
+    ANY=pl.BlockSpec(memory_space=pltpu.HBM); VM=pl.BlockSpec(memory_space=pltpu.VMEM); SM=pl.BlockSpec(memory_space=pltpu.SMEM)
     V=pltpu.VMEM
-    return pl.pallas_call(functools.partial(kc,CLS=CLS),out_shape=sds((rows,128),F32),
-        in_specs=[SM,SM]+[ANY]*10+[VM]*9,out_specs=VM,
-        scratch_shapes=[V((BLK+1,128,128),BF)]+[V((NS,U8,128,128),BF)]*3+[V((NS,U8,128,H),BF)]*2+[
-            V((NB,128,H),F32),V((NB,128,H),F32),V((NB,2*MY,128),BF),V((NB,CP,128),F32),V((NB,2*CP,128),BF),V((NB+1,max(3*MY,2*CP),128),F32),
-            V((NB,3*MY,128),BF),V((NB,MY,128),F32),
+    return pl.pallas_call(functools.partial(kc,CLS=CLS),out_shape=jax.ShapeDtypeStruct((rows,128),F32),
+        in_specs=[SM,SM]+[VM]*5+[ANY]*5+[VM]*9,out_specs=VM,
+        scratch_shapes=[V((NS,U8,128,H),BF)]*2+[V((NS,U8,128,128),BF)]*3+[
+            V((NB,128,H),F32),V((NB,2*CP,128),BF),V((NB+1,max(3*MY,2*CP),128),F32),V((NB,3*MY,128),BF),
             V((2,8,H),F32),V((1,128),F32),V((2*MY,3*CP),F32),V((4*MY,H),F32),V((2*MY,H),F32),V((2*MY,128),F32),V((MY,256),F32),V((2,MY,128),F32),
-            pltpu.SemaphoreType.DMA((5,)),pltpu.SemaphoreType.DMA((NS,5))],
-        compiler_params=pltpu.CompilerParams(vmem_limit_bytes=VLIM))(sizes,lists,S,fth,ftl,af,h1h,h1l,pre,pre1,h2t,lg,st,own,recv,labels,pairs,wt,w2m,npar,ncol)
+            pltpu.SemaphoreType.DMA((NS,5))],
+        compiler_params=pltpu.CompilerParams(vmem_limit_bytes=VLIM))(sizes,lists,*in_vmem(S,pre,pre1,h2t,lg),h1h,h1l,fth,ftl,af,st,*in_vmem(own,recv),labels,pairs,wt,w2m,npar,ncol)
 
 def at(index): return {"graph": index}
 def meet(n):
@@ -431,9 +441,9 @@
 
 def call_kx(own,n):
     VM=pl.BlockSpec(memory_space=pltpu.VMEM)
-    return pl.pallas_call(functools.partial(kx,n=n),out_shape=jax.ShapeDtypeStruct(own.shape,own.dtype),in_specs=[VM],out_specs=VM,
+    return pl.pallas_call(functools.partial(kx,n=n),out_shape=pltpu.VMEM(own.shape,own.dtype),in_specs=[VM],out_specs=VM,
         scratch_shapes=[pltpu.SemaphoreType.DMA((n-1,)),pltpu.SemaphoreType.DMA((n-1,))],
-        compiler_params=pltpu.CompilerParams(collective_id=1,has_side_effects=True))(own)
+        compiler_params=pltpu.CompilerParams(vmem_limit_bytes=8<<20,collective_id=1,has_side_effects=True))(*in_vmem(own))
 
 def kr(g,out,parts,send1,recv1,send2,recv2,n):
     me=lax.axis_index("graph")
@@ -584,8 +594,8 @@
     S,lists,fth,ftl,af=call_k0(sizes,blocks[0],features.transpose(1,0,2),block_values[0])
     w1,w2,wh,npar,wt,w2m,ncol=call_kw(packed,halves,H,CP)
     pairs=pair_nodes[0].reshape(2*G,PEER)
-    h1h,h1l,pre,pre1,st,h2t,lg,own=call_kb(sizes,lists,S,fth,ftl,af,w1,w2,wh,npar,pairs,MY=MY,CP=CP)
-    recv=call_kx(own.reshape(G,2*PEER,128),n_graph)
+    h1h,h1l,pre,pre1,st,h2t,lg,own,S=call_kb(sizes,lists,S,fth,ftl,af,w1,w2,wh,npar,pairs,MY=MY,CP=CP)
+    recv=call_kx(own,n_graph)
     unit=8*n_graph; rows=-(-(2*H//128*MY+3*MY+8)//unit)*unit
     g=call_kc(sizes,lists,S,fth,ftl,af,h1h,h1l,pre,pre1,h2t,lg,st,own,recv,labels[0].reshape(NB,1,128),pairs,wt,w2m,npar,ncol,CLS=CLS,rows=rows)
     g=call_kr(g,n_graph)

time: 155 us -> 148 us (0.955)
  Pallas kernels: 146 us -> 139 us
    pallas_call x4, Pallas kernels: 126 us -> 118 us  [the longest x1 47.4 us: call_kb(): pl.pallas_call(kb, out_shape=(pltpu.HBM((NB, 128, H), BF), pltpu.HBM((NB,...]
  transfers between devices with their start and end apart: 3 -> 3, of which waited for: 0 -> 0; matrix products, arithmetic and copies ran while one was open for 0% -> 0% of each run, Pallas kernels for 18% -> 17%
where the time goes in v4:
time: 148 us; the launch traced here: 147 us
  Pallas kernels  139 us (94%)
  starting transfers between devices  6.96 us (5%)
    pallas_call x1, Pallas kernels, call_kb(): pl.pallas_call(kb, out_shape=(pltpu.HBM((NB, 128, H), BF), pltpu.HBM((NB,...  47.4 us
    pallas_call x1, Pallas kernels, call_kc(): pl.pallas_call(functools.partial(kc, CLS=CLS), out_shape=jax.ShapeDtypeSt...  41.1 us
    pallas_call x1, Pallas kernels, call_k0(): pl.pallas_call(k0, out_shape=(pltpu.HBM((SL, 128, 128), BF), pltpu.HBM((8...  24.6 us
    pallas_call x1, Pallas kernels, call_kr(): pl.pallas_call(functools.partial(kr, n=n), out_shape=jax.ShapeDtypeStruct...  12.4 us
    ppermute x3, starting transfers between devices, per_device(): lax.ppermute(half, 'col', [((j + k) % n_col, j) for j in range(n_col)])  6.96 us
    pallas_call x1, Pallas kernels, call_kx(): pl.pallas_call(functools.partial(kx, n=n), out_shape=pltpu.VMEM(own.shape...  4.78 us
    pallas_call x1, Pallas kernels, call_kw(): pl.pallas_call(functools.partial(kw, n_col=n_col, CP=CP), out_shape=(sds(...  4.25 us
  transfers between devices with their start and end apart: 3, of which 0 were waited for; matrix products, arithmetic and copies ran while one was open for 0% of the time, Pallas kernels for 17%

profile of v4, /device:TPU:0, one launch (start us, length us, event | category | flops | bytes accessed | tf_op | source)
XLA Modules:
  0.0 147.2 jit_solution(15296158311627192275)
XLA Ops:
  0.6 1.7 %shard_map.282 = (f32[496,128]{1,0:T(8,128)}, f32[248,128]{1,0:T(8,128)}) custom-call(f32[2,64,100]{2,1,0:T(8,128)} %bitcast.30, f32[2,64,256]{2,1,0:T(8,128)} %bitcast.28, f32[47,2,64]{2,1,0:T(2,128)} %bitcast.32, f32[2,2,64]{2,1,0:T(2,128)} %refs_3_.1), custom_call_target="tpu_custom_call" | custom-call | tf_op jit(solution)/shard_map/pallas_call | solution.py:494
  2.3 3.0 %collective-permute-start.2 = (f32[248,128]{1,0:T(8,128)}, f32[248,128]{1,0:T(8,128)S(1)}, u32[]{:S(2)}, u32[]{:S(2)}) collective-permute-start(f32[248,128]{1,0:T(8,128)} %get-tuple-element.57), channel_id=1, source_target_pairs={{3,0},{0,1},{1,2},{2,3},{7,4},{4,5},{5,6},{6,7},{11,8},{8,9},{9,10... | collective-permute-start | bytes 380936 | tf_op jit(solution)/shard_map/ppermute | solution.py:592
  5.4 2.6 %collective-permute-start.1 = (f32[248,128]{1,0:T(8,128)}, f32[248,128]{1,0:T(8,128)S(1)}, u32[]{:S(2)}, u32[]{:S(2)}) collective-permute-start(f32[248,128]{1,0:T(8,128)} %get-tuple-element.57), channel_id=1, source_target_pairs={{2,0},{3,1},{0,2},{1,3},{6,4},{7,5},{4,6},{5,7},{10,8},{11,9},{8,1... | collective-permute-start | bytes 380936 | tf_op jit(solution)/shard_map/ppermute | solution.py:592
  8.0 1.3 collective-permute-start
  9.3 24.6 %shard_map.281 = (bf16[576,128,128]{2,1,0:T(8,128)(2,1)}, s32[8,640]{1,0:T(8,128)}, bf16[64,128,128]{2,1,0:T(8,128)(2,1)}, bf16[64,128,128]{2,1,0:T(8,128)(2,1)}, bf16[64,128,128]{2,1,0:T(8,128)(2,1)}) custom-call(s32[2,8]{1,0:T(2,128)} %bitcast.43, s32[2,512]{1,0:T(2,128)} %bitcast.47, f32[100,1,8192]{2,1,0:T(1,128)} %bitcast.27, f32[512,128,128]{2,1,0:T(8,128)} %bitcast.26), custom_call_target="tpu_custom_call" | custom-call | tf_op jit(solution)/shard_map/pallas_call | solution.py:147
  33.9 0.0 collective-permute-done.2.refs_2_
  33.9 0.0 copy-start
  33.9 0.0 collective-permute-done.1.refs_1_
  33.9 0.0 copy-start.1
  34.0 0.0 collective-permute-done.refs_0_
  34.0 0.0 copy-start.2
  34.0 0.6 copy-done
  34.6 0.0 copy-done.1
  34.6 0.0 copy-done.2
  34.7 4.2 %shard_map.283 = (bf16[256,512]{1,0:T(8,128)(2,1)}, bf16[256,1536]{1,0:T(8,128)(2,1)}, bf16[256,256]{1,0:T(8,128)(2,1)}, f32[8,256]{1,0:T(8,128)}, bf16[384,256]...) custom-call(f32[496,128]{1,0:T(8,128)} %get-tuple-element.56.own, f32[248,128]{1,0:T(8,128)} %copy-done.2, ...), custom_call_target="tpu_custom_call" | custom-call | tf_op jit(solution)/shard_map/pallas_call | solution.py:544
  38.9 47.4 %shard_map.284 = (bf16[64,128,256]{2,1,0:T(8,128)(2,1)}, bf16[64,128,256]{2,1,0:T(8,128)(2,1)}, f32[64,128,256]{2,1,0:T(8,128)S(1)}, f32[64,64,128]{2,1,0:T(8,12...) custom-call(s32[2,8]{1,0:T(2,128)} %bitcast.44, ...), custom_call_target="tpu_custom_call" | custom-call | tf_op jit(solution)/shard_map/pallas_call | solution.py:274
  86.3 4.8 %shard_map.285.recv = f32[8,16,128]{2,1,0:T(8,128)S(1)} custom-call(f32[8,16,128]{2,1,0:T(8,128)S(1)} %get-tuple-element.70.own), custom_call_target="tpu_custom_call" | custom-call | tf_op jit(solution)/shard_map/pallas_call | solution.py:444
  91.1 41.1 %shard_map.286.g = f32[512,128]{1,0:T(8,128)} custom-call(s32[2,8]{1,0:T(2,128)} %bitcast.45, s32[8,640]{1,0:T(8,128)} %get-tuple-element.51.lists, bf16[577,128,128]{2,1,0:T(8,128)(2,1)S(1)} %get-tuple-element.62.S, f32[64,128,256]{2,1,0:T(8,128)S(1)} %get-tuple-element.63.pre, f32[64,64,128]{2,1,0:T(8,128)S(1)} %get-tuple-element.64.pre1, ...), custom_call_target="tpu_custom_call" | custom-call | tf_op jit(solution)/shard_map/pallas_call | solution.py:414
  132.2 12.4 %shard_map.287.g = f32[512,128]{1,0:T(8,128)} custom-call(f32[512,128]{1,0:T(8,128)} %shard_map.286.g), custom_call_target="tpu_custom_call" | custom-call | tf_op jit(solution)/shard_map/pallas_call | solution.py:474
  144.6 2.4 %shard_map.288 = (f32[2,64,100]{2,1,0:T(8,128)}, f32[2,64,100]{2,1,0:T(8,128)}, f32[2,64,100]{2,1,0:T(8,128)}, f32[2,64,256]{2,1,0:T(8,128)}, f32[2,64,256]{2,1,...) custom-call(s32[2,8]{1,0:T(2,128)} %bitcast.46, ...), custom_call_target="tpu_custom_call" | custom-call | tf_op jit(solution)/shard_map/pallas_call | solution.py:577
Async XLA Ops:
  2.3 31.6 %collective-permute-start.2 = (f32[248,128]{1,0:T(8,128)}, f32[248,128]{1,0:T(8,128)S(1)}, u32[]{:S(2)}, u32[]{:S(2)}) collective-permute-start(f32[248,128]{1,0:T(8,128)} %get-tuple-element.57), channel_id=1, source_target_pairs={{3,0},{0,1},{1,2},{2,3},{7,4},{4,5},{5,6},{6,7},{11,8},{8,9},{9,10... | collective-permute-start | bytes 380936 | tf_op jit(solution)/shard_map/ppermute | solution.py:592
  5.4 28.6 %collective-permute-start.1 = (f32[248,128]{1,0:T(8,128)}, f32[248,128]{1,0:T(8,128)S(1)}, u32[]{:S(2)}, u32[]{:S(2)}) collective-permute-start(f32[248,128]{1,0:T(8,128)} %get-tuple-element.57), channel_id=1, source_target_pairs={{2,0},{3,1},{0,2},{1,3},{6,4},{7,5},{4,6},{5,7},{10,8},{11,9},{8,1... | collective-permute-start | bytes 380936 | tf_op jit(solution)/shard_map/ppermute | solution.py:592
  8.0 26.0 %collective-permute-start = (f32[248,128]{1,0:T(8,128)}, f32[248,128]{1,0:T(8,128)S(1)}, u32[]{:S(2)}, u32[]{:S(2)}) collective-permute-start(f32[248,128]{1,0:T(8,128)} %get-tuple-element.57), channel_id=1, source_target_pairs={{1,0},{2,1},{3,2},{0,3},{5,4},{6,5},{7,6},{4,7},{9,8},{10,9},{11,1... | collective-permute-start | bytes 380936 | tf_op jit(solution)/shard_map/ppermute | solution.py:592
  33.9 0.7 copy-start
  33.9 0.7 copy-start.1
  34.0 0.7 copy-start.2

commit v5 on v4

--- a/solution.py
+++ b/solution.py
@@ -185,9 +185,44 @@
 def one_hot(slots,b):
     return jnp.where(slots==lax.broadcasted_iota(I32,(1,128),1)+b*128,1.0,0.0).astype(BF)
 
-def kb(sizes,lists,pairs,S_in,fth_in,ftl_in,af_in,w1,w2,wh,npar,
-       h1h_out,h1l_out,pre,pre1,st,h2t,lg,own_out,S,
-       fth,ftl,af,h1h,h1l,acc,zz,sums,sem_i,sem_o,sem_S):
+def prepare(x,w1_out,w2_out,wh_out,npar_out,wt_out,w2m_out,ncol_out,CP):
+    n_col=len(x)
+    H=w1_out.shape[0]; MY=H//n_col; nk=H//128
+    col=lax.axis_index("col")
+    back=lax.rem(H-col*MY,H)
+    heads=([],[]); norms=[]; mine=([],[])
+    for k in range(n_col):
+        r=slice(k*MY,k*MY+MY)
+        q=2*nk*MY
+        h,l=split(x[k][q:q+MY,:])
+        w1_out[r,:]=jnp.concatenate([h,h,l,x[k][q+MY:q+2*MY,:].astype(BF)],axis=1)
+        two=[]
+        for half in range(2):
+            w=jnp.concatenate([x[k][(half*nk+i)*MY:(half*nk+i+1)*MY,:] for i in range(nk)],axis=1)
+            w=pltpu.roll(w,back,1)
+            mine[half].append(w[:,:128])
+            h,l=split(w); two+=[h,h,l]
+            heads[half].append(x[k][q+2*MY+half*CP:q+2*MY+(half+1)*CP,:MY])
+        w2_out[r,:]=jnp.concatenate(two,axis=1)
+        norms.append(x[k][q+2*MY+2*CP:q+2*MY+2*CP+8,:MY])
+    npar=jnp.concatenate(norms,axis=1)
+    npar_out[...]=npar
+    ncol_out[...]=npar[:,:128].T[:MY]
+    (ch,cl),(dh,dl)=[split(jnp.concatenate(p,axis=1)) for p in heads]
+    z=jnp.zeros((HP-CP,H),BF)
+    wh_out[...]=jnp.concatenate([ch,z,dh,z,cl,z,dl,z],axis=0)
+    z=jnp.zeros((128-2*CP,H),BF)
+    th=jnp.concatenate([ch,dh,z],axis=0); tl=jnp.concatenate([cl,dl,z],axis=0)
+    wt_out[...]=jnp.concatenate([th,th,tl],axis=0)
+    for half in range(2):
+        h,l=split(jnp.concatenate(mine[half],axis=0).T[:MY])
+        w2m_out[2*half*MY:(2*half+2)*MY,:]=jnp.concatenate([h,l],axis=0)
+
+def kb(sizes,lists,pairs,S_in,fth_in,ftl_in,af_in,*refs,n_col):
+    shards=refs[:n_col]
+    (
+       h1h_out,h1l_out,pre,pre1,st,h2t,lg,own_out,S,npar,wt,w2m,ncol,
+       w1,w2,wh,fth,ftl,af,h1h,h1l,acc,zz,sums,sem_i,sem_o,sem_S)=refs[n_col:]
     nb,_,_=my_sizes(sizes); NB=fth.shape[0]; CP=lg.shape[1]; MY=pre1.shape[1]
     count=(nb*128).astype(F32)
     cs=[pltpu.make_async_copy(a,b,sem_i.at[i]) for i,(a,b) in enumerate(((fth_in,fth),(ftl_in,ftl),(af_in,af)))]
@@ -195,6 +230,7 @@
     S_start,S_wait=load_S(lists,S_in,S,sem_S); S_start()
     S[S_in.shape[0]]=jnp.zeros((128,128),BF)
     st[...]=jnp.zeros_like(st)
+    prepare(shards,w1,w2,wh,npar,wt,w2m,ncol,CP)
     for c in cs: c.wait()
     def first(b0,U):
         h=blk(fth,b0,U)
@@ -266,16 +302,16 @@
     lax.fori_loop(0,G,slot,0)
     for o in outs: o.wait()
 
-def call_kb(sizes,lists,S,fth,ftl,af,w1,w2,wh,npar,pairs,MY,CP):
-    NB=fth.shape[0]; H=w2.shape[0]; SL=S.shape[0]; G=pairs.shape[0]//2; K=pairs.shape[1]
+def call_kb(sizes,lists,S,fth,ftl,af,shards,pairs,MY,CP):
+    n_col=len(shards); NB=fth.shape[0]; H=MY*n_col; SL=S.shape[0]; G=pairs.shape[0]//2; K=pairs.shape[1]
     sds=jax.ShapeDtypeStruct
     ANY=pl.BlockSpec(memory_space=pltpu.HBM); VM=pl.BlockSpec(memory_space=pltpu.VMEM); SM=pl.BlockSpec(memory_space=pltpu.SMEM)
     V=pltpu.VMEM
-    return pl.pallas_call(kb,
-        out_shape=(pltpu.HBM((NB,128,H),BF),pltpu.HBM((NB,128,H),BF),V((NB,128,H),F32),V((NB,MY,128),F32),sds((8,H),F32),V((NB,2*MY,128),BF),V((NB,CP,128),F32),V((G,2*K,128),F32),V((SL+1,128,128),BF)),
-        in_specs=[SM]*3+[ANY]*4+[VM]*4,out_specs=[ANY]*2+[VM]*7,
-        scratch_shapes=[V((NB,128,128),BF)]*3+[V((NB,128,H),BF)]*2+[V((NB+1,128,H),F32),V((NB,128,2*HP),BF),V((2,8,H),F32),pltpu.SemaphoreType.DMA((3,)),pltpu.SemaphoreType.DMA((2,)),pltpu.SemaphoreType.DMA((SL//(2*GP),))],
-        compiler_params=pltpu.CompilerParams(vmem_limit_bytes=VLIM))(sizes,lists,pairs,S,fth,ftl,af,w1,w2,wh,npar)
+    return pl.pallas_call(functools.partial(kb,n_col=n_col),
+        out_shape=(pltpu.HBM((NB,128,H),BF),pltpu.HBM((NB,128,H),BF),V((NB,128,H),F32),V((NB,MY,128),F32),sds((8,H),F32),V((NB,2*MY,128),BF),V((NB,CP,128),F32),V((G,2*K,128),F32),V((SL+1,128,128),BF),sds((8,H),F32),sds((384,H),BF),sds((4*MY,H),BF),sds((MY,8),F32)),
+        in_specs=[SM]*3+[ANY]*4+[VM]*n_col,out_specs=[ANY]*2+[VM]*11,
+        scratch_shapes=[V((H,512),BF),V((H,6*H),BF),V((4*HP,H),BF)]+[V((NB,128,128),BF)]*3+[V((NB,128,H),BF)]*2+[V((NB+1,128,H),F32),V((NB,128,2*HP),BF),V((2,8,H),F32),pltpu.SemaphoreType.DMA((3,)),pltpu.SemaphoreType.DMA((2,)),pltpu.SemaphoreType.DMA((SL//(2*GP),))],
+        compiler_params=pltpu.CompilerParams(vmem_limit_bytes=VLIM))(sizes,lists,pairs,S,fth,ftl,af,*shards)
 
 
 def kc(sizes,lists,S,pre,pre1,h2t,lg,h1h_in,h1l_in,fth_in,ftl_in,af_in,st,own,recv,labels,pairs,wt,w2m,npar,ncol,
@@ -475,7 +511,7 @@
         scratch_shapes=[pltpu.VMEM((n-1,g.shape[0]//n,128),F32),D,D,D,D],
         compiler_params=pltpu.CompilerParams(collective_id=2,has_side_effects=True))(g)
 
-def kp(wf,ws,wh,npar,out,half):
+def kp(wf,ws,wh,npar,out):
     _,MY,FIN=wf.shape; H=ws.shape[2]; CLS=wh.shape[0]; CP=-(-CLS//16)*16; nk=H//128
     out[...]=jnp.zeros_like(out)
     for h in range(2):
@@ -484,68 +520,12 @@
         r=2*nk*MY+h*MY; out[r:r+MY,:FIN]=wf[h]
         r=2*nk*MY+2*MY+h*CP; out[r:r+CLS,:MY]=wh[:,h,:]
         r=2*nk*MY+2*MY+2*CP+2*h; out[r:r+2,:MY]=npar[h]
-    core=lax.rem(lax.axis_index("graph"),2); n=half.shape[0]
-    half[...]=out[pl.ds(pl.multiple_of(core*n,8),n),:]
 
 def call_kp(wf,ws,wh,npar):
     _,MY,FIN=wf.shape; H=ws.shape[2]; CP=-(-wh.shape[0]//16)*16
     rows=-(-(2*H//128*MY+2*MY+2*CP+8)//16)*16
     VM=pl.BlockSpec(memory_space=pltpu.VMEM)
-    return pl.pallas_call(kp,out_shape=(jax.ShapeDtypeStruct((rows,128),F32),jax.ShapeDtypeStruct((rows//2,128),F32)),in_specs=[VM]*4,out_specs=[VM]*2)(wf,ws,wh,npar)
-
-def kw(own,*refs,n_col,CP):
-    halves=refs[:n_col-1]; w1_out,w2_out,wh_out,npar_out,wt_out,w2m_out,ncol_out,x,send,recv=refs[n_col-1:]
-    me=lax.axis_index("graph"); core=lax.rem(me,2); twin=me+1-2*core
-    barrier=pltpu.get_barrier_semaphore()
-    pl.semaphore_signal(barrier,inc=1,device_id=at(twin),device_id_type=pl.DeviceIdType.MESH)
-    n=own.shape[0]//2; rows=pl.ds(pl.multiple_of(core*n,8),n)
-    pl.semaphore_wait(barrier,1)
-    copies=[]
-    for k in range(1,n_col):
-        c=pltpu.make_async_remote_copy(src_ref=halves[k-1],dst_ref=x.at[k,rows],send_sem=send.at[k-1],recv_sem=recv.at[k-1],
-            device_id=at(twin),device_id_type=pl.DeviceIdType.MESH)
-        c.start(); copies.append(c)
-    x[0]=own[...]
-    for k in range(1,n_col): x[k,rows,:]=halves[k-1][...]
-    for c in copies: c.wait()
-    H=w1_out.shape[0]; MY=H//n_col; nk=H//128
-    col=lax.axis_index("col")
-    back=lax.rem(H-col*MY,H)
-    heads=([],[]); norms=[]; mine=([],[])
-    for k in range(n_col):
-        j=k; r=slice(k*MY,k*MY+MY)
-        q=2*nk*MY
-        h,l=split(x[j,q:q+MY,:])
-        w1_out[r,:]=jnp.concatenate([h,h,l,x[j,q+MY:q+2*MY,:].astype(BF)],axis=1)
-        two=[]
-        for half in range(2):
-            w=jnp.concatenate([x[j,(half*nk+i)*MY:(half*nk+i+1)*MY,:] for i in range(nk)],axis=1)
-            w=pltpu.roll(w,back,1)
-            mine[half].append(w[:,:128])
-            h,l=split(w); two+=[h,h,l]
-            heads[half].append(x[j,q+2*MY+half*CP:q+2*MY+(half+1)*CP,:MY])
-        w2_out[r,:]=jnp.concatenate(two,axis=1)
-        norms.append(x[j,q+2*MY+2*CP:q+2*MY+2*CP+8,:MY])
-    npar=jnp.concatenate(norms,axis=1)
-    npar_out[...]=npar
-    ncol_out[...]=npar[:,:128].T[:MY]
-    (ch,cl),(dh,dl)=[split(jnp.concatenate(p,axis=1)) for p in heads]
-    z=jnp.zeros((HP-CP,H),BF)
-    wh_out[...]=jnp.concatenate([ch,z,dh,z,cl,z,dl,z],axis=0)
-    z=jnp.zeros((128-2*CP,H),BF)
-    th=jnp.concatenate([ch,dh,z],axis=0); tl=jnp.concatenate([cl,dl,z],axis=0)
-    wt_out[...]=jnp.concatenate([th,th,tl],axis=0)
-    for half in range(2):
-        h,l=split(jnp.concatenate(mine[half],axis=0).T[:MY])
-        w2m_out[2*half*MY:(2*half+2)*MY,:]=jnp.concatenate([h,l],axis=0)
-
-def call_kw(own,halves,H,CP):
-    n_col=1+len(halves); MY=H//n_col; sds=jax.ShapeDtypeStruct; VM=pl.BlockSpec(memory_space=pltpu.VMEM)
-    return pl.pallas_call(functools.partial(kw,n_col=n_col,CP=CP),
-        out_shape=(sds((H,512),BF),sds((H,6*H),BF),sds((4*HP,H),BF),sds((8,H),F32),sds((384,H),BF),sds((4*MY,H),BF),sds((MY,8),F32)),
-        in_specs=[VM]*n_col,out_specs=[VM]*7,
-        scratch_shapes=[pltpu.VMEM((n_col,)+own.shape,F32),pltpu.SemaphoreType.DMA((n_col-1,)),pltpu.SemaphoreType.DMA((n_col-1,))],
-        compiler_params=pltpu.CompilerParams(collective_id=3,has_side_effects=True))(own,*halves)
+    return pl.pallas_call(kp,out_shape=jax.ShapeDtypeStruct((rows,128),F32),in_specs=[VM]*4,out_specs=VM)(wf,ws,wh,npar)
 
 def renew(weight, momentum, average, gradient):
     momentum_new = MOMENTUM * momentum + gradient
@@ -588,13 +568,12 @@
     weights=native(weight_first,weight_second,weight_head,norm_params)
     momenta=native(momentum_first,momentum_second,momentum_head,momentum_norms)
     averages=native(average_first,average_second,average_head,average_norms)
-    packed,half=call_kp(*weights)
-    halves=[lax.ppermute(half,"col",[((j+k)%n_col,j) for j in range(n_col)]) for k in range(1,n_col)]
+    packed=call_kp(*weights)
+    shards=[packed]+[lax.ppermute(packed,"col",[((j+k)%n_col,j) for j in range(n_col)]) for k in range(1,n_col)]
     sizes=group_sizes.T
     S,lists,fth,ftl,af=call_k0(sizes,blocks[0],features.transpose(1,0,2),block_values[0])
-    w1,w2,wh,npar,wt,w2m,ncol=call_kw(packed,halves,H,CP)
     pairs=pair_nodes[0].reshape(2*G,PEER)
-    h1h,h1l,pre,pre1,st,h2t,lg,own,S=call_kb(sizes,lists,S,fth,ftl,af,w1,w2,wh,npar,pairs,MY=MY,CP=CP)
+    h1h,h1l,pre,pre1,st,h2t,lg,own,S,npar,wt,w2m,ncol=call_kb(sizes,lists,S,fth,ftl,af,shards,pairs,MY=MY,CP=CP)
     recv=call_kx(own,n_graph)
     unit=8*n_graph; rows=-(-(2*H//128*MY+3*MY+8)//unit)*unit
     g=call_kc(sizes,lists,S,fth,ftl,af,h1h,h1l,pre,pre1,h2t,lg,st,own,recv,labels[0].reshape(NB,1,128),pairs,wt,w2m,npar,ncol,CLS=CLS,rows=rows)

time: 148 us -> 144 us (0.973)
  Pallas kernels: 139 us -> 132 us
  waiting for transfers between devices: 0.01 us -> 2.73 us
    pallas_call x1, Pallas kernels: 4.78 us -> 46.1 us  [call_kx(): pl.pallas_call(functools.partial(kx, n=n), out_shape=pltpu.VMEM(own.shape...]
    pallas_call x3 -> x2, Pallas kernels: 53.3 us -> 17.1 us  [the longest x1 15.5 us: call_kb(): pl.pallas_call(functools.partial(kb, n_col=n_col), out_shape=(pltpu.HBM((...]
    pallas_call x1, Pallas kernels: 41.1 us -> 11.2 us  [call_kc(): pl.pallas_call(functools.partial(kc, CLS=CLS), out_shape=jax.ShapeDtypeSt...]
    pallas_call x1, Pallas kernels: 12.4 us -> 42.1 us  [call_kr(): pl.pallas_call(functools.partial(kr, n=n), out_shape=jax.ShapeDtypeStruct...]
    pallas_call x1, Pallas kernels: 24.6 us -> 12.7 us  [call_k0(): pl.pallas_call(k0, out_shape=(pltpu.HBM((SL, 128, 128), BF), pltpu.HBM((8...]
    ppermute x3, waiting for transfers between devices: 0.01 us -> 2.73 us  [per_device(): lax.ppermute(packed, 'col', [((j + k) % n_col, j) for j in range(n_col)])]
  transfers between devices with their start and end apart: 3 -> 3, of which waited for: 0 -> 1; matrix products, arithmetic and copies ran while one was open for 0% -> 0% of each run, Pallas kernels for 17% -> 9%
where the time goes in v5:
time: 144 us; the launch traced here: 143 us
  Pallas kernels  132 us (92%)
  starting transfers between devices  6.96 us (5%)
  waiting for transfers between devices  2.73 us (2%)
    pallas_call x1, Pallas kernels, call_kx(): pl.pallas_call(functools.partial(kx, n=n), out_shape=pltpu.VMEM(own.shape...  46.1 us
    pallas_call x1, Pallas kernels, call_kr(): pl.pallas_call(functools.partial(kr, n=n), out_shape=jax.ShapeDtypeStruct...  42.1 us
    pallas_call x1, Pallas kernels, call_kb(): pl.pallas_call(functools.partial(kb, n_col=n_col), out_shape=(pltpu.HBM((...  15.5 us
    pallas_call x1, Pallas kernels, call_k0(): pl.pallas_call(k0, out_shape=(pltpu.HBM((SL, 128, 128), BF), pltpu.HBM((8...  12.7 us
    pallas_call x1, Pallas kernels, call_kc(): pl.pallas_call(functools.partial(kc, CLS=CLS), out_shape=jax.ShapeDtypeSt...  11.2 us
    ppermute x3, starting transfers between devices, per_device(): lax.ppermute(packed, 'col', [((j + k) % n_col, j) for j in range(n_col)])  6.96 us
  transfers between devices with their start and end apart: 3, of which 1 were waited for; matrix products, arithmetic and copies ran while one was open for 0% of the time, Pallas kernels for 9%

profile of v5, /device:TPU:0, one launch (start us, length us, event | category | flops | bytes accessed | tf_op | source)
XLA Modules:
  0.0 143.0 jit_solution(8980594341137195199)
XLA Ops:
  0.6 1.7 %shard_map.282.refs_0_ = f32[496,128]{1,0:T(8,128)} custom-call(f32[2,64,100]{2,1,0:T(8,128)} %bitcast.30, f32[2,64,256]{2,1,0:T(8,128)} %bitcast.28, f32[47,2,64]{2,1,0:T(2,128)} %bitcast.32, f32[2,2,64]{2,1,0:T(2,128)} %refs_3_.1), custom_call_target="tpu_custom_call" | custom-call | tf_op jit(solution)/shard_map/pallas_call | solution.py:528
  2.3 3.0 %collective-permute-start.2 = (f32[496,128]{1,0:T(8,128)}, f32[496,128]{1,0:T(8,128)S(1)}, u32[]{:S(2)}, u32[]{:S(2)}) collective-permute-start(f32[496,128]{1,0:T(8,128)} %shard_map.282.refs_0_), channel_id=1, source_target_pairs={{3,0},{0,1},{1,2},{2,3},{7,4},{4,5},{5,6},{6,7},{11,8},{8,9},{9,10... | collective-permute-start | bytes 761864 | tf_op jit(solution)/shard_map/ppermute | solution.py:572
  5.3 2.6 %collective-permute-start.1 = (f32[496,128]{1,0:T(8,128)}, f32[496,128]{1,0:T(8,128)S(1)}, u32[]{:S(2)}, u32[]{:S(2)}) collective-permute-start(f32[496,128]{1,0:T(8,128)} %shard_map.282.refs_0_), channel_id=1, source_target_pairs={{2,0},{3,1},{0,2},{1,3},{6,4},{7,5},{4,6},{5,7},{10,8},{11,9},{8,1... | collective-permute-start | bytes 761864 | tf_op jit(solution)/shard_map/ppermute | solution.py:572
  7.9 1.3 collective-permute-start
  9.3 12.7 %shard_map.281 = (bf16[576,128,128]{2,1,0:T(8,128)(2,1)}, s32[8,640]{1,0:T(8,128)}, bf16[64,128,128]{2,1,0:T(8,128)(2,1)}, bf16[64,128,128]{2,1,0:T(8,128)(2,1)}, bf16[64,128,128]{2,1,0:T(8,128)(2,1)}) custom-call(s32[2,8]{1,0:T(2,128)} %bitcast.43, s32[2,512]{1,0:T(2,128)} %bitcast.47, f32[100,1,8192]{2,1,0:T(1,128)} %bitcast.27, f32[512,128,128]{2,1,0:T(8,128)} %bitcast.26), custom_call_target="tpu_custom_call" | custom-call | tf_op jit(solution)/shard_map/pallas_call | solution.py:147
  22.0 0.0 collective-permute-done.2.refs_3_
  22.0 0.0 copy-start
  22.0 2.7 %collective-permute-done.1.refs_2_ = f32[496,128]{1,0:T(8,128)S(1)} collective-permute-done((f32[496,128]{1,0:T(8,128)}, f32[496,128]{1,0:T(8,128)S(1)}, u32[]{:S(2)}, u32[]{:S(2)}) %collective-permute-start.1) | collective-permute-done | bytes 253984 | tf_op jit(solution)/shard_map/ppermute | solution.py:572
  24.7 0.0 copy-start.1
  24.7 0.0 collective-permute-done.refs_1_
  24.7 0.0 copy-start.2
  24.7 0.0 copy-done
  24.7 0.7 copy-done.1
  25.4 0.1 copy-done.2
  25.5 15.5 %shard_map.283 = (bf16[64,128,256]{2,1,0:T(8,128)(2,1)}, bf16[64,128,256]{2,1,0:T(8,128)(2,1)}, f32[64,128,256]{2,1,0:T(8,128)S(1)}, f32[64,64,128]{2,1,0:T(8,12...) custom-call(s32[2,8]{1,0:T(2,128)} %bitcast.44, ...), custom_call_target="tpu_custom_call" | custom-call | tf_op jit(solution)/shard_map/pallas_call | solution.py:310
  41.0 46.1 %shard_map.284.recv = f32[8,16,128]{2,1,0:T(8,128)S(1)} custom-call(f32[8,16,128]{2,1,0:T(8,128)S(1)} %get-tuple-element.59.own), custom_call_target="tpu_custom_call" | custom-call | tf_op jit(solution)/shard_map/pallas_call | solution.py:480
  87.1 11.2 %shard_map.285.g = f32[512,128]{1,0:T(8,128)} custom-call(s32[2,8]{1,0:T(2,128)} %bitcast.45, s32[8,640]{1,0:T(8,128)} %get-tuple-element.46.lists, bf16[577,128,128]{2,1,0:T(8,128)(2,1)S(1)} %get-tuple-element.51.S, f32[64,128,256]{2,1,0:T(8,128)S(1)} %get-tuple-element.52.pre, f32[64,64,128]{2,1,0:T(8,128)S(1)} %get-tuple-element.53.pre1, ...), custom_call_target="tpu_custom_call" | custom-call | tf_op jit(solution)/shard_map/pallas_call | solution.py:450
  98.3 42.1 %shard_map.286.g = f32[512,128]{1,0:T(8,128)} custom-call(f32[512,128]{1,0:T(8,128)} %shard_map.285.g), custom_call_target="tpu_custom_call" | custom-call | tf_op jit(solution)/shard_map/pallas_call | solution.py:510
  140.4 2.4 %shard_map.287 = (f32[2,64,100]{2,1,0:T(8,128)}, f32[2,64,100]{2,1,0:T(8,128)}, f32[2,64,100]{2,1,0:T(8,128)}, f32[2,64,256]{2,1,0:T(8,128)}, f32[2,64,256]{2,1,...) custom-call(s32[2,8]{1,0:T(2,128)} %bitcast.46, ...), custom_call_target="tpu_custom_call" | custom-call | tf_op jit(solution)/shard_map/pallas_call | solution.py:557
Async XLA Ops:
  2.3 19.7 %collective-permute-start.2 = (f32[496,128]{1,0:T(8,128)}, f32[496,128]{1,0:T(8,128)S(1)}, u32[]{:S(2)}, u32[]{:S(2)}) collective-permute-start(f32[496,128]{1,0:T(8,128)} %shard_map.282.refs_0_), channel_id=1, source_target_pairs={{3,0},{0,1},{1,2},{2,3},{7,4},{4,5},{5,6},{6,7},{11,8},{8,9},{9,10... | collective-permute-start | bytes 761864 | tf_op jit(solution)/shard_map/ppermute | solution.py:572
  5.3 19.4 %collective-permute-start.1 = (f32[496,128]{1,0:T(8,128)}, f32[496,128]{1,0:T(8,128)S(1)}, u32[]{:S(2)}, u32[]{:S(2)}) collective-permute-start(f32[496,128]{1,0:T(8,128)} %shard_map.282.refs_0_), channel_id=1, source_target_pairs={{2,0},{3,1},{0,2},{1,3},{6,4},{7,5},{4,6},{5,7},{10,8},{11,9},{8,1... | collective-permute-start | bytes 761864 | tf_op jit(solution)/shard_map/ppermute | solution.py:572
  7.9 16.8 %collective-permute-start = (f32[496,128]{1,0:T(8,128)}, f32[496,128]{1,0:T(8,128)S(1)}, u32[]{:S(2)}, u32[]{:S(2)}) collective-permute-start(f32[496,128]{1,0:T(8,128)} %shard_map.282.refs_0_), channel_id=1, source_target_pairs={{1,0},{2,1},{3,2},{0,3},{5,4},{6,5},{7,6},{4,7},{9,8},{10,9},{11,1... | collective-permute-start | bytes 761864 | tf_op jit(solution)/shard_map/ppermute | solution.py:572
  22.0 2.7 %copy-start = (f32[496,128]{1,0:T(8,128)}, f32[496,128]{1,0:T(8,128)S(1)}, u32[]{:S(2)}) copy-start(f32[496,128]{1,0:T(8,128)S(1)} %collective-permute-done.2.refs_3_) | copy-start | bytes 761860
  24.7 0.7 copy-start.1
  24.7 0.8 copy-start.2

commit v6 on v5

--- a/solution.py
+++ b/solution.py
@@ -10,7 +10,7 @@
 def dot_nt(a,b): return lax.dot_general(a,b,(((1,),(1,)),((),())),preferred_element_type=F32)
 def split(x):
     h=x.astype(BF); return h,(x-h.astype(F32)).astype(BF)
-GROUP=32
+GROUP=72
 GP=16
 
 def my_sizes(sizes):
@@ -259,7 +259,7 @@
         h,l=split(gelu_half(blk(pre,b0,U)*a+c))
         put_blk(h1h,b0,U,h); put_blk(h1l,b0,U,l)
         put_blk(acc,b0,U,jnp.zeros((U*128,acc.shape[2]),F32))
-    for_blocks(nb,4,n1)
+    for_blocks(nb,8,n1)
     acc[NB]=jnp.zeros(acc.shape[1:],F32)
     outs=[pltpu.make_async_copy(x,y,sem_o.at[i]) for i,(x,y) in enumerate(((h1h,h1h_out),(h1l,h1l_out)))]
     for o in outs: o.start()
@@ -354,7 +354,7 @@
             cross[...]+=c[:,w]
             gz[b0+k]=jnp.concatenate([h[:,w],l[:,w]],axis=0)
             acc[b0+k,:2*CP]=jnp.zeros((2*CP,128),F32)
-    for_blocks(nb,4,soft)
+    for_blocks(nb,8,soft)
     agg_rows(lists,S,gz,acc,slice(0,2*CP))
     mean2=st[2:3,:]; inv2=st[3:4,:]
     a2=npar[2:3,:]*inv2; c2=npar[3:4,:]-mean2*a2
@@ -401,7 +401,7 @@
             d=acc[b0+k,:MY]*dgelu_half(p*ha1+hc1)
             acc[b0+k,:MY]=d
             colsum[0]+=d; colsum[1]+=d*(p-mean1)
-    for_blocks(nb,4,back1)
+    for_blocks(nb,8,back1)
     sb1=lane(colsum[0]); sg1=lane(colsum[1])*inv1
     A1=-a1*inv1*sg1/count; C1=-a1*sb1/count-A1*mean1
     def last(i,_):
@@ -436,12 +436,11 @@
     g_out[q:q+MY,:]=R1v[:MY]+R1v[MY:]+R2v[:,:128]
     g_out[q+MY:q+2*MY,:]=R2v[:,128:]
     RHv=RH[...]; gh=RHv[:MY]+RHv[MY:]
-    gh=jnp.concatenate([RHv[:MY,:CP]+RHv[:MY,CP:2*CP]+RHv[MY:,:CP],gh[:,2*CP:3*CP],sg1,sb1,jnp.zeros((MY,128-2*CP-2),F32)],axis=1)
+    loss=jnp.sum(cross[...])+pair_loss
+    extra=jnp.concatenate([sg2[:,:128],sb2[:,:128],jnp.broadcast_to(loss,(1,128)),jnp.zeros((5,128),F32)],axis=0).T[:MY]
+    gh=jnp.concatenate([RHv[:MY,:CP]+RHv[:MY,CP:2*CP]+RHv[MY:,:CP],gh[:,2*CP:3*CP],sg1,sb1,extra,jnp.zeros((MY,128-2*CP-10),F32)],axis=1)
     g_out[q+2*MY:q+3*MY,:]=gh
-    loss=jnp.sum(cross[...])+pair_loss
-    pad=[jnp.zeros((1,128-MY),F32)]
-    g_out[q+3*MY:,:]=jnp.zeros((g_out.shape[0]-q-3*MY,128),F32)
-    g_out[q+3*MY:q+3*MY+8,:]=jnp.concatenate([jnp.concatenate([sg2[:,:MY]]+pad,axis=1),jnp.concatenate([sb2[:,:MY]]+pad,axis=1),jnp.broadcast_to(loss,(1,128)),jnp.zeros((5,128),F32)],axis=0)
+    if g_out.shape[0]>q+3*MY: g_out[q+3*MY:,:]=jnp.zeros((g_out.shape[0]-q-3*MY,128),F32)
 
 def call_kc(sizes,lists,S,fth,ftl,af,h1h,h1l,pre,pre1,h2t,lg,st,own,recv,labels,pairs,wt,w2m,npar,ncol,CLS,rows):
     NB=fth.shape[0]; H=pre.shape[2]; CP=lg.shape[1]; MY=ncol.shape[0]; NS=3; U8=8
@@ -547,8 +546,8 @@
         store(0,(h,),g[q+h*MY:q+h*MY+MY,:FIN])
         store(2,(slice(None),h,slice(None)),head[h*CP:h*CP+CLS,:MY])
     store(3,(0,),head[2*CP:2*CP+2,:MY])
-    store(3,(1,),g[q+3*MY:q+3*MY+2,:MY])
-    loss[0,0]=g[q+3*MY+2,0]
+    store(3,(1,),head[2*CP+2:2*CP+4,:MY])
+    loss[0,0]=g[q+2*MY,2*CP+4]
     count[0,0]=my_sizes(sizes)[2].astype(F32)
 
 def call_ku(sizes,g,weights,momenta,averages):
@@ -575,7 +574,7 @@
     pairs=pair_nodes[0].reshape(2*G,PEER)
     h1h,h1l,pre,pre1,st,h2t,lg,own,S,npar,wt,w2m,ncol=call_kb(sizes,lists,S,fth,ftl,af,shards,pairs,MY=MY,CP=CP)
     recv=call_kx(own,n_graph)
-    unit=8*n_graph; rows=-(-(2*H//128*MY+3*MY+8)//unit)*unit
+    unit=8*n_graph; rows=-(-(2*H//128*MY+3*MY)//unit)*unit
     g=call_kc(sizes,lists,S,fth,ftl,af,h1h,h1l,pre,pre1,h2t,lg,st,own,recv,labels[0].reshape(NB,1,128),pairs,wt,w2m,npar,ncol,CLS=CLS,rows=rows)
     g=call_kr(g,n_graph)
     *new,loss,count=call_ku(sizes,g,weights,momenta,averages)

time: 144 us -> 140 us (0.972)
  waiting for transfers between devices: 2.73 us -> 0.37 us
    pallas_call x1, Pallas kernels: 42.1 us -> 38.7 us  [call_kr(): pl.pallas_call(functools.partial(kr, n=n), out_shape=jax.ShapeDtypeStruct...]
    pallas_call x1, Pallas kernels: 12.7 us -> 15.1 us  [call_k0(): pl.pallas_call(k0, out_shape=(pltpu.HBM((SL, 128, 128), BF), pltpu.HBM((8...]
    ppermute x3, waiting for transfers between devices: 2.73 us -> 0.37 us  [per_device(): lax.ppermute(packed, 'col', [((j + k) % n_col, j) for j in range(n_col)])]
  transfers between devices with their start and end apart: 3 -> 3, of which waited for: 1 -> 1; matrix products, arithmetic and copies ran while one was open for 0% -> 0% of each run, Pallas kernels for 9% -> 11%
where the time goes in v6:
time: 140 us
  Pallas kernels  131 us (94%)
  starting transfers between devices  6.96 us (5%)
    pallas_call x1, Pallas kernels, call_kx(): pl.pallas_call(functools.partial(kx, n=n), out_shape=pltpu.VMEM(own.shape...  45.2 us
    pallas_call x1, Pallas kernels, call_kr(): pl.pallas_call(functools.partial(kr, n=n), out_shape=jax.ShapeDtypeStruct...  38.7 us
    pallas_call x1, Pallas kernels, call_kb(): pl.pallas_call(functools.partial(kb, n_col=n_col), out_shape=(pltpu.HBM((...  16.5 us
    pallas_call x1, Pallas kernels, call_k0(): pl.pallas_call(k0, out_shape=(pltpu.HBM((SL, 128, 128), BF), pltpu.HBM((8...  15.1 us
    pallas_call x1, Pallas kernels, call_kc(): pl.pallas_call(functools.partial(kc, CLS=CLS), out_shape=jax.ShapeDtypeSt...  11.5 us
    ppermute x3, starting transfers between devices, per_device(): lax.ppermute(packed, 'col', [((j + k) % n_col, j) for j in range(n_col)])  6.96 us
  transfers between devices with their start and end apart: 3, of which 1 were waited for; matrix products, arithmetic and copies ran while one was open for 0% of the time, Pallas kernels for 11%

profile of v6, /device:TPU:0, one launch (start us, length us, event | category | flops | bytes accessed | tf_op | source)
XLA Modules:
  0.0 140.0 jit_solution(17099640202277854856)
XLA Ops:
  0.6 1.7 %shard_map.282.refs_0_ = f32[496,128]{1,0:T(8,128)} custom-call(f32[2,64,100]{2,1,0:T(8,128)} %bitcast.30, f32[2,64,256]{2,1,0:T(8,128)} %bitcast.28, f32[47,2,64]{2,1,0:T(2,128)} %bitcast.32, f32[2,2,64]{2,1,0:T(2,128)} %refs_3_.1), custom_call_target="tpu_custom_call" | custom-call | tf_op jit(solution)/shard_map/pallas_call | solution.py:527
  2.3 3.0 %collective-permute-start.2 = (f32[496,128]{1,0:T(8,128)}, f32[496,128]{1,0:T(8,128)S(1)}, u32[]{:S(2)}, u32[]{:S(2)}) collective-permute-start(f32[496,128]{1,0:T(8,128)} %shard_map.282.refs_0_), channel_id=1, source_target_pairs={{3,0},{0,1},{1,2},{2,3},{7,4},{4,5},{5,6},{6,7},{11,8},{8,9},{9,10... | collective-permute-start | bytes 761864 | tf_op jit(solution)/shard_map/ppermute | solution.py:571
  5.3 2.6 %collective-permute-start.1 = (f32[496,128]{1,0:T(8,128)}, f32[496,128]{1,0:T(8,128)S(1)}, u32[]{:S(2)}, u32[]{:S(2)}) collective-permute-start(f32[496,128]{1,0:T(8,128)} %shard_map.282.refs_0_), channel_id=1, source_target_pairs={{2,0},{3,1},{0,2},{1,3},{6,4},{7,5},{4,6},{5,7},{10,8},{11,9},{8,1... | collective-permute-start | bytes 761864 | tf_op jit(solution)/shard_map/ppermute | solution.py:571
  7.9 1.3 collective-permute-start
  9.3 15.1 %shard_map.281 = (bf16[576,128,128]{2,1,0:T(8,128)(2,1)}, s32[8,640]{1,0:T(8,128)}, bf16[64,128,128]{2,1,0:T(8,128)(2,1)}, bf16[64,128,128]{2,1,0:T(8,128)(2,1)}, bf16[64,128,128]{2,1,0:T(8,128)(2,1)}) custom-call(s32[2,8]{1,0:T(2,128)} %bitcast.43, s32[2,512]{1,0:T(2,128)} %bitcast.47, f32[100,1,8192]{2,1,0:T(1,128)} %bitcast.27, f32[512,128,128]{2,1,0:T(8,128)} %bitcast.26), custom_call_target="tpu_custom_call" | custom-call | tf_op jit(solution)/shard_map/pallas_call | solution.py:147
  24.3 0.0 collective-permute-done.2.refs_3_
  24.3 0.0 copy-start
  24.3 0.4 collective-permute-done.1.refs_2_
  24.7 0.0 copy-start.1
  24.7 0.0 collective-permute-done.refs_1_
  24.7 0.0 copy-start.2
  24.7 0.3 copy-done
  25.0 0.4 copy-done.1
  25.4 0.1 copy-done.2
  25.5 16.5 %shard_map.283 = (bf16[64,128,256]{2,1,0:T(8,128)(2,1)}, bf16[64,128,256]{2,1,0:T(8,128)(2,1)}, f32[64,128,256]{2,1,0:T(8,128)S(1)}, f32[64,64,128]{2,1,0:T(8,12...) custom-call(s32[2,8]{1,0:T(2,128)} %bitcast.44, ...), custom_call_target="tpu_custom_call" | custom-call | tf_op jit(solution)/shard_map/pallas_call | solution.py:310
  42.0 45.2 %shard_map.284.recv = f32[8,16,128]{2,1,0:T(8,128)S(1)} custom-call(f32[8,16,128]{2,1,0:T(8,128)S(1)} %get-tuple-element.59.own), custom_call_target="tpu_custom_call" | custom-call | tf_op jit(solution)/shard_map/pallas_call | solution.py:479
  87.2 11.5 %shard_map.285.g = f32[448,128]{1,0:T(8,128)} custom-call(s32[2,8]{1,0:T(2,128)} %bitcast.45, s32[8,640]{1,0:T(8,128)} %get-tuple-element.46.lists, bf16[577,128,128]{2,1,0:T(8,128)(2,1)S(1)} %get-tuple-element.51.S, f32[64,128,256]{2,1,0:T(8,128)S(1)} %get-tuple-element.52.pre, f32[64,64,128]{2,1,0:T(8,128)S(1)} %get-tuple-element.53.pre1, ...), custom_call_target="tpu_custom_call" | custom-call | tf_op jit(solution)/shard_map/pallas_call | solution.py:449
  98.7 38.7 %shard_map.286.g = f32[448,128]{1,0:T(8,128)} custom-call(f32[448,128]{1,0:T(8,128)} %shard_map.285.g), custom_call_target="tpu_custom_call" | custom-call | tf_op jit(solution)/shard_map/pallas_call | solution.py:509
  137.3 2.5 %shard_map.287 = (f32[2,64,100]{2,1,0:T(8,128)}, f32[2,64,100]{2,1,0:T(8,128)}, f32[2,64,100]{2,1,0:T(8,128)}, f32[2,64,256]{2,1,0:T(8,128)}, f32[2,64,256]{2,1,...) custom-call(s32[2,8]{1,0:T(2,128)} %bitcast.46, ...), custom_call_target="tpu_custom_call" | custom-call | tf_op jit(solution)/shard_map/pallas_call | solution.py:556
Async XLA Ops:
  2.3 22.0 %collective-permute-start.2 = (f32[496,128]{1,0:T(8,128)}, f32[496,128]{1,0:T(8,128)S(1)}, u32[]{:S(2)}, u32[]{:S(2)}) collective-permute-start(f32[496,128]{1,0:T(8,128)} %shard_map.282.refs_0_), channel_id=1, source_target_pairs={{3,0},{0,1},{1,2},{2,3},{7,4},{4,5},{5,6},{6,7},{11,8},{8,9},{9,10... | collective-permute-start | bytes 761864 | tf_op jit(solution)/shard_map/ppermute | solution.py:571
  5.3 19.4 %collective-permute-start.1 = (f32[496,128]{1,0:T(8,128)}, f32[496,128]{1,0:T(8,128)S(1)}, u32[]{:S(2)}, u32[]{:S(2)}) collective-permute-start(f32[496,128]{1,0:T(8,128)} %shard_map.282.refs_0_), channel_id=1, source_target_pairs={{2,0},{3,1},{0,2},{1,3},{6,4},{7,5},{4,6},{5,7},{10,8},{11,9},{8,1... | collective-permute-start | bytes 761864 | tf_op jit(solution)/shard_map/ppermute | solution.py:571
  7.9 16.8 %collective-permute-start = (f32[496,128]{1,0:T(8,128)}, f32[496,128]{1,0:T(8,128)S(1)}, u32[]{:S(2)}, u32[]{:S(2)}) collective-permute-start(f32[496,128]{1,0:T(8,128)} %shard_map.282.refs_0_), channel_id=1, source_target_pairs={{1,0},{2,1},{3,2},{0,3},{5,4},{6,5},{7,6},{4,7},{9,8},{10,9},{11,1... | collective-permute-start | bytes 761864 | tf_op jit(solution)/shard_map/ppermute | solution.py:571
  24.3 0.7 copy-start
  24.7 0.7 copy-start.1
  24.7 0.8 copy-start.2

commit v7 on v6

--- a/solution.py
+++ b/solution.py
@@ -10,7 +10,7 @@
 def dot_nt(a,b): return lax.dot_general(a,b,(((1,),(1,)),((),())),preferred_element_type=F32)
 def split(x):
     h=x.astype(BF); return h,(x-h.astype(F32)).astype(BF)
-GROUP=72
+GROUP=96
 GP=16
 
 def my_sizes(sizes):
@@ -286,7 +286,7 @@
             y=x[:,:2*HP]+s+pltpu.roll(s,HP,1)
             acc[b0+k,:,:2*HP]=y
             lg[b0+k]=y.T[:CP]
-    for_blocks(nb,8,fin)
+    for_blocks(nb,16,fin)
     G=pairs.shape[0]//2; K=pairs.shape[1]
     lane=lax.broadcasted_iota(I32,(1,128),1); sub=lax.broadcasted_iota(I32,(8,1),0)
     def slot(g,_):
@@ -446,7 +446,7 @@
     NB=fth.shape[0]; H=pre.shape[2]; CP=lg.shape[1]; MY=ncol.shape[0]; NS=3; U8=8
     ANY=pl.BlockSpec(memory_space=pltpu.HBM); VM=pl.BlockSpec(memory_space=pltpu.VMEM); SM=pl.BlockSpec(memory_space=pltpu.SMEM)
     V=pltpu.VMEM
-    return pl.pallas_call(functools.partial(kc,CLS=CLS),out_shape=jax.ShapeDtypeStruct((rows,128),F32),
+    return pl.pallas_call(functools.partial(kc,CLS=CLS),out_shape=V((rows,128),F32),
         in_specs=[SM,SM]+[VM]*5+[ANY]*5+[VM]*9,out_specs=VM,
         scratch_shapes=[V((NS,U8,128,H),BF)]*2+[V((NS,U8,128,128),BF)]*3+[
             V((NB,128,H),F32),V((NB,2*CP,128),BF),V((NB+1,max(3*MY,2*CP),128),F32),V((NB,3*MY,128),BF),
@@ -508,7 +508,7 @@
     VM=pl.BlockSpec(memory_space=pltpu.VMEM); D=pltpu.SemaphoreType.DMA((n-1,))
     return pl.pallas_call(functools.partial(kr,n=n),out_shape=jax.ShapeDtypeStruct(g.shape,g.dtype),in_specs=[VM],out_specs=VM,
         scratch_shapes=[pltpu.VMEM((n-1,g.shape[0]//n,128),F32),D,D,D,D],
-        compiler_params=pltpu.CompilerParams(collective_id=2,has_side_effects=True))(g)
+        compiler_params=pltpu.CompilerParams(vmem_limit_bytes=8<<20,collective_id=2,has_side_effects=True))(*in_vmem(g))
 
 def kp(wf,ws,wh,npar,out):
     _,MY,FIN=wf.shape; H=ws.shape[2]; CLS=wh.shape[0]; CP=-(-CLS//16)*16; nk=H//128

time: 140 us -> 135 us (0.964)
  Pallas kernels: 131 us -> 122 us
  waiting for transfers between devices: 0.37 us -> 4.65 us
    pallas_call x1, Pallas kernels: 38.7 us -> 32.1 us  [call_kr(): pl.pallas_call(functools.partial(kr, n=n), out_shape=jax.ShapeDtypeStruct...]
    pallas_call x1, Pallas kernels: 45.2 us -> 39 us  [call_kx(): pl.pallas_call(functools.partial(kx, n=n), out_shape=pltpu.VMEM(own.shape...]
    pallas_call x1, Pallas kernels: 16.5 us -> 21.6 us  [call_kb(): pl.pallas_call(functools.partial(kb, n_col=n_col), out_shape=(pltpu.HBM((...]
    ppermute x3, waiting for transfers between devices: 0.37 us -> 4.65 us  [per_device(): lax.ppermute(packed, 'col', [((j + k) % n_col, j) for j in range(n_col)])]
    pallas_call x1, Pallas kernels: 15.1 us -> 10.8 us  [call_k0(): pl.pallas_call(k0, out_shape=(pltpu.HBM((SL, 128, 128), BF), pltpu.HBM((8...]
    pallas_call x1, Pallas kernels: 11.5 us -> 14.4 us  [call_kc(): pl.pallas_call(functools.partial(kc, CLS=CLS), out_shape=V((rows, 128), F...]
  transfers between devices with their start and end apart: 3 -> 3, of which waited for: 1 -> 1; matrix products, arithmetic and copies ran while one was open for 0% -> 0% of each run, Pallas kernels for 11% -> 8%
where the time goes in v7:
time: 135 us; the launch traced here: 136 us
  Pallas kernels  122 us (90%)
  starting transfers between devices  6.96 us (5%)
  waiting for transfers between devices  4.65 us (3%)
  local copies, waits for them, and re-layouts  1.46 us (1%)
    pallas_call x1, Pallas kernels, call_kx(): pl.pallas_call(functools.partial(kx, n=n), out_shape=pltpu.VMEM(own.shape...  39 us
    pallas_call x1, Pallas kernels, call_kr(): pl.pallas_call(functools.partial(kr, n=n), out_shape=jax.ShapeDtypeStruct...  32.1 us
    pallas_call x1, Pallas kernels, call_kb(): pl.pallas_call(functools.partial(kb, n_col=n_col), out_shape=(pltpu.HBM((...  21.6 us
    pallas_call x1, Pallas kernels, call_kc(): pl.pallas_call(functools.partial(kc, CLS=CLS), out_shape=V((rows, 128), F...  14.4 us
    pallas_call x1, Pallas kernels, call_k0(): pl.pallas_call(k0, out_shape=(pltpu.HBM((SL, 128, 128), BF), pltpu.HBM((8...  10.8 us
    ppermute x3, starting transfers between devices, per_device(): lax.ppermute(packed, 'col', [((j + k) % n_col, j) for j in range(n_col)])  6.96 us
    ppermute x3, waiting for transfers between devices, per_device(): lax.ppermute(packed, 'col', [((j + k) % n_col, j) for j in range(n_col)])  4.65 us
  transfers between devices with their start and end apart: 3, of which 1 were waited for; matrix products, arithmetic and copies ran while one was open for 0% of the time, Pallas kernels for 8%

profile of v7, /device:TPU:0, one launch (start us, length us, event | category | flops | bytes accessed | tf_op | source)
XLA Modules:
  0.0 136.0 jit_solution(1610540846521231783)
XLA Ops:
  0.6 1.6 %shard_map.282.refs_0_ = f32[496,128]{1,0:T(8,128)} custom-call(f32[2,64,100]{2,1,0:T(8,128)} %bitcast.30, f32[2,64,256]{2,1,0:T(8,128)} %bitcast.28, f32[47,2,64]{2,1,0:T(2,128)} %bitcast.32, f32[2,2,64]{2,1,0:T(2,128)} %refs_3_.1), custom_call_target="tpu_custom_call" | custom-call | tf_op jit(solution)/shard_map/pallas_call | solution.py:527
  2.3 3.0 %collective-permute-start.2 = (f32[496,128]{1,0:T(8,128)}, f32[496,128]{1,0:T(8,128)S(1)}, u32[]{:S(2)}, u32[]{:S(2)}) collective-permute-start(f32[496,128]{1,0:T(8,128)} %shard_map.282.refs_0_), channel_id=1, source_target_pairs={{3,0},{0,1},{1,2},{2,3},{7,4},{4,5},{5,6},{6,7},{11,8},{8,9},{9,10... | collective-permute-start | bytes 761864 | tf_op jit(solution)/shard_map/ppermute | solution.py:571
  5.3 2.6 %collective-permute-start.1 = (f32[496,128]{1,0:T(8,128)}, f32[496,128]{1,0:T(8,128)S(1)}, u32[]{:S(2)}, u32[]{:S(2)}) collective-permute-start(f32[496,128]{1,0:T(8,128)} %shard_map.282.refs_0_), channel_id=1, source_target_pairs={{2,0},{3,1},{0,2},{1,3},{6,4},{7,5},{4,6},{5,7},{10,8},{11,9},{8,1... | collective-permute-start | bytes 761864 | tf_op jit(solution)/shard_map/ppermute | solution.py:571
  7.9 1.3 collective-permute-start
  9.3 10.8 %shard_map.281 = (bf16[576,128,128]{2,1,0:T(8,128)(2,1)}, s32[8,640]{1,0:T(8,128)}, bf16[64,128,128]{2,1,0:T(8,128)(2,1)}, bf16[64,128,128]{2,1,0:T(8,128)(2,1)}, bf16[64,128,128]{2,1,0:T(8,128)(2,1)}) custom-call(s32[2,8]{1,0:T(2,128)} %bitcast.43, s32[2,512]{1,0:T(2,128)} %bitcast.47, f32[100,1,8192]{2,1,0:T(1,128)} %bitcast.27, f32[512,128,128]{2,1,0:T(8,128)} %bitcast.26), custom_call_target="tpu_custom_call" | custom-call | tf_op jit(solution)/shard_map/pallas_call | solution.py:147
  20.0 0.0 collective-permute-done.2.refs_3_
  20.0 0.0 copy-start.1
  20.1 4.6 %collective-permute-done.1.refs_2_ = f32[496,128]{1,0:T(8,128)S(1)} collective-permute-done((f32[496,128]{1,0:T(8,128)}, f32[496,128]{1,0:T(8,128)S(1)}, u32[]{:S(2)}, u32[]{:S(2)}) %collective-permute-start.1) | collective-permute-done | bytes 253984 | tf_op jit(solution)/shard_map/ppermute | solution.py:571
  24.7 0.0 copy-start.2
  24.7 0.0 collective-permute-done.refs_1_
  24.7 0.0 copy-start.3
  24.7 0.0 copy-done.1
  24.7 0.7 copy-done.2
  25.4 0.1 copy-done.3
  25.5 21.6 %shard_map.283 = (bf16[64,128,256]{2,1,0:T(8,128)(2,1)}, bf16[64,128,256]{2,1,0:T(8,128)(2,1)}, f32[64,128,256]{2,1,0:T(8,128)S(1)}, f32[64,64,128]{2,1,0:T(8,12...) custom-call(s32[2,8]{1,0:T(2,128)} %bitcast.44, ...), custom_call_target="tpu_custom_call" | custom-call | tf_op jit(solution)/shard_map/pallas_call | solution.py:310
  47.1 39.0 %shard_map.284.recv = f32[8,16,128]{2,1,0:T(8,128)S(1)} custom-call(f32[8,16,128]{2,1,0:T(8,128)S(1)} %get-tuple-element.59.own), custom_call_target="tpu_custom_call" | custom-call | tf_op jit(solution)/shard_map/pallas_call | solution.py:479
  86.1 14.4 %shard_map.285.g = f32[448,128]{1,0:T(8,128)S(1)} custom-call(s32[2,8]{1,0:T(2,128)} %bitcast.45, s32[8,640]{1,0:T(8,128)} %get-tuple-element.46.lists, bf16[577,128,128]{2,1,0:T(8,128)(2,1)S(1)} %get-tuple-element.51.S, f32[64,128,256]{2,1,0:T(8,128)S(1)} %get-tuple-element.52.pre, f32[64,64,128]{2,1,0:T(8,128)S(1)} %get-tuple-element.53.pre1, ...), custom_call_target="tpu_custom_call" | custom-call | tf_op jit(solution)/shard_map/pallas_call | solution.py:449
  100.6 32.1 %shard_map.286.g = f32[448,128]{1,0:T(8,128)S(1)} custom-call(f32[448,128]{1,0:T(8,128)S(1)} %shard_map.285.g), custom_call_target="tpu_custom_call" | custom-call | tf_op jit(solution)/shard_map/pallas_call | solution.py:509
  132.7 0.0 copy-start
  132.7 0.7 copy-done
  133.4 2.4 %shard_map.287 = (f32[2,64,100]{2,1,0:T(8,128)}, f32[2,64,100]{2,1,0:T(8,128)}, f32[2,64,100]{2,1,0:T(8,128)}, f32[2,64,256]{2,1,0:T(8,128)}, f32[2,64,256]{2,1,...) custom-call(s32[2,8]{1,0:T(2,128)} %bitcast.46, ...), custom_call_target="tpu_custom_call" | custom-call | tf_op jit(solution)/shard_map/pallas_call | solution.py:556
Async XLA Ops:
  2.3 17.7 %collective-permute-start.2 = (f32[496,128]{1,0:T(8,128)}, f32[496,128]{1,0:T(8,128)S(1)}, u32[]{:S(2)}, u32[]{:S(2)}) collective-permute-start(f32[496,128]{1,0:T(8,128)} %shard_map.282.refs_0_), channel_id=1, source_target_pairs={{3,0},{0,1},{1,2},{2,3},{7,4},{4,5},{5,6},{6,7},{11,8},{8,9},{9,10... | collective-permute-start | bytes 761864 | tf_op jit(solution)/shard_map/ppermute | solution.py:571
  5.3 19.4 %collective-permute-start.1 = (f32[496,128]{1,0:T(8,128)}, f32[496,128]{1,0:T(8,128)S(1)}, u32[]{:S(2)}, u32[]{:S(2)}) collective-permute-start(f32[496,128]{1,0:T(8,128)} %shard_map.282.refs_0_), channel_id=1, source_target_pairs={{2,0},{3,1},{0,2},{1,3},{6,4},{7,5},{4,6},{5,7},{10,8},{11,9},{8,1... | collective-permute-start | bytes 761864 | tf_op jit(solution)/shard_map/ppermute | solution.py:571
  7.9 16.8 %collective-permute-start = (f32[496,128]{1,0:T(8,128)}, f32[496,128]{1,0:T(8,128)S(1)}, u32[]{:S(2)}, u32[]{:S(2)}) collective-permute-start(f32[496,128]{1,0:T(8,128)} %shard_map.282.refs_0_), channel_id=1, source_target_pairs={{1,0},{2,1},{3,2},{0,3},{5,4},{6,5},{7,6},{4,7},{9,8},{10,9},{11,1... | collective-permute-start | bytes 761864 | tf_op jit(solution)/shard_map/ppermute | solution.py:571
  20.0 4.7 %copy-start.1 = (f32[496,128]{1,0:T(8,128)}, f32[496,128]{1,0:T(8,128)S(1)}, u32[]{:S(2)}) copy-start(f32[496,128]{1,0:T(8,128)S(1)} %collective-permute-done.2.refs_3_) | copy-start | bytes 761860
  24.7 0.7 copy-start.2
  24.7 0.8 copy-start.3
  132.7 0.7 copy-start
